TPU v7x, 32 devices: a whole 2x2x4 slice. The times are simulated.
32 devices in a mesh: ctx: 8 (over z, y), fsdp: 4 (over x, core).
Axes of the slice: x: 2, y: 2, z: 4, core: 2. Of those that a mesh axis runs over, the one named last changes fastest.
Arguments:
- tokens: bfloat16 [4, 1024, 2048], P('fsdp', 'ctx'), may hold values from -6 to 6
- teacher: bfloat16 [4, 1024, 2048], P('fsdp', 'ctx'), may hold values from -6 to 6
- valid_mask: int32 [4, 1024], P('fsdp', 'ctx'), may hold values 0 or 1
- lengths: int32 [4, 4], P('fsdp'), may hold values from 1 to 512, 1024 in all within a row
- span_order: int32 [4, 8], P('fsdp', 'ctx'), may hold values from 0 to 7, as said below
- w_query: bfloat16 [2048, 2048], P(('ctx', 'fsdp')), may hold values from -0.125 to 0.125
- w_key: bfloat16 [2048, 512], P(('ctx', 'fsdp')), may hold values from -0.125 to 0.125
- w_value: bfloat16 [2048, 512], P(('ctx', 'fsdp')), may hold values from -0.125 to 0.125
- w_out: bfloat16 [2048, 2048], P(('ctx', 'fsdp')), may hold values from -1 to 1
- w_gate: bfloat16 [2048, 8192], P(('ctx', 'fsdp')), may hold values from -0.125 to 0.125
- w_up: bfloat16 [2048, 8192], P(('ctx', 'fsdp')), may hold values from -0.125 to 0.125
- w_down: bfloat16 [8192, 2048], P(('ctx', 'fsdp')), may hold values from -0.0625 to 0.0625
- gain_attn: bfloat16 [2048], P(('ctx', 'fsdp')), may hold values from 0.099609375 to 1.8984375
- gain_ffn: bfloat16 [2048], P(('ctx', 'fsdp')), may hold values from 0.099609375 to 1.8984375
Outputs:
- output: bfloat16 [4, 1024, 2048], P('fsdp', 'ctx')
- loss_value: float32 [], replicated
- grad_tokens: float32 [4, 1024, 2048], P('fsdp', 'ctx')
- grad_w_query: float32 [2048, 2048], P(('ctx', 'fsdp'))
- grad_w_key: float32 [2048, 512], P(('ctx', 'fsdp'))
- grad_w_value: float32 [2048, 512], P(('ctx', 'fsdp'))
- grad_w_out: float32 [2048, 2048], P(('ctx', 'fsdp'))
- grad_w_gate: float32 [2048, 8192], P(('ctx', 'fsdp'))
- grad_w_up: float32 [2048, 8192], P(('ctx', 'fsdp'))
- grad_w_down: float32 [8192, 2048], P(('ctx', 'fsdp'))
- grad_gain_attn: float32 [2048], P(('ctx', 'fsdp'))
- grad_gain_ffn: float32 [2048], P(('ctx', 'fsdp'))
Inputs may be any that keep to these rules, and one draw needn't show every extreme that they name: Each row lists the lengths of the 4 sequences of one stream in stream order; they sum to 1024 and the longest is exactly 512. `span_order`: each row is a permutation of the span numbers of one stream; entry c names the stream span held in token slots c * 128 to c * 128 + 127. The spans of one context device, in slot order, are r, r + 8, r + 16, ..., one residue r for each device.
All inputs are finite; a program needn't handle non-finite values. No bound on the sum of `valid_mask` on one device may be relied on, other than what follows from the above.
Results may differ from a plain program's by a relative error of at most 0.015.
Values may be sent and summed in bfloat16 or wider, within the bound.
No kernel may reach another device: no remote copies, remote signals or barrier semaphores. Data moves between devices by JAX's collectives and lax.ppermute only.
A program may use at most 576 MiB of HBM per device.

v0:
```python
import math

import jax
import jax.numpy as jnp
import numpy as np
from jax import lax
from jax.sharding import PartitionSpec as P

HEADS = 32
KV_HEADS = 8
HEAD_DIM = 64
SPAN = 128


EPSILON = 1e-05
FLOOR_SCORE = -1e30


def rope_rates(head_width):
    frequency = 1.0 / 500000.0 ** (np.arange(0, head_width, 2) / head_width)
    wavelength = 2.0 * np.pi / frequency
    blend_share = (8192.0 / wavelength - 1.0) / 3.0
    blended = (1.0 - blend_share) * frequency / 32.0 + blend_share * frequency
    frequency = np.where(
        wavelength < 2048.0, frequency, np.where(wavelength > 8192.0, frequency / 32.0, blended)
    )
    return np.concatenate([frequency, frequency]).astype(np.float32)


def rotate(values, angles):
    half_dim = values.shape[-1] // 2
    turned = jnp.concatenate([-values[..., half_dim:], values[..., :half_dim]], axis=-1)
    return values * jnp.cos(angles)[:, None, :] + turned * jnp.sin(angles)[:, None, :]


def rotate_back(grads_in, angles):
    half_dim = grads_in.shape[-1] // 2
    sined = grads_in * jnp.sin(angles)[:, None, :]
    turned = jnp.concatenate([-sined[..., half_dim:], sined[..., :half_dim]], axis=-1)
    return grads_in * jnp.cos(angles)[:, None, :] - turned


def transposed(left, right):
    return lax.dot_general(
        left, right, (((0,), (0,)), ((), ())), preferred_element_type=jnp.float32
    )


def against(left, right):
    return lax.dot_general(
        left, right, (((1,), (1,)), ((), ())), preferred_element_type=jnp.float32
    )


def rms_inverse(values):
    return lax.rsqrt(jnp.mean(values * values, axis=1, keepdims=True) + EPSILON)


def norm_back(grad_normed, values, inverse, gain):
    scaled = grad_normed * gain
    unit_rows = values * inverse
    grad_values = inverse * (
        scaled - unit_rows * jnp.mean(scaled * unit_rows, axis=1, keepdims=True)
    )
    return (grad_values, jnp.sum(grad_normed * unit_rows, axis=0))


def body(
    tokens,
    teacher,
    valid_mask,
    lengths,
    span_order,
    w_query,
    w_key,
    w_value,
    w_out,
    w_gate,
    w_up,
    w_down,
    gain_attn,
    gain_ffn,
):
    inputs = tokens[0].astype(jnp.float32)
    tok_rows, width = inputs.shape
    group_size = HEADS // KV_HEADS
    kv_width = KV_HEADS * HEAD_DIM
    score_scale = 1.0 / math.sqrt(HEAD_DIM)
    slot_index = jnp.arange(tok_rows, dtype=jnp.int32)
    stream_place = jnp.repeat(span_order[0], SPAN) * SPAN + slot_index % SPAN
    seq_ends = jnp.cumsum(lengths[0])
    passed = seq_ends[None, :] <= stream_place[:, None]
    segment = jnp.sum(passed.astype(jnp.int32), axis=1)
    seq_begin = jnp.sum(jnp.where(passed, lengths[0][None, :], 0), axis=1)
    angles = (stream_place - seq_begin).astype(jnp.float32)[:, None] * jnp.asarray(
        rope_rates(HEAD_DIM)
    )[None, :]
    query_full, key_full, value_full, out_full, attn_gain = (
        lax.all_gather(w_query, ("ctx", "fsdp"), axis=0, tiled=True),
        lax.all_gather(w_key, ("ctx", "fsdp"), axis=0, tiled=True),
        lax.all_gather(w_value, ("ctx", "fsdp"), axis=0, tiled=True),
        lax.all_gather(w_out, ("ctx", "fsdp"), axis=0, tiled=True),
        lax.all_gather(gain_attn, ("ctx", "fsdp"), axis=0, tiled=True),
    )
    inverse_attn = rms_inverse(inputs)
    normed_attn = (inputs * inverse_attn * attn_gain.astype(jnp.float32)).astype(jnp.bfloat16)
    query_act = jnp.dot(normed_attn, query_full, preferred_element_type=jnp.float32)
    key_act = jnp.dot(normed_attn, key_full, preferred_element_type=jnp.float32)
    value_act = jnp.dot(normed_attn, value_full, preferred_element_type=jnp.float32)
    query_rot = rotate(query_act.reshape(tok_rows, HEADS, HEAD_DIM), angles).astype(jnp.bfloat16)
    query_grouped = query_rot.reshape(tok_rows, KV_HEADS, group_size, HEAD_DIM)
    key_rot = (
        rotate(key_act.reshape(tok_rows, KV_HEADS, HEAD_DIM), angles)
        .astype(jnp.bfloat16)
        .reshape(tok_rows, kv_width)
    )
    value_low = value_act.astype(jnp.bfloat16)

    def visible(place_piece, seg_piece):
        return (seg_piece[None, :] == segment[:, None]) & (
            place_piece[None, :] <= stream_place[:, None]
        )

    start_state = (
        jnp.full((tok_rows, KV_HEADS, group_size), FLOOR_SCORE, jnp.float32),
        jnp.zeros((tok_rows, KV_HEADS, group_size), jnp.float32),
        jnp.zeros((tok_rows, KV_HEADS, group_size, HEAD_DIM), jnp.float32),
    )
    key_piece = lax.all_gather(key_rot, "ctx", axis=0, tiled=True)
    value_piece = lax.all_gather(value_low, "ctx", axis=0, tiled=True)
    place_piece = lax.all_gather(stream_place, "ctx", axis=0, tiled=True)
    seg_piece = lax.all_gather(segment, "ctx", axis=0, tiled=True)
    visible_now = visible(place_piece, seg_piece)
    piece_rows = key_piece.shape[0]

    def update(carried):
        row_max, row_sum, accumulated = carried
        key_heads = key_piece.reshape(piece_rows, KV_HEADS, HEAD_DIM)
        value_heads = value_piece.reshape(piece_rows, KV_HEADS, HEAD_DIM)
        scores = (
            jnp.einsum(
                "qgrd,kgd->qgrk", query_grouped, key_heads, preferred_element_type=jnp.float32
            )
            * score_scale
        )
        mask_wide = visible_now[:, None, None, :]
        scores = jnp.where(mask_wide, scores, FLOOR_SCORE)
        new_max = jnp.maximum(row_max, jnp.max(scores, axis=-1))
        probs = jnp.where(mask_wide, jnp.exp(scores - new_max[..., None]), 0.0)
        mixed_heads = jnp.einsum(
            "qgrk,kgd->qgrd",
            probs.astype(jnp.bfloat16),
            value_heads,
            preferred_element_type=jnp.float32,
        )
        return (new_max, jnp.sum(probs, axis=-1), mixed_heads)

    row_max, row_sum, accumulated = lax.cond(
        jnp.any(visible_now), update, lambda carried: carried, start_state
    )
    log_total = row_max + jnp.log(row_sum)
    attended_f = accumulated / row_sum[..., None]
    attended = attended_f.reshape(tok_rows, width).astype(jnp.bfloat16)
    middle = inputs + jnp.dot(attended, out_full, preferred_element_type=jnp.float32)
    gate_full, up_full, down_full, ffn_gain = (
        lax.all_gather(w_gate, ("ctx", "fsdp"), axis=0, tiled=True),
        lax.all_gather(w_up, ("ctx", "fsdp"), axis=0, tiled=True),
        lax.all_gather(w_down, ("ctx", "fsdp"), axis=0, tiled=True),
        lax.all_gather(gain_ffn, ("ctx", "fsdp"), axis=0, tiled=True),
    )
    inverse_ffn = rms_inverse(middle)
    normed_ffn = (middle * inverse_ffn * ffn_gain.astype(jnp.float32)).astype(jnp.bfloat16)
    gate_act = jnp.dot(normed_ffn, gate_full, preferred_element_type=jnp.float32)
    up_act = jnp.dot(normed_ffn, up_full, preferred_element_type=jnp.float32)
    hidden = (jax.nn.silu(gate_act) * up_act).astype(jnp.bfloat16)
    output = middle + jnp.dot(hidden, down_full, preferred_element_type=jnp.float32)
    teacher_f = teacher[0].astype(jnp.float32)
    valid_f = valid_mask[0].astype(jnp.float32)
    missed = (output - teacher_f) * valid_f[:, None]
    valid_count, square_sum = lax.psum(
        (jnp.sum(valid_f), jnp.sum(missed * missed)), ("ctx", "fsdp")
    )
    loss_value = 0.5 * square_sum / (width * valid_count)
    all_tokens = tok_rows * lax.axis_size("ctx") * lax.axis_size("fsdp")
    grad_out = missed * (all_tokens / valid_count)
    grad_low = grad_out.astype(jnp.bfloat16)
    gate_full, up_full, down_full, ffn_gain = (
        lax.all_gather(w_gate, ("ctx", "fsdp"), axis=0, tiled=True),
        lax.all_gather(w_up, ("ctx", "fsdp"), axis=0, tiled=True),
        lax.all_gather(w_down, ("ctx", "fsdp"), axis=0, tiled=True),
        lax.all_gather(gain_ffn, ("ctx", "fsdp"), axis=0, tiled=True),
    )
    grad_hidden = against(grad_low, down_full)
    sigmoid_gate = jax.nn.sigmoid(gate_act)
    silu_gate = gate_act * sigmoid_gate
    grad_gate = (
        grad_hidden * up_act * sigmoid_gate * (1.0 + gate_act * (1.0 - sigmoid_gate))
    ).astype(jnp.bfloat16)
    grad_up = (grad_hidden * silu_gate).astype(jnp.bfloat16)
    grad_normed_ffn = against(grad_gate, gate_full) + against(grad_up, up_full)
    grad_middle_part, grad_gain_ffn = norm_back(
        grad_normed_ffn, middle, inverse_ffn, ffn_gain.astype(jnp.float32)
    )
    grad_middle = grad_out + grad_middle_part
    middle_low = grad_middle.astype(jnp.bfloat16)
    ff_width = hidden.shape[1]
    ffn_in_term = transposed(normed_ffn, jnp.concatenate([grad_gate, grad_up], axis=1))
    ffn_in_mine = lax.psum_scatter(ffn_in_term, ("ctx", "fsdp"), scatter_dimension=0, tiled=True)
    down_mine = lax.psum_scatter(
        transposed(hidden, grad_low), ("ctx", "fsdp"), scatter_dimension=0, tiled=True
    )
    query_full, key_full, value_full, out_full, attn_gain = (
        lax.all_gather(w_query, ("ctx", "fsdp"), axis=0, tiled=True),
        lax.all_gather(w_key, ("ctx", "fsdp"), axis=0, tiled=True),
        lax.all_gather(w_value, ("ctx", "fsdp"), axis=0, tiled=True),
        lax.all_gather(w_out, ("ctx", "fsdp"), axis=0, tiled=True),
        lax.all_gather(gain_attn, ("ctx", "fsdp"), axis=0, tiled=True),
    )
    grad_attended = against(middle_low, out_full).astype(jnp.bfloat16)
    grad_heads = grad_attended.reshape(tok_rows, KV_HEADS, group_size, HEAD_DIM)
    delta_rows = jnp.sum(grad_heads.astype(jnp.float32) * attended_f, axis=-1)
    key_all, value_all, place_all, seg_all = (
        lax.all_gather(key_rot, "ctx", axis=0, tiled=True),
        lax.all_gather(value_low, "ctx", axis=0, tiled=True),
        lax.all_gather(stream_place, "ctx", axis=0, tiled=True),
        lax.all_gather(segment, "ctx", axis=0, tiled=True),
    )
    stream_rows = key_all.shape[0]
    block_rows = math.gcd(512, stream_rows)
    block_count = stream_rows // block_rows

    def key_block(grad_query, block_items):
        key_piece, value_piece, place_piece, seg_piece = block_items
        visible_now = visible(place_piece, seg_piece)

        def work(grad_carried):
            key_heads = key_piece.reshape(block_rows, KV_HEADS, HEAD_DIM)
            value_heads = value_piece.reshape(block_rows, KV_HEADS, HEAD_DIM)
            scores = (
                jnp.einsum(
                    "qgrd,kgd->qgrk", query_grouped, key_heads, preferred_element_type=jnp.float32
                )
                * score_scale
            )
            mask_wide = visible_now[:, None, None, :]
            probs = jnp.where(mask_wide, jnp.exp(scores - log_total[..., None]), 0.0)
            grad_value_block = jnp.einsum(
                "qgrk,qgrd->kgd",
                probs.astype(jnp.bfloat16),
                grad_heads,
                preferred_element_type=jnp.float32,
            )
            grad_probs = jnp.einsum(
                "qgrd,kgd->qgrk", grad_heads, value_heads, preferred_element_type=jnp.float32
            )
            grad_scores = (probs * (grad_probs - delta_rows[..., None]) * score_scale).astype(
                jnp.bfloat16
            )
            grad_next = grad_carried + jnp.einsum(
                "qgrk,kgd->qgrd", grad_scores, key_heads, preferred_element_type=jnp.float32
            )
            grad_key_block = jnp.einsum(
                "qgrk,qgrd->kgd", grad_scores, query_grouped, preferred_element_type=jnp.float32
            )
            return (grad_next, (grad_key_block, grad_value_block))

        def skip(grad_carried):
            empty_block = jnp.zeros((block_rows, KV_HEADS, HEAD_DIM), jnp.float32)
            return (grad_carried, (empty_block, empty_block))

        return lax.cond(jnp.any(visible_now), work, skip, grad_query)

    grad_query, (grad_keys, grad_values) = lax.scan(
        key_block,
        jnp.zeros((tok_rows, KV_HEADS, group_size, HEAD_DIM), jnp.float32),
        (
            key_all.reshape(block_count, block_rows, kv_width),
            value_all.reshape(block_count, block_rows, kv_width),
            place_all.reshape(block_count, block_rows),
            seg_all.reshape(block_count, block_rows),
        ),
    )
    key_mine, value_mine = (
        lax.psum_scatter(
            grad_keys.reshape(stream_rows, kv_width).astype(jnp.bfloat16),
            "ctx",
            scatter_dimension=0,
            tiled=True,
        ).astype(jnp.float32),
        lax.psum_scatter(
            grad_values.reshape(stream_rows, kv_width).astype(jnp.bfloat16),
            "ctx",
            scatter_dimension=0,
            tiled=True,
        ).astype(jnp.float32),
    )
    grad_query_low = (
        rotate_back(grad_query.reshape(tok_rows, HEADS, HEAD_DIM), angles)
        .astype(jnp.bfloat16)
        .reshape(tok_rows, width)
    )
    grad_key_low = (
        rotate_back(key_mine.reshape(tok_rows, KV_HEADS, HEAD_DIM), angles)
        .astype(jnp.bfloat16)
        .reshape(tok_rows, kv_width)
    )
    grad_value_low = value_mine.astype(jnp.bfloat16)
    grad_normed_attn = (
        against(grad_query_low, query_full)
        + against(grad_key_low, key_full)
        + against(grad_value_low, value_full)
    )
    grad_input_part, grad_gain_attn = norm_back(
        grad_normed_attn, inputs, inverse_attn, attn_gain.astype(jnp.float32)
    )
    grad_input = grad_middle + grad_input_part
    grad_qkv = jnp.concatenate([grad_query_low, grad_key_low, grad_value_low], axis=1)
    gain_block = jnp.concatenate(
        [grad_gain_attn[:, None], grad_gain_ffn[:, None], jnp.zeros((width, 126), jnp.float32)],
        axis=1,
    )
    attn_term = jnp.concatenate(
        [transposed(normed_attn, grad_qkv), transposed(attended, middle_low), gain_block], axis=1
    )
    attn_mine = lax.psum_scatter(attn_term, ("ctx", "fsdp"), scatter_dimension=0, tiled=True)
    offset_value = width + kv_width
    offset_out = offset_value + kv_width
    offset_gain = offset_out + width
    return (
        output.astype(jnp.bfloat16)[None],
        loss_value,
        grad_input[None],
        attn_mine[:, :width],
        attn_mine[:, width:offset_value],
        attn_mine[:, offset_value:offset_out],
        attn_mine[:, offset_out:offset_gain],
        ffn_in_mine[:, :ff_width],
        ffn_in_mine[:, ff_width:],
        down_mine,
        attn_mine[:, offset_gain],
        attn_mine[:, offset_gain + 1],
    )


def solution(mesh):
    in_specs = (
        P("fsdp", "ctx", None),
        P("fsdp", "ctx", None),
        P("fsdp", "ctx"),
        P("fsdp", None),
        P("fsdp", "ctx"),
        P(("ctx", "fsdp"), None),
        P(("ctx", "fsdp"), None),
        P(("ctx", "fsdp"), None),
        P(("ctx", "fsdp"), None),
        P(("ctx", "fsdp"), None),
        P(("ctx", "fsdp"), None),
        P(("ctx", "fsdp"), None),
        P(("ctx", "fsdp")),
        P(("ctx", "fsdp")),
    )
    out_specs = (
        P("fsdp", "ctx", None),
        P(),
        P("fsdp", "ctx", None),
        P(("ctx", "fsdp"), None),
        P(("ctx", "fsdp"), None),
        P(("ctx", "fsdp"), None),
        P(("ctx", "fsdp"), None),
        P(("ctx", "fsdp"), None),
        P(("ctx", "fsdp"), None),
        P(("ctx", "fsdp"), None),
        P(("ctx", "fsdp")),
        P(("ctx", "fsdp")),
    )
    return jax.shard_map(body, mesh=mesh, in_specs=in_specs, out_specs=out_specs, check_vma=False)
```

profile of v0, /device:TPU:0, one launch (start us, length us, event | category | flops | bytes accessed | tf_op | source)
XLA Modules:
  0.0 4298.2 jit_solution(1333154628256226455)
XLA Ops:
  10.4 42.1 all-reduce.4
  53.8 16.3 all-gather.18.cloned.1.call-done
  70.0 2.9 convolution_convert_fusion.1
  76.2 52.0 %all-gather.12.cloned.1.call-done = bf16[2048,512]{1,0:T(8,128)(2,1)} async-done(((bf16[64,512]{1,0:T(8,128)(2,1)}), bf16[2048,512]{1,0:T(8,128)(2,1)}) %all-gather.12.cloned.1.call-update) | async-done | bytes 2097168 | tf_op jit(solution)/shard_map/all_gather | solution.py:100
  128.2 2.9 copy.80
  131.1 1.8 fusion.73
  137.3 19.2 all-gather
  157.7 16.2 all-gather.1
  176.9 2.3 copy.87
  179.1 32.4 all-gather.14.cloned.1.call-done
  211.5 2.3 copy.86
  213.8 76.7 %all-gather.16.cloned.1.call-done = bf16[2048,2048]{1,0:T(8,128)(2,1)} async-done(((bf16[64,2048]{1,0:T(8,128)(2,1)}), bf16[2048,2048]{1,0:T(8,128)(2,1)}) %all-gather.16.cloned.1.call-update) | async-done | bytes 8388624 | tf_op jit(solution)/shard_map/all_gather | solution.py:99
  290.4 12.3 copy.82
  302.8 5.9 fusion.71
  309.1 17.4 conditional.2
  310.7 1.5 copy.83
  312.2 2.4 fusion.2
  315.3 4.5 fusion.8
  319.7 5.5 fusion.4
  328.1 41.1 all-gather.22.cloned.1.call-done
  369.2 4.7 multiply_reduce_fusion.4
  374.2 191.3 %all-gather.24.cloned.1.call-done = bf16[2048,8192]{1,0:T(8,128)(2,1)} async-done(((bf16[64,8192]{1,0:T(8,128)(2,1)}), bf16[2048,8192]{1,0:T(8,128)(2,1)}) %all-gather.24.cloned.1.call-update) | async-done | bytes 33554448 | tf_op jit(solution)/shard_map/all_gather | solution.py:166
  565.5 17.8 fusion.91
  583.2 178.1 %all-gather.26.cloned.1.call-done = bf16[2048,8192]{1,0:T(8,128)(2,1)} async-done(((bf16[64,8192]{1,0:T(8,128)(2,1)}), bf16[2048,8192]{1,0:T(8,128)(2,1)}) %all-gather.26.cloned.1.call-update) | async-done | bytes 33554448 | tf_op jit(solution)/shard_map/all_gather | solution.py:167
  761.3 20.7 multiply_convert_fusion.2
  782.0 175.2 %all-gather.28.cloned.1.call-done = bf16[8192,2048]{1,0:T(8,128)(2,1)} async-done(((bf16[256,2048]{1,0:T(8,128)(2,1)}), bf16[8192,2048]{1,0:T(8,128)(2,1)}) %all-gather.28.cloned.1.call-update) | async-done | bytes 33554448 | tf_op jit(solution)/shard_map/all_gather | solution.py:168
  957.2 14.3 multiply_reduce_fusion.3
  971.5 38.7 all-reduce.3
  1010.8 19.8 multiply_convert_fusion
  1030.7 17.3 fusion.92
  1047.9 17.5 multiply_reduce_fusion
  1067.7 6.3 convolution_convert_fusion
  1074.3 1.5 multiply_reduce_fusion.1
  1075.8 25.5 while.18
  1077.7 9.9 conditional.5
  1080.3 1.6 fusion.23
  1082.0 3.2 fusion.16
  1085.2 1.4 convolution_bitcast_fusion.1
  1090.3 9.9 conditional.5
  1092.9 1.6 fusion.23
  1094.6 3.2 fusion.16
  1097.8 1.4 convolution_bitcast_fusion.1
  1101.3 3.5 copy.108
  1104.8 4.0 reshape.287
  1109.0 3.5 copy.109
  1112.4 4.0 reshape.289
  1116.6 46.2 %fusion.30 = f32[2048,16384]{1,0:T(8,128)} fusion(bf16[128,2048]{1,0:T(8,128)(2,1)S(1)} %copy-done.12, bf16[128,8192]{1,0:T(8,128)(2,1)} %get-tuple-element.348, bf16[128,8192]{1,0:T(8,128)(2,1)} %get-tuple-element.349), kind=kOutput, calls=%fused_computation.38 | convolution fusion | flops 8598323200 | bytes 138936320 | tf_op jit(solution)/shard_map/dot_general | solution.py:44
  1163.5 1.3 copy.92
  1165.3 6.4 fusion.93
  1171.8 8.1 fusion.66
  1181.0 3.4 convolution_add_fusion.1
  1184.4 55.3 %reduce-scatter.15.cloned.1.call-done = bf16[128,512]{1,0:T(8,128)(2,1)} async-done(((bf16[1024,512]{1,0:T(8,128)(2,1)}), bf16[128,512]{1,0:T(8,128)(2,1)}) %reduce-scatter.15.cloned.1.call-update) | async-done | bytes 131088
  1239.7 3.7 fusion.47
  1243.4 1.3 copy.91
  1245.8 12.1 fusion.55
  1259.0 45.1 %concatenate.32 = f32[2048,5248]{1,0:T(8,128)} concatenate(f32[2048,3072]{1,0:T(8,128)} %fusion.55, f32[2048,2048]{1,0:T(8,128)} %fusion.66, f32[2048,1]{1,0:T(8,128)} %copy.91, f32[2048,1]{1,0:T(8,128)S(1)} %copy-done.13, f32[2048,126]{1,0:T(8,128)} %broadcast_in_dim.134), dimensions={1} | concatenate | bytes 85983232 | tf_op jit(solution)/shard_map/concatenate | solution.py:322
  1305.6 25.9 fusion.69
  1334.2 1788.6 %all-reduce.7.cloned.1.call-done = f32[2048,16384]{1,0:T(8,128)} async-done(((f32[2048,16384]{1,0:T(8,128)}), f32[2048,16384]{1,0:T(8,128)}) %all-reduce.7.cloned.1.call-update) | async-done | bytes 134217744
  3122.8 4.9 fusion.87
  3127.7 449.4 %reduce-scatter.9.cloned.1.call-done = f32[64,5248]{1,0:T(8,128)} async-done(((f32[2048,5248]{1,0:T(8,128)}), f32[64,5248]{1,0:T(8,128)}) %reduce-scatter.9.cloned.1.call-update) | async-done | bytes 1343504 | tf_op jit(solution)/shard_map/reduce_scatter | solution.py:325
  3577.1 1.5 slice_reduce_fusion
  3578.7 1.7 fusion.89
  3580.4 2.3 fusion.88
  3582.6 707.7 %reduce-scatter.11.cloned.1.call-done = f32[256,2048]{1,0:T(8,128)} async-done(((f32[8192,2048]{1,0:T(8,128)}), f32[256,2048]{1,0:T(8,128)}) %reduce-scatter.11.cloned.1.call-update) | async-done | bytes 2097168 | tf_op jit(solution)/shard_map/reduce_scatter | solution.py:209
  (157 shorter events, 40.5 us)
Async XLA Ops:
  7.2 169.1 %copy-start.28 = (s32[1,128]{1,0:T(1,128)S(1)}, s32[1,128]{1,0:T(1,128)}, u32[]{:S(2)}) copy-start(s32[1,128]{1,0:T(1,128)} %param.23) | copy-start | bytes 1540
  7.2 62.9 %all-gather.18.cloned.1.call-start = ((), (), s32[]{:S(2)}) async-start(), calls=%async_computation.7 | async-start | bytes 2162688 | tf_op jit(solution)/shard_map/all_gather | solution.py:101
  7.9 120.2 %all-gather.12.cloned.1.call-start = ((), (), s32[]{:S(2)}) async-start(), calls=%async_computation.4 | async-start | bytes 2162688 | tf_op jit(solution)/shard_map/all_gather | solution.py:100
  8.7 168.2 %all-gather.20.cloned.1.call-start = ((), (), s32[]{:S(2)}) async-start(), calls=%async_computation.8 | async-start | bytes 1179648 | tf_op jit(solution)/shard_map/all_gather | solution.py:130
  52.5 250.2 %copy-start.21 = (f32[2048]{0:T(1024)}, f32[2048]{0:T(1024)S(1)}, u32[]{:S(2)}) copy-start(f32[2048]{0:T(1024)S(1)} %convert_element_type.144) | copy-start | bytes 24580
  53.8 249.0 %copy-start.24 = (f32[128]{0:T(128)}, f32[128]{0:T(128)S(1)}, u32[]{:S(2)}) copy-start(f32[128]{0:T(128)S(1)} %add_rsqrt_fusion.1) | copy-start | bytes 1540
  73.0 138.5 %all-gather.14.cloned.1.call-start = ((), (), s32[]{:S(2)}) async-start(), calls=%async_computation.5 | async-start | bytes 1179648 | tf_op jit(solution)/shard_map/all_gather | solution.py:129
  76.1 232.7 %copy-start.17 = (f32[128,64]{0,1:T(8,128)}, f32[128,64]{0,1:T(8,128)S(1)}, u32[]{:S(2)}) copy-start(f32[128,64]{0,1:T(8,128)S(1)} %get-tuple-element.365) | copy-start | bytes 98308
  76.1 232.7 %copy-start.19 = (f32[128,64]{0,1:T(8,128)}, f32[128,64]{0,1:T(8,128)S(1)}, u32[]{:S(2)}) copy-start(f32[128,64]{0,1:T(8,128)S(1)} %get-tuple-element.364) | copy-start | bytes 98308
  133.8 156.6 %all-gather.16.cloned.1.call-start = ((), (), s32[]{:S(2)}) async-start(), calls=%async_computation.6 | async-start | bytes 8650752 | tf_op jit(solution)/shard_map/all_gather | solution.py:99
  134.4 234.8 %all-gather.22.cloned.1.call-start = ((), (), s32[]{:S(2)}) async-start(), calls=%async_computation.9 | async-start | bytes 8650752 | tf_op jit(solution)/shard_map/all_gather | solution.py:102
  135.0 430.5 %all-gather.24.cloned.1.call-start = ((), (), s32[]{:S(2)}) async-start(), calls=%async_computation.10 | async-start | bytes 34603008 | tf_op jit(solution)/shard_map/all_gather | solution.py:166
  135.7 625.6 %all-gather.26.cloned.1.call-start = ((), (), s32[]{:S(2)}) async-start(), calls=%async_computation.11 | async-start | bytes 34603008 | tf_op jit(solution)/shard_map/all_gather | solution.py:167
  136.5 820.7 %all-gather.28.cloned.1.call-start = ((), (), s32[]{:S(2)}) async-start(), calls=%async_computation.12 | async-start | bytes 34603008 | tf_op jit(solution)/shard_map/all_gather | solution.py:168
  137.2 1042.6 %reduce-scatter.13.cloned.1.call-start = ((), (), s32[]{:S(2)}) async-start(), calls=%async_computation.15 | async-start | bytes 1179648
  176.8 888.6 %copy-start.26 = (f32[128]{0:T(128)}, f32[128]{0:T(128)S(1)}, u32[]{:S(2)}) copy-start(f32[128]{0:T(128)S(1)} %convert_bitcast_fusion.2) | copy-start | bytes 1540
  290.4 12.4 copy-start
  302.8 6.3 copy-start.14
  312.2 3.0 copy-start.16
  326.5 42.7 copy-start.6
  328.1 45.9 %copy-start.7 = (bf16[128,8,4,64]{0,3,2,1:T(8,128)(2,1)}, bf16[128,8,4,64]{0,3,2,1:T(8,128)(2,1)S(1)}, u32[]{:S(2)}) copy-start(bf16[128,8,4,64]{0,3,2,1:T(8,128)(2,1)S(1)} %fusion.62) | copy-start | bytes 1572868
  374.2 387.2 %copy-start.11 = (bf16[128,2048]{1,0:T(8,128)(2,1)}, bf16[128,2048]{1,0:T(8,128)(2,1)S(1)}, u32[]{:S(2)}) copy-start(bf16[128,2048]{1,0:T(8,128)(2,1)S(1)} %multiply_convert_fusion.3) | copy-start | bytes 1572868
  583.2 373.9 %copy-start.9 = (bf16[1,128,2048]{2,1,0:T(8,128)(2,1)S(1)}, bf16[1,128,2048]{2,1,0:T(8,128)(2,1)}, u32[]{:S(2)}) copy-start(bf16[1,128,2048]{2,1,0:T(8,128)(2,1)} %param.22) | copy-start | bytes 1572868
  971.5 94.0 %copy-start.4 = (f32[128,2048]{1,0:T(8,128)}, f32[128,2048]{1,0:T(8,128)S(1)}, u32[]{:S(2)}) copy-start(f32[128,2048]{1,0:T(8,128)S(1)} %get-tuple-element.371) | copy-start | bytes 3145732
  1066.7 1.0 copy-start.2
  1101.3 15.3 copy-start.12
  1108.9 130.8 %reduce-scatter.15.cloned.1.call-start = ((), (), s32[]{:S(2)}) async-start(), calls=%async_computation.16 | async-start | bytes 1179648
  1116.5 2006.3 %all-reduce.7.cloned.1.call-start = ((), (), s32[]{:S(2)}) async-start(), calls=%async_computation.17 | async-start | bytes 268435456
  1162.8 0.7 copy-start.23
  1162.8 2.0 copy-start.18
  1162.8 2.4 copy-start.20
  1162.8 2414.4 %reduce-scatter.9.cloned.1.call-start = ((), (), s32[]{:S(2)}) async-start(), calls=%async_computation.13 | async-start | bytes 44335104 | tf_op jit(solution)/shard_map/reduce_scatter | solution.py:325
  1164.9 6.8 copy-start.3
  1164.9 6.8 copy-start.8
  1171.8 68.0 %copy-start.1 = (bf16[1,128,2048]{2,1,0:T(8,128)(2,1)S(1)}, bf16[1,128,2048]{2,1,0:T(8,128)(2,1)}, u32[]{:S(2)}) copy-start(bf16[1,128,2048]{2,1,0:T(8,128)(2,1)} %param.21) | copy-start | bytes 1572868
  1171.8 68.0 %copy-start.22 = (f32[2048]{0:T(1024)S(1)}, f32[2048]{0:T(1024)}, u32[]{:S(2)}) copy-start(f32[2048]{0:T(1024)} %copy-done.21) | copy-start | bytes 24580
  1171.8 67.9 %copy-start.25 = (f32[128]{0:T(128)S(1)}, f32[128]{0:T(128)}, u32[]{:S(2)}) copy-start(f32[128]{0:T(128)} %copy-done.24) | copy-start | bytes 1540
  1245.8 13.2 copy-start.13
  1304.1 1.3 copy-start.5
  1304.1 1.4 copy-start.10
  1304.1 1.4 copy-start.27
  1304.2 2986.2 %reduce-scatter.11.cloned.1.call-start = ((), (), s32[]{:S(2)}) async-start(), calls=%async_computation.14 | async-start | bytes 69206016 | tf_op jit(solution)/shard_map/reduce_scatter | solution.py:209
  1331.5 1.4 copy-start.15
Sparse Core Ops, SparseCore 0:
  10.9 59.1 all-gather.17
  72.9 55.2 all-gather.11
  130.9 39.0 all-gather.19
  172.5 38.9 all-gather.13
  214.2 76.1 all-gather.15
  293.1 76.0 all-gather.21
  372.1 193.3 all-gather.23
  568.3 192.9 all-gather.25
  764.2 192.9 all-gather.27
  1109.0 64.4 reduce-scatter.12
  1177.3 62.3 reduce-scatter.14
  1246.0 1876.7 all-reduce.6
  3125.1 451.9 reduce-scatter.8
  3579.9 710.3 reduce-scatter.10
where the time goes:
time: 4310 us; the launch traced here: 4300 us
  waiting for transfers between devices  3770 us (87%)
  matrix products  259 us (6%)
  blocking collectives  116 us (3%)
  local copies, waits for them, and re-layouts  110 us (3%)
    unnamed x17, waiting for transfers between devices  1850 us
    reduce_scatter x1, waiting for transfers between devices, body(): lax.psum_scatter(transposed(hidden, grad_low), ('ctx', 'fsdp'), scatter_d...  708 us
    reduce_scatter x1, waiting for transfers between devices, body(): lax.psum_scatter(attn_term, ('ctx', 'fsdp'), scatter_dimension=0, tiled=T...  449 us
    all_gather x1, waiting for transfers between devices, body(): lax.all_gather(w_gate, ('ctx', 'fsdp'), axis=0, tiled=True)  191 us
    all_gather x1, waiting for transfers between devices, body(): lax.all_gather(w_up, ('ctx', 'fsdp'), axis=0, tiled=True)  178 us
    all_gather x1, waiting for transfers between devices, body(): lax.all_gather(w_down, ('ctx', 'fsdp'), axis=0, tiled=True)  175 us
    dot_general x4, matrix products, transposed(): lax.dot_general(left, right, (((0,), (0,)), ((), ())), preferred_element_...  92.2 us
  transfers between devices with their start and end apart: 14, of which 12 were waited for; matrix products, arithmetic and copies ran while one was open for 6% of the time, Pallas kernels for 0%

commit v1 on v0

v1 whole, which is shorter than its diff:
```python
import functools
import math

import jax
import jax.numpy as jnp
import numpy as np
from jax import lax
from jax.experimental import pallas as pl
from jax.experimental.pallas import tpu as pltpu
from jax.sharding import PartitionSpec as P

HEADS = 32
KV_HEADS = 8
HEAD_DIM = 64
SPAN = 128
EPSILON = 1e-05
HIDE = -1e30
BF = jnp.bfloat16
F32 = jnp.float32


def rope_rates(head_width):
    frequency = 1.0 / 500000.0 ** (np.arange(0, head_width, 2) / head_width)
    wavelength = 2.0 * np.pi / frequency
    blend_share = (8192.0 / wavelength - 1.0) / 3.0
    blended = (1.0 - blend_share) * frequency / 32.0 + blend_share * frequency
    frequency = np.where(
        wavelength < 2048.0, frequency, np.where(wavelength > 8192.0, frequency / 32.0, blended)
    )
    return np.concatenate([frequency, frequency]).astype(np.float32)


def turn_matrix(heads):
    half = HEAD_DIM // 2
    one = np.zeros((HEAD_DIM, HEAD_DIM), np.float32)
    for i in range(half):
        one[i + half, i] = -1.0
        one[i, i + half] = 1.0
    return np.kron(np.eye(heads, dtype=np.float32), one)


def mm(left, right):
    return jnp.dot(left, right, preferred_element_type=F32)


def mm_t(left, right):
    return lax.dot_general(left, right, (((0,), (0,)), ((), ())), preferred_element_type=F32)


def against(left, right):
    return lax.dot_general(left, right, (((1,), (1,)), ((), ())), preferred_element_type=F32)


def pick(array, index, axis=0):
    return lax.dynamic_index_in_dim(array, index, axis, keepdims=False)


class Links:
    def __init__(self):
        self.n = lax.axis_size("ctx")
        self.m = lax.axis_size("fsdp")
        self.ring = self.n // 2
        self.c = lax.axis_index("ctx")
        self.f = lax.axis_index("fsdp")
        self.a = self.c // 2
        self.b = self.c % 2

    def shift(self, x, da, dq):
        perm = [
            (a * 2 + b, ((a + da) % self.ring) * 2 + (b ^ dq))
            for a in range(self.ring)
            for b in range(2)
        ]
        return lax.ppermute(x, "ctx", perm)

    def flip(self, x, axis, bit):
        size = self.n if axis == "ctx" else self.m
        return lax.ppermute(x, axis, [(i, i ^ bit) for i in range(size)])

    def total(self, x, axes):
        for axis in axes:
            bit = 1
            while bit < (self.n if axis == "ctx" else self.m):
                x = x + self.flip(x, axis, bit)
                bit *= 2
        return x

    def gather_ctx(self, x):
        out = []
        for r in range(self.ring):
            if r:
                x = self.shift(x, 1, 0)
            out.append((x, self.shift(x, 0, 1)))
        return out

    def scatter_order(self):
        return list(range(1, self.ring)) + [0]

    def scatter_ctx(self, part):
        held = None
        for r in self.scatter_order():
            mine, other = part(r)
            term = mine + self.shift(other.astype(BF), 0, 1).astype(F32)
            if held is not None:
                term = term + self.shift(held.astype(BF), 1, 0).astype(F32)
            held = term
        return held

    def exchange_ctx(self, pieces):
        out = pieces
        zeros = (0,) * (pieces.ndim - 1)
        for da in range(self.ring):
            for dq in range(2):
                if da == 0 and dq == 0:
                    continue
                dest = ((self.a + da) % self.ring) * 2 + (self.b ^ dq)
                src = ((self.a + self.ring - da) % self.ring) * 2 + (self.b ^ dq)
                got = self.shift(pick(pieces, dest), da, dq)
                out = lax.dynamic_update_slice(out, got[None], (src,) + zeros)
        return out

    def gather_fsdp(self, x, axis):
        held = [(0, x)]
        bit = self.m // 2
        while bit:
            held = held + [(mark | bit, self.flip(block, "fsdp", bit)) for mark, block in held]
            bit //= 2
        shape = x.shape[:axis] + (self.m,) + x.shape[axis:]
        out = jnp.zeros(shape, x.dtype)
        for mark, block in held:
            start = [0] * len(shape)
            start[axis] = self.f ^ mark
            out = lax.dynamic_update_slice(out, jnp.expand_dims(block, axis), tuple(start))
        return out

    def scatter_fsdp(self, x, axis):
        bit = 1
        while bit < self.m:
            mine = (self.f // bit) % 2
            shape = x.shape[:axis] + (x.shape[axis] // 2, 2) + x.shape[axis + 1 :]
            x = x.reshape(shape)
            sent = self.flip(pick(x, 1 - mine, axis + 1).astype(BF), "fsdp", bit)
            x = pick(x, mine, axis + 1) + sent.astype(F32)
            bit *= 2
        return lax.squeeze(x, (axis,))


def attend_kernel(heads, q_ref, k_ref, v_ref, info_q, info_k, o_ref, lse_ref, kpad, vpad):
    width = heads * HEAD_DIM
    head_of = lax.broadcasted_iota(jnp.int32, (1, width), 1) // HEAD_DIM

    @pl.when(pl.program_id(0) == 0)
    def _():
        for h in range(heads):
            kpad[h] = jnp.where(head_of == h, k_ref[...], 0).astype(BF)
            vpad[h] = jnp.where(head_of == h, v_ref[...], 0).astype(BF)

    seen = (info_q[:, 0:1] == info_k[0:1, :]) & (info_k[1:2, :] <= info_q[:, 1:2])
    bias = jnp.where(seen, 0.0, HIDE)
    lane = lax.broadcasted_iota(jnp.int32, (1, 128), 1)
    q = q_ref[...]
    out = jnp.zeros((q.shape[0], width), F32)
    lse = jnp.zeros((q.shape[0], 128), F32)
    for h in range(heads):
        s = against(q, kpad[h]) + bias
        top = jnp.max(s, axis=1, keepdims=True)
        p = jnp.exp(s - top)
        total = jnp.sum(p, axis=1, keepdims=True)
        out = out + mm(p.astype(BF), vpad[h]) / total
        lse = jnp.where(lane == h, top + jnp.log(total), lse)
    o_ref[...] = out.astype(BF)
    lse_ref[...] = lse


def attend_back_kernel(
    heads, q_ref, g_ref, k_ref, v_ref, info_q, info_k, lse_ref,
    dq_ref, dk_ref, dv_ref, kpad, vpad,
):
    width = heads * HEAD_DIM
    head_of = lax.broadcasted_iota(jnp.int32, (1, width), 1) // HEAD_DIM

    @pl.when(pl.program_id(0) == 0)
    def _():
        for h in range(heads):
            kpad[h] = jnp.where(head_of == h, k_ref[...], 0).astype(BF)
            vpad[h] = jnp.where(head_of == h, v_ref[...], 0).astype(BF)
        dk_ref[...] = jnp.zeros_like(dk_ref)
        dv_ref[...] = jnp.zeros_like(dv_ref)

    seen = (info_q[:, 0:1] == info_k[0:1, :]) & (info_k[1:2, :] <= info_q[:, 1:2])
    bias = jnp.where(seen, 0.0, HIDE)
    q = q_ref[...]
    g = g_ref[...]
    dq = jnp.zeros((q.shape[0], width), F32)
    for h in range(heads):
        p = jnp.exp(against(q, kpad[h]) + (bias - lse_ref[:, h : h + 1]))
        dp = against(g, vpad[h])
        delta = jnp.sum(p * dp, axis=1, keepdims=True)
        ds = (p * (dp - delta)).astype(BF)
        dq = dq + mm(ds, kpad[h])
        own = head_of == h
        dk_ref[...] += mm_t(ds, jnp.where(own, q, 0).astype(BF))
        dv_ref[...] += mm_t(p.astype(BF), jnp.where(own, g, 0).astype(BF))
    dq_ref[...] = dq * (1.0 / math.sqrt(HEAD_DIM))


def attend_specs(rows, stream, width):
    by_row = pl.BlockSpec((rows, width), lambda i: (i, 0))
    whole = pl.BlockSpec((stream, width), lambda i: (0, 0))
    mark = pl.BlockSpec((rows, 128), lambda i: (i, 0))
    marks = pl.BlockSpec((8, stream), lambda i: (0, 0))
    return by_row, whole, mark, marks


def attend(heads, q, k, v, info_q, info_k):
    stream, width = q.shape
    rows = 256 if stream <= 1024 else 128
    by_row, whole, mark, marks = attend_specs(rows, stream, width)
    return pl.pallas_call(
        functools.partial(attend_kernel, heads),
        grid=(stream // rows,),
        in_specs=[by_row, whole, whole, mark, marks],
        out_specs=[by_row, mark],
        out_shape=[
            jax.ShapeDtypeStruct((stream, width), BF),
            jax.ShapeDtypeStruct((stream, 128), F32),
        ],
        scratch_shapes=[pltpu.VMEM((heads, stream, width), BF)] * 2,
        compiler_params=pltpu.CompilerParams(vmem_limit_bytes=40 << 20),
        cost_estimate=pl.CostEstimate(
            flops=4 * stream * stream * heads * 256,
            bytes_accessed=8 * stream * width,
            transcendentals=stream * stream * heads,
        ),
    )(q, k, v, info_q, info_k)


def attend_back(heads, q, g, k, v, info_q, info_k, lse):
    stream, width = q.shape
    rows = 256 if stream <= 1024 else 128
    by_row, whole, mark, marks = attend_specs(rows, stream, width)
    return pl.pallas_call(
        functools.partial(attend_back_kernel, heads),
        grid=(stream // rows,),
        in_specs=[by_row, by_row, whole, whole, mark, marks, mark],
        out_specs=[by_row, whole, whole],
        out_shape=[jax.ShapeDtypeStruct((stream, width), F32)] * 3,
        scratch_shapes=[pltpu.VMEM((heads, stream, width), BF)] * 2,
        compiler_params=pltpu.CompilerParams(vmem_limit_bytes=40 << 20),
        cost_estimate=pl.CostEstimate(
            flops=10 * stream * stream * heads * 256,
            bytes_accessed=20 * stream * width,
            transcendentals=stream * stream * heads,
        ),
    )(q, g, k, v, info_q, info_k, lse)


def norm_back(grad_scaled, unit_rows, inverse):
    return inverse * (
        grad_scaled - unit_rows * jnp.mean(grad_scaled * unit_rows, axis=1, keepdims=True)
    )


def rms_inverse(values):
    return lax.rsqrt(jnp.mean(values * values, axis=1, keepdims=True) + EPSILON)


def body(
    tokens,
    teacher,
    valid_mask,
    lengths,
    span_order,
    w_query,
    w_key,
    w_value,
    w_out,
    w_gate,
    w_up,
    w_down,
    gain_attn,
    gain_ffn,
):
    net = Links()
    n, m, ring = net.n, net.m, net.ring
    x_low = tokens[0]
    tok_rows, width = x_low.shape
    rows = w_query.shape[0]
    heads = HEADS // n
    q_width = heads * HEAD_DIM
    sharers = n // KV_HEADS
    ff_slice = w_gate.shape[1] // n
    stream = tok_rows * n
    spans = tok_rows // SPAN

    own_spans = jnp.where(
        lax.broadcasted_iota(jnp.int32, (n, spans), 0) == net.c, span_order[0][None, :], 0
    ).reshape(1, n * spans)
    own_count = jnp.sum(valid_mask).astype(jnp.int32).reshape(1, 1)
    small = net.total(jnp.concatenate([own_spans, own_count], axis=1), ["ctx"])
    order_all = small[0, : n * spans].reshape(n, spans)
    valid_count = net.total(small[:, n * spans :], ["fsdp"])[0, 0].astype(F32)

    token_blocks = net.gather_ctx(x_low)
    gain_a = gain_attn.astype(F32)[:, None]
    gain_f = gain_ffn.astype(F32)[:, None]

    def folded(weight, gain):
        return (weight.astype(F32) * gain).astype(BF)

    def by_slice(weight, count):
        return jnp.swapaxes(weight.reshape(rows, count, weight.shape[1] // count), 0, 1)

    def kv_slices(weight):
        return jnp.repeat(by_slice(weight, KV_HEADS), sharers, axis=0)

    qkv_pieces = jnp.concatenate(
        [
            by_slice(folded(w_query, gain_a), n),
            kv_slices(folded(w_key, gain_a)),
            kv_slices(folded(w_value, gain_a)),
        ],
        axis=2,
    )
    qkv_w = net.gather_fsdp(net.exchange_ctx(qkv_pieces), 1).reshape(width, q_width + 2 * HEAD_DIM)
    wq = qkv_w[:, :q_width]
    wk = jnp.tile(qkv_w[:, q_width : q_width + HEAD_DIM], (1, heads))
    wv = jnp.tile(qkv_w[:, q_width + HEAD_DIM :], (1, heads))
    turn = jnp.asarray(turn_matrix(2 * heads), BF)
    w_lin = jnp.concatenate([wq, wk, wv], axis=1)
    w_turn = mm(w_lin[:, : 2 * q_width], turn).astype(BF)
    w_attn = jnp.concatenate([w_lin, w_turn], axis=1)
    out_w = net.gather_fsdp(w_out, 0).reshape(q_width, width)

    def slot_source(r, q):
        return ((net.a + ring - r) % ring) * 2 + (net.b ^ q)

    spans_here = jnp.concatenate(
        [pick(order_all, slot_source(r, q)) for r in range(ring) for q in range(2)]
    )
    place = (
        spans_here[:, None] * SPAN + lax.broadcasted_iota(jnp.int32, (n * spans, SPAN), 1)
    ).reshape(stream)
    seq_ends = jnp.cumsum(lengths[0])
    passed = seq_ends[None, :] <= place[:, None]
    segment = jnp.sum(passed.astype(jnp.int32), axis=1)
    seq_begin = jnp.sum(jnp.where(passed, lengths[0][None, :], 0), axis=1)
    rates = jnp.asarray(rope_rates(HEAD_DIM)[: HEAD_DIM // 2])
    angles = (place - seq_begin).astype(F32)[:, None] * rates[None, :]
    cosines = jnp.tile(jnp.cos(angles), (1, 2 * 2 * heads))
    sines = jnp.tile(jnp.sin(angles), (1, 2 * 2 * heads))
    info_q = jnp.pad(jnp.stack([segment, place], axis=1), ((0, 0), (0, 126)))
    info_k = jnp.pad(jnp.stack([segment, place], axis=0), ((0, 6), (0, 0)))
    score_scale = 1.0 / math.sqrt(HEAD_DIM)

    x_all, inverse_all, q_all, k_all, v_all = [], [], [], [], []
    pair_rows = 2 * tok_rows
    for r in range(ring):
        x_pair = jnp.concatenate(token_blocks[r], axis=0)
        inverse = rms_inverse(x_pair.astype(F32))
        act = mm(x_pair, w_attn)
        cos_r = cosines[r * pair_rows : (r + 1) * pair_rows]
        sin_r = sines[r * pair_rows : (r + 1) * pair_rows]
        rot = (act[:, : 2 * q_width] * cos_r + act[:, 3 * q_width :] * sin_r) * inverse
        x_all.append(x_pair)
        inverse_all.append(inverse)
        q_all.append((rot[:, :q_width] * score_scale).astype(BF))
        k_all.append(rot[:, q_width:].astype(BF))
        v_all.append((act[:, 2 * q_width : 3 * q_width] * inverse).astype(BF))
    x_all = jnp.concatenate(x_all, axis=0)
    inverse_all = jnp.concatenate(inverse_all, axis=0)
    q_all = jnp.concatenate(q_all, axis=0)
    k_all = jnp.concatenate(k_all, axis=0)
    v_all = jnp.concatenate(v_all, axis=0)
    attended, lse = attend(heads, q_all, k_all, v_all, info_q, info_k)

    def split_pair(block):
        return block[:tok_rows], block[tok_rows:]

    def pair_of(array, r):
        return array[r * pair_rows : (r + 1) * pair_rows]

    inputs = x_low.astype(F32)
    middle = inputs + net.scatter_ctx(lambda r: split_pair(mm(pair_of(attended, r), out_w)))

    gate_up_pieces = jnp.concatenate(
        [by_slice(folded(w_gate, gain_f), n), by_slice(folded(w_up, gain_f), n)], axis=2
    )
    gate_up_w = net.gather_fsdp(net.exchange_ctx(gate_up_pieces), 1).reshape(width, 2 * ff_slice)
    down_w = net.gather_fsdp(w_down, 0).reshape(ff_slice, width)

    inverse_ffn = rms_inverse(middle)
    unit_ffn = middle * inverse_ffn
    unit_blocks = net.gather_ctx(unit_ffn.astype(BF))
    z_pairs = [jnp.concatenate(blocks, axis=0) for blocks in unit_blocks]
    acts, hiddens = {}, {}

    def down_part(r):
        both = mm(z_pairs[r], gate_up_w)
        gate, up = both[:, :ff_slice], both[:, ff_slice:]
        acts[r] = (gate, up)
        hiddens[r] = (gate * jax.nn.sigmoid(gate) * up).astype(BF)
        return split_pair(mm(hiddens[r], down_w))

    out_full = middle + net.scatter_ctx(down_part)

    valid_f = valid_mask[0].astype(F32)[:, None]
    missed = (out_full - teacher[0].astype(F32)) * valid_f
    square_sum = net.total(jnp.sum(missed * missed).reshape(1, 1), ["ctx", "fsdp"])[0, 0]
    loss_value = 0.5 * square_sum / (width * valid_count)
    grad_out = missed * ((tok_rows * n * m) / valid_count)

    grad_blocks = net.gather_ctx(grad_out.astype(BF))
    grad_pairs = [jnp.concatenate(blocks, axis=0) for blocks in grad_blocks]
    grad_acts = {}

    def unit_part(r):
        gate, up = acts[r]
        grad_hidden = against(grad_pairs[r], down_w)
        share = jax.nn.sigmoid(gate)
        grad_gate = grad_hidden * up * share * (1.0 + gate * (1.0 - share))
        grad_up = grad_hidden * (gate * share)
        grad_acts[r] = jnp.concatenate([grad_gate.astype(BF), grad_up.astype(BF)], axis=1)
        return split_pair(against(grad_acts[r], gate_up_w))

    grad_unit = net.scatter_ctx(unit_part)
    grad_middle = grad_out + norm_back(grad_unit, unit_ffn, inverse_ffn)
    middle_low = grad_middle.astype(BF)

    def joined(items):
        return jnp.concatenate([items[r] for r in range(ring)], axis=0)

    down_term = mm_t(joined(hiddens), joined(grad_pairs))
    gate_up_term = mm_t(joined(z_pairs), joined(grad_acts))
    grad_down = net.scatter_fsdp(down_term.reshape(m, ff_slice // m, width), 0)
    gate_up_mine = net.exchange_ctx(
        net.scatter_fsdp(gate_up_term.reshape(n, m, rows, 2 * ff_slice), 1).astype(BF)
    ).astype(F32)

    middle_pairs = [jnp.concatenate(blocks, axis=0) for blocks in net.gather_ctx(middle_low)]
    grad_attended = jnp.concatenate(
        [against(pair, out_w).astype(BF) for pair in middle_pairs], axis=0
    )
    grad_q, grad_k, grad_v = attend_back(
        heads, q_all, grad_attended, k_all, v_all, info_q, info_k, lse
    )
    grad_rot = jnp.concatenate([grad_q, grad_k], axis=1)
    sined = grad_rot * sines
    sined_high = sined.astype(BF)
    sined_low = (sined - sined_high.astype(F32)).astype(BF)
    turned = against(sined_high, turn) + against(sined_low, turn)
    grad_act = jnp.concatenate([grad_rot * cosines + turned, grad_v], axis=1)
    grad_act_low = grad_act.astype(BF)
    grad_attn = net.scatter_ctx(lambda r: split_pair(against(pair_of(grad_act_low, r), w_lin)))
    inverse_attn = rms_inverse(inputs)
    grad_input = grad_middle + norm_back(grad_attn, inputs * inverse_attn, inverse_attn)

    qkv_term = mm_t(x_all, (grad_act * inverse_all).astype(BF))

    def fold(block):
        return jnp.sum(block.reshape(width, heads, HEAD_DIM), axis=1)

    qkv_term = jnp.concatenate(
        [
            qkv_term[:, :q_width],
            fold(qkv_term[:, q_width : 2 * q_width]),
            fold(qkv_term[:, 2 * q_width :]),
        ],
        axis=1,
    )
    qkv_mine = net.exchange_ctx(
        net.scatter_fsdp(qkv_term.reshape(n, m, rows, q_width + 2 * HEAD_DIM), 1).astype(BF)
    ).astype(F32)
    out_term = mm_t(attended, joined(middle_pairs))
    grad_w_out = net.scatter_fsdp(out_term.reshape(m, rows, width), 0)

    def laid(pieces):
        return jnp.swapaxes(pieces, 0, 1).reshape(rows, pieces.shape[0] * pieces.shape[2])

    def kv_laid(pieces):
        return laid(jnp.sum(pieces.reshape(KV_HEADS, sharers, rows, HEAD_DIM), axis=1))

    raw_q = laid(qkv_mine[:, :, :q_width])
    raw_k = kv_laid(qkv_mine[:, :, q_width : q_width + HEAD_DIM])
    raw_v = kv_laid(qkv_mine[:, :, q_width + HEAD_DIM :])
    raw_gate = laid(gate_up_mine[:, :, :ff_slice])
    raw_up = laid(gate_up_mine[:, :, ff_slice:])

    def gain_sum(pairs):
        return sum(jnp.sum(w.astype(F32) * g, axis=1) for w, g in pairs)

    grad_gain_attn = gain_sum([(w_query, raw_q), (w_key, raw_k), (w_value, raw_v)])
    grad_gain_ffn = gain_sum([(w_gate, raw_gate), (w_up, raw_up)])
    return (
        out_full.astype(BF)[None],
        loss_value,
        grad_input[None],
        raw_q * gain_a,
        raw_k * gain_a,
        raw_v * gain_a,
        grad_w_out,
        raw_gate * gain_f,
        raw_up * gain_f,
        grad_down,
        grad_gain_attn,
        grad_gain_ffn,
    )


def solution(mesh):
    token_spec = P("fsdp", "ctx", None)
    row_spec = P(("ctx", "fsdp"), None)
    gain_spec = P(("ctx", "fsdp"))
    in_specs = (
        token_spec,
        token_spec,
        P("fsdp", "ctx"),
        P("fsdp", None),
        P("fsdp", "ctx"),
        *([row_spec] * 7),
        gain_spec,
        gain_spec,
    )
    out_specs = (token_spec, P(), token_spec, *([row_spec] * 7), gain_spec, gain_spec)
    return jax.shard_map(body, mesh=mesh, in_specs=in_specs, out_specs=out_specs, check_vma=False)
```

time: 4310 us -> 941 us (0.22)
  waiting for transfers between devices: 3770 us -> 334 us
  matrix products: 259 us -> 108 us
  local copies, waits for them, and re-layouts: 110 us -> 248 us
  starting transfers between devices: 1.13 us -> 120 us
  blocking collectives: 116 us -> 0 us
  other arithmetic: 21.3 us -> 80.4 us
    unnamed x17 -> x0, waiting for transfers between devices: 1850 us -> none
    reduce_scatter x2 -> x0, waiting for transfers between devices: 1160 us -> none  [the longest x1 708 us: body(): lax.psum_scatter(transposed(hidden, grad_low), ('ctx', 'fsdp'), scatter_d...]
    all_gather x9 -> x0, waiting for transfers between devices: 763 us -> none  [the longest x1 191 us: body(): lax.all_gather(w_gate, ('ctx', 'fsdp'), axis=0, tiled=True)]
    ppermute x0 -> x114, waiting for transfers between devices: none -> 334 us  [the longest x84 301 us: shift(): return lax.ppermute(x, 'ctx', perm)]
    dot_general x23 -> x22, matrix products: 184 us -> 63.3 us  [the longest x18 35.4 us: mm(): return jnp.dot(left, right, preferred_element_type=F32)]
    ppermute x0 -> x114, starting transfers between devices: none -> 120 us  [the longest x84 93.4 us: shift(): return lax.ppermute(x, 'ctx', perm)]
    dynamic_update_slice x2 -> x44, local copies, waits for them, and re-layouts: 2.18 us -> 110 us  [the longest x28 88.7 us: exchange_ctx(): out = lax.dynamic_update_slice(out, got[None], (src,) + zeros)]
  transfers between devices with their start and end apart: 14 -> 114, of which waited for: 12 -> 53; matrix products, arithmetic and copies ran while one was open for 6% -> 44% of each run, Pallas kernels for 0% -> 3%
where the time goes in v1:
time: 941 us; the launch traced here: 929 us
  waiting for transfers between devices  334 us (35%)
  local copies, waits for them, and re-layouts  248 us (26%)
  starting transfers between devices  120 us (13%)
  matrix products  108 us (11%)
  other arithmetic  80.4 us (9%)
  Pallas kernels  26.5 us (3%)
  between operations  11.3 us (1%)
    ppermute x84, waiting for transfers between devices, shift(): return lax.ppermute(x, 'ctx', perm)  301 us
    ppermute x84, starting transfers between devices, shift(): return lax.ppermute(x, 'ctx', perm)  93.4 us
    dynamic_update_slice x28, local copies, waits for them, and re-layouts, exchange_ctx(): out = lax.dynamic_update_slice(out, got[None], (src,) + zeros)  88.7 us
    unnamed x209, local copies, waits for them, and re-layouts  51.4 us
    dot_general x18, matrix products, against(): lax.dot_general(left, right, (((1,), (1,)), ((), ())), preferred_element_...  44.6 us
    dot_general x18, matrix products, mm(): return jnp.dot(left, right, preferred_element_type=F32)  35.4 us
    ppermute x30, waiting for transfers between devices, flip(): return lax.ppermute(x, axis, [(i, i ^ bit) for i in range(size)])  33.9 us
    dot_general x4, matrix products, mm_t(): lax.dot_general(left, right, (((0,), (0,)), ((), ())), preferred_element_...  27.9 us
  transfers between devices with their start and end apart: 114, of which 53 were waited for; matrix products, arithmetic and copies ran while one was open for 44% of the time, Pallas kernels for 3%

profile of v1, /device:TPU:0, one launch (start us, length us, event | category | flops | bytes accessed | tf_op | source)
XLA Modules:
  0.0 928.5 jit_solution(10631796895120767798)
XLA Ops:
  22.6 4.5 fusion.144
  52.8 5.2 concatenate.161
  68.1 3.6 collective-permute-start.5
  73.5 13.5 %collective-permute-done.5 = bf16[64,384]{1,0:T(8,128)(2,1)S(1)} collective-permute-done((bf16[64,384]{1,0:T(8,128)(2,1)S(1)}, bf16[64,384]{1,0:T(8,128)(2,1)S(1)}, u32[]{:S(2)}, u32[]{:S(2)}) %collective-permute-start.5) | collective-permute-done | bytes 49184 | tf_op jit(solution)/shard_map/ppermute | solution.py:74
  87.1 10.9 %collective-permute-start.33 = (bf16[64,2048]{1,0:T(8,128)(2,1)}, bf16[64,2048]{1,0:T(8,128)(2,1)}, u32[]{:S(2)}, u32[]{:S(2)}) collective-permute-start(bf16[64,2048]{1,0:T(8,128)(2,1)} %bitcast.322), channel_id=1, source_target_pairs={{0,12},{4,8},{8,20},{12,16},{16,28},{20,24},{24,4},{28,0},{1,13},{... | collective-permute-start | bytes 786440 | tf_op jit(solution)/shard_map/ppermute | solution.py:74
  99.4 4.1 collective-permute-start.37
  162.2 10.4 %dynamic_update_slice.147 = bf16[8,64,2048]{2,0,1:T(8,128)(2,1)} dynamic-update-slice(bf16[8,64,2048]{2,0,1:T(8,128)(2,1)} %pad_maximum_fusion.1, bf16[1,64,2048]{2,0,1:T(2,128)(2,1)} %copy.192, s32[]{:T(128)S(6)} %select_n.342, s32[]{:T(128)} %constant.418.clone.1, s32[]{:T(128)} %constant.418.clone.1) | dynamic-update-slice | bytes 524292 | tf_op jit(solution)/shard_map/dynamic_update_slice | solution.py:119
  172.6 10.3 %dynamic_update_slice.148 = bf16[8,64,2048]{2,0,1:T(8,128)(2,1)} dynamic-update-slice(bf16[8,64,2048]{2,0,1:T(8,128)(2,1)} %dynamic_update_slice.147, bf16[1,64,2048]{2,0,1:T(2,128)(2,1)} %copy.193, s32[]{:T(128)S(6)} %select_n.346, s32[]{:T(128)} %constant.418.clone.1, s32[]{:T(128)} %constant.418.clone.1) | dynamic-update-slice | bytes 524292 | tf_op jit(solution)/shard_map/dynamic_update_slice | solution.py:119
  182.9 10.3 %dynamic_update_slice.149 = bf16[8,64,2048]{2,0,1:T(8,128)(2,1)} dynamic-update-slice(bf16[8,64,2048]{2,0,1:T(8,128)(2,1)} %dynamic_update_slice.148, bf16[1,64,2048]{2,0,1:T(2,128)(2,1)} %copy.194, s32[]{:T(128)S(6)} %select_n.348, s32[]{:T(128)} %constant.418.clone.1, s32[]{:T(128)} %constant.418.clone.1) | dynamic-update-slice | bytes 524292 | tf_op jit(solution)/shard_map/dynamic_update_slice | solution.py:119
  193.1 10.3 %dynamic_update_slice.150 = bf16[8,64,2048]{2,0,1:T(8,128)(2,1)} dynamic-update-slice(bf16[8,64,2048]{2,0,1:T(8,128)(2,1)} %dynamic_update_slice.149, bf16[1,64,2048]{2,0,1:T(2,128)(2,1)} %copy.195, s32[]{:T(128)S(6)} %select_n.350, s32[]{:T(128)} %constant.418.clone.1, s32[]{:T(128)} %constant.418.clone.1) | dynamic-update-slice | bytes 524292 | tf_op jit(solution)/shard_map/dynamic_update_slice | solution.py:119
  203.4 10.3 %dynamic_update_slice.151 = bf16[8,64,2048]{2,0,1:T(8,128)(2,1)} dynamic-update-slice(bf16[8,64,2048]{2,0,1:T(8,128)(2,1)} %dynamic_update_slice.150, bf16[1,64,2048]{2,0,1:T(2,128)(2,1)} %copy.196, s32[]{:T(128)S(6)} %select_n.351, s32[]{:T(128)} %constant.418.clone.1, s32[]{:T(128)} %constant.418.clone.1) | dynamic-update-slice | bytes 524292 | tf_op jit(solution)/shard_map/dynamic_update_slice | solution.py:119
  213.6 10.3 %dynamic_update_slice.152 = bf16[8,64,2048]{2,0,1:T(8,128)(2,1)} dynamic-update-slice(bf16[8,64,2048]{2,0,1:T(8,128)(2,1)} %dynamic_update_slice.151, bf16[1,64,2048]{2,0,1:T(2,128)(2,1)} %copy.197, s32[]{:T(128)S(6)} %select_n.344, s32[]{:T(128)} %constant.418.clone.1, s32[]{:T(128)} %constant.418.clone.1) | dynamic-update-slice | bytes 524292 | tf_op jit(solution)/shard_map/dynamic_update_slice | solution.py:119
  223.9 10.3 %dynamic_update_slice.153 = bf16[8,64,2048]{2,0,1:T(8,128)(2,1)} dynamic-update-slice(bf16[8,64,2048]{2,0,1:T(8,128)(2,1)} %dynamic_update_slice.152, bf16[1,64,2048]{2,0,1:T(2,128)(2,1)} %copy.198, s32[]{:T(128)S(6)} %select_n.347, s32[]{:T(128)} %constant.418.clone.1, s32[]{:T(128)} %constant.418.clone.1) | dynamic-update-slice | bytes 524292 | tf_op jit(solution)/shard_map/dynamic_update_slice | solution.py:119
  241.7 9.3 %collective-permute-done.8 = bf16[8,64,384]{2,0,1:T(8,128)(2,1)S(1)} collective-permute-done((bf16[8,64,384]{2,0,1:T(8,128)(2,1)S(1)}, bf16[8,64,384]{2,0,1:T(8,128)(2,1)S(1)}, u32[]{:S(2)}, u32[]{:S(2)}) %collective-permute-start.8) | collective-permute-done | bytes 393248 | tf_op jit(solution)/shard_map/ppermute | solution.py:78
  273.6 9.3 %pad_maximum_fusion = bf16[2048,1280]{0,1:T(8,128)(2,1)S(1)} fusion(bf16[2048,512]{0,1:T(8,128)(2,1)S(1)} %add_convert_fusion, bf16[2048,256]{0,1:T(8,128)(2,1)S(1)} %bitcast.381, bf16[2048,256]{0,1:T(8,128)(2,1)S(1)} %bitcast.357, bf16[2048,256]{0,1:T(8,128)(2,1)S(1)} %copy-done.17), kind=kLoop, calls=%fused_computation.2 | loop fusion | flops 20971520 | bytes 10485760 | tf_op jit(solution)/shard_map/concatenate | solution.py:332
  291.4 11.3 %collective-permute-done.16 = bf16[128,2048]{1,0:T(8,128)(2,1)S(1)} collective-permute-done((bf16[128,2048]{1,0:T(8,128)(2,1)}, bf16[128,2048]{1,0:T(8,128)(2,1)S(1)}, u32[]{:S(2)}, u32[]{:S(2)}) %collective-permute-start.16) | collective-permute-done | bytes 524320 | tf_op jit(solution)/shard_map/ppermute | solution.py:74
  309.8 6.2 collective-permute-done.17
  321.5 9.9 %collective-permute-done.19 = bf16[128,2048]{1,0:T(8,128)(2,1)S(1)} collective-permute-done((bf16[128,2048]{1,0:T(8,128)(2,1)S(1)}, bf16[128,2048]{1,0:T(8,128)(2,1)S(1)}, u32[]{:S(2)}, u32[]{:S(2)}) %collective-permute-start.19) | collective-permute-done | bytes 524320 | tf_op jit(solution)/shard_map/ppermute | solution.py:74
  334.8 9.3 shard_map.247
  348.2 11.3 %collective-permute-done.26 = bf16[128,2048]{1,0:T(8,128)(2,1)S(1)} collective-permute-done((bf16[128,2048]{1,0:T(8,128)(2,1)S(1)}, bf16[128,2048]{1,0:T(8,128)(2,1)S(1)}, u32[]{:S(2)}, u32[]{:S(2)}) %collective-permute-start.26) | collective-permute-done | bytes 524320 | tf_op jit(solution)/shard_map/ppermute | solution.py:74
  363.0 7.8 collective-permute-done.25
  374.1 7.9 collective-permute-done.24
  382.0 5.3 collective-permute-done.28
  390.5 12.4 %collective-permute-done.29 = bf16[128,2048]{1,0:T(8,128)(2,1)S(1)} collective-permute-done((bf16[128,2048]{1,0:T(8,128)(2,1)S(1)}, bf16[128,2048]{1,0:T(8,128)(2,1)S(1)}, u32[]{:S(2)}, u32[]{:S(2)}) %collective-permute-start.29) | collective-permute-done | bytes 524320 | tf_op jit(solution)/shard_map/ppermute | solution.py:74
  407.9 11.2 %collective-permute-done.45 = bf16[128,2048]{1,0:T(8,128)(2,1)S(1)} collective-permute-done((bf16[128,2048]{1,0:T(8,128)(2,1)S(1)}, bf16[128,2048]{1,0:T(8,128)(2,1)S(1)}, u32[]{:S(2)}, u32[]{:S(2)}) %collective-permute-start.45) | collective-permute-done | bytes 524320 | tf_op jit(solution)/shard_map/ppermute | solution.py:74
  423.1 10.6 %collective-permute-done.46 = bf16[128,2048]{1,0:T(8,128)(2,1)S(1)} collective-permute-done((bf16[128,2048]{1,0:T(8,128)(2,1)S(1)}, bf16[128,2048]{1,0:T(8,128)(2,1)S(1)}, u32[]{:S(2)}, u32[]{:S(2)}) %collective-permute-start.46) | collective-permute-done | bytes 524320 | tf_op jit(solution)/shard_map/ppermute | solution.py:74
  442.1 6.4 collective-permute-done.50
  459.7 10.6 %collective-permute-done.48 = bf16[128,2048]{1,0:T(8,128)(2,1)S(1)} collective-permute-done((bf16[128,2048]{1,0:T(8,128)(2,1)S(1)}, bf16[128,2048]{1,0:T(8,128)(2,1)S(1)}, u32[]{:S(2)}, u32[]{:S(2)}) %collective-permute-start.48) | collective-permute-done | bytes 524320 | tf_op jit(solution)/shard_map/ppermute | solution.py:74
  477.3 4.3 collective-permute-done.51
  486.2 6.5 collective-permute-done.49
  495.6 4.7 collective-permute-done.44
  500.4 8.2 collective-permute-done.56
  514.5 5.0 collective-permute-done.57
  525.1 3.7 collective-permute-start.59
  537.3 5.0 multiply_convert_fusion.9
  542.3 3.6 fusion.86
  552.1 4.9 multiply_convert_fusion.3
  556.9 5.6 collective-permute-done.67
  573.0 4.7 collective-permute-done.71
  577.6 5.1 multiply_convert_fusion.5
  591.2 9.0 collective-permute-done.69
  600.2 4.1 multiply_convert_fusion.7
  607.6 3.7 collective-permute-done.72
  619.5 4.4 collective-permute-done.76
  624.2 6.5 fusion.23
  638.3 16.3 %fusion.1 = f32[2048,2048]{1,0:T(8,128)} fusion(bf16[1024,2048]{1,0:T(8,128)(2,1)} %copy-done.56, bf16[256,1024]{1,0:T(8,128)(2,1)} %copy-done.78, bf16[256,1024]{1,0:T(8,128)(2,1)} %copy-done.77, bf16[256,1024]{1,0:T(8,128)(2,1)} %get-tuple-element.44, bf16[256,1024]{1,0:T(8,128)(2,1)} %get-tuple-element.43, bf16[256,1024]{1,0:T(8,128)(2,1)} %get-tuple-element.42, ...), kind=kOutput, calls=%fused_computation.4 | convolution fusion | flops 8623489024 | bytes 25165824 | tf_op jit(solution)/shard_map/dot_general | solution.py:47
  654.7 6.3 fusion
  667.9 9.4 %collective-permute-done.81 = bf16[128,2048]{1,0:T(8,128)(2,1)S(1)} collective-permute-done((bf16[128,2048]{1,0:T(8,128)(2,1)S(1)}, bf16[128,2048]{1,0:T(8,128)(2,1)S(1)}, u32[]{:S(2)}, u32[]{:S(2)}) %collective-permute-start.81) | collective-permute-done | bytes 524320 | tf_op jit(solution)/shard_map/ppermute | solution.py:74
  679.2 13.6 %collective-permute-done.83 = bf16[128,2048]{1,0:T(8,128)(2,1)S(1)} collective-permute-done((bf16[128,2048]{1,0:T(8,128)(2,1)S(1)}, bf16[128,2048]{1,0:T(8,128)(2,1)S(1)}, u32[]{:S(2)}, u32[]{:S(2)}) %collective-permute-start.83) | collective-permute-done | bytes 524320 | tf_op jit(solution)/shard_map/ppermute | solution.py:74
  696.3 9.3 %collective-permute-done.84 = bf16[128,2048]{1,0:T(8,128)(2,1)S(1)} collective-permute-done((bf16[128,2048]{1,0:T(8,128)(2,1)S(1)}, bf16[128,2048]{1,0:T(8,128)(2,1)S(1)}, u32[]{:S(2)}, u32[]{:S(2)}) %collective-permute-start.84) | collective-permute-done | bytes 524320 | tf_op jit(solution)/shard_map/ppermute | solution.py:74
  709.0 17.2 %shard_map.248 = (f32[1024,256]{1,0:T(8,128)S(1)}, f32[1024,256]{1,0:T(8,128)S(1)}, f32[1024,256]{1,0:T(8,128)S(1)}) custom-call(bf16[1024,256]{1,0:T(8,128)(2,1)S(1)} %pad_maximum_fusion.7.q_ref, bf16[1024,256]{1,0:T(8,128)(2,1)S(1)} %pad_maximum_fusion.10.g_ref, bf16[1024,256]{1,0:T(8,128)(2,1)S(1)} %pad_maximum_fusion.8.k_ref, ...), custom_call_target="tpu_custom_call" | custom-call | flops 10737418240 | bytes 5242880 | tf_op jit(solution)/shard_map/pallas_call | solution.py:242
  732.4 3.8 fusion.31
  753.2 3.6 copy.207
  771.7 15.1 %collective-permute-done.88 = bf16[128,2048]{1,0:T(8,128)(2,1)S(1)} collective-permute-done((bf16[128,2048]{1,0:T(8,128)(2,1)S(1)}, bf16[128,2048]{1,0:T(8,128)(2,1)S(1)}, u32[]{:S(2)}, u32[]{:S(2)}) %collective-permute-start.88) | collective-permute-done | bytes 524320 | tf_op jit(solution)/shard_map/ppermute | solution.py:74
  789.8 6.4 collective-permute-done.102
  797.9 5.9 bitcast_add_fusion
  813.4 13.3 %collective-permute-done.95 = bf16[64,384]{1,0:T(8,128)(2,1)S(1)} collective-permute-done((bf16[64,384]{1,0:T(8,128)(2,1)S(1)}, bf16[64,384]{1,0:T(8,128)(2,1)S(1)}, u32[]{:S(2)}, u32[]{:S(2)}) %collective-permute-start.95) | collective-permute-done | bytes 49184 | tf_op jit(solution)/shard_map/ppermute | solution.py:74
  826.8 6.9 collective-permute-done.96
  833.6 5.0 collective-permute-done.97
  839.0 5.8 collective-permute-done.98
  863.5 9.6 %collective-permute-done.91 = bf16[128,2048]{1,0:T(8,128)(2,1)S(1)} collective-permute-done((bf16[128,2048]{1,0:T(8,128)(2,1)S(1)}, bf16[128,2048]{1,0:T(8,128)(2,1)S(1)}, u32[]{:S(2)}, u32[]{:S(2)}) %collective-permute-start.91) | collective-permute-done | bytes 524320 | tf_op jit(solution)/shard_map/ppermute | solution.py:74
  890.0 14.8 %collective-permute-done.106 = bf16[64,2048]{1,0:T(8,128)(2,1)S(1)} collective-permute-done((bf16[64,2048]{1,0:T(8,128)(2,1)S(1)}, bf16[64,2048]{1,0:T(8,128)(2,1)S(1)}, u32[]{:S(2)}, u32[]{:S(2)}) %collective-permute-start.106) | collective-permute-done | bytes 262176 | tf_op jit(solution)/shard_map/ppermute | solution.py:74
  904.8 10.0 %collective-permute-start.107 = (bf16[64,2048]{1,0:T(8,128)(2,1)S(1)}, bf16[64,2048]{1,0:T(8,128)(2,1)S(1)}, u32[]{:S(2)}, u32[]{:S(2)}) collective-permute-start(bf16[64,2048]{1,0:T(8,128)(2,1)S(1)} %get-tuple-element.55), channel_id=1, source_target_pairs={{0,12},{4,8},{8,20},{12,16},{16,28},{20,24},{24,4},{28,0},{1,13},{... | collective-permute-start | bytes 786440 | tf_op jit(solution)/shard_map/ppermute | solution.py:74
  914.8 4.5 collective-permute-done.107
  (656 shorter events, 398.8 us)
Async XLA Ops:
  3.6 39.3 %collective-permute-start.11 = (s32[1,9]{1,0:T(1,128)S(1)}, s32[1,9]{1,0:T(1,128)S(1)}, u32[]{:S(2)}, u32[]{:S(2)}) collective-permute-start(s32[1,9]{1,0:T(1,128)S(1)} %pad_add_fusion.2), channel_id=1, source_target_pairs={{0,4},{4,0},{8,12},{12,8},{16,20},{20,16},{24,28},{28,24},{1,5},{5... | collective-permute-start | bytes 116 | tf_op jit(solution)/shard_map/ppermute | solution.py:78
  11.1 56.2 %collective-permute-start.1 = (bf16[64,384]{1,0:T(8,128)(2,1)}, bf16[64,384]{1,0:T(8,128)(2,1)}, u32[]{:S(2)}, u32[]{:S(2)}) collective-permute-start(bf16[64,384]{1,0:T(8,128)(2,1)} %bitcast.331), channel_id=1, source_target_pairs={{0,4},{4,0},{8,12},{12,8},{16,20},{20,16},{24,28},{28,24},{1,5},{5... | collective-permute-start | bytes 147464 | tf_op jit(solution)/shard_map/ppermute | solution.py:74
  11.8 56.3 %collective-permute-start.2 = (bf16[64,384]{1,0:T(8,128)(2,1)}, bf16[64,384]{1,0:T(8,128)(2,1)}, u32[]{:S(2)}, u32[]{:S(2)}) collective-permute-start(bf16[64,384]{1,0:T(8,128)(2,1)} %bitcast.330), channel_id=1, source_target_pairs={{0,8},{4,12},{8,16},{12,20},{16,24},{20,28},{24,0},{28,4},{1,9},{5... | collective-permute-start | bytes 147464 | tf_op jit(solution)/shard_map/ppermute | solution.py:74
  14.4 57.3 %collective-permute-start.3 = (bf16[64,384]{1,0:T(8,128)(2,1)}, bf16[64,384]{1,0:T(8,128)(2,1)}, u32[]{:S(2)}, u32[]{:S(2)}) collective-permute-start(bf16[64,384]{1,0:T(8,128)(2,1)} %bitcast.329), channel_id=1, source_target_pairs={{0,12},{4,8},{8,20},{12,16},{16,28},{20,24},{24,4},{28,0},{1,13},{... | collective-permute-start | bytes 147464 | tf_op jit(solution)/shard_map/ppermute | solution.py:74
  17.6 54.6 %collective-permute-start.4 = (bf16[64,384]{1,0:T(8,128)(2,1)}, bf16[64,384]{1,0:T(8,128)(2,1)}, u32[]{:S(2)}, u32[]{:S(2)}) collective-permute-start(bf16[64,384]{1,0:T(8,128)(2,1)} %bitcast.328), channel_id=1, source_target_pairs={{0,16},{4,20},{8,24},{12,28},{16,0},{20,4},{24,8},{28,12},{1,17},{... | collective-permute-start | bytes 147464 | tf_op jit(solution)/shard_map/ppermute | solution.py:74
  64.6 33.4 %collective-permute-start.36 = (bf16[64,2048]{1,0:T(8,128)(2,1)S(1)}, bf16[64,2048]{1,0:T(8,128)(2,1)S(1)}, u32[]{:S(2)}, u32[]{:S(2)}) collective-permute-start(bf16[64,2048]{1,0:T(8,128)(2,1)S(1)} %bitcast.409), channel_id=1, source_target_pairs={{0,24},{4,28},{8,0},{12,4},{16,8},{20,12},{24,16},{28,20},{1,25},{... | collective-permute-start | bytes 786440 | tf_op jit(solution)/shard_map/ppermute | solution.py:74
  67.3 32.1 %collective-permute-start.35 = (bf16[64,2048]{1,0:T(8,128)(2,1)S(1)}, bf16[64,2048]{1,0:T(8,128)(2,1)S(1)}, u32[]{:S(2)}, u32[]{:S(2)}) collective-permute-start(bf16[64,2048]{1,0:T(8,128)(2,1)S(1)} %bitcast.410), channel_id=1, source_target_pairs={{0,20},{4,16},{8,28},{12,24},{16,4},{20,0},{24,12},{28,8},{1,21},{... | collective-permute-start | bytes 786440 | tf_op jit(solution)/shard_map/ppermute | solution.py:74
  68.1 18.9 %collective-permute-start.5 = (bf16[64,384]{1,0:T(8,128)(2,1)S(1)}, bf16[64,384]{1,0:T(8,128)(2,1)S(1)}, u32[]{:S(2)}, u32[]{:S(2)}) collective-permute-start(bf16[64,384]{1,0:T(8,128)(2,1)S(1)} %bitcast.415), channel_id=1, source_target_pairs={{0,20},{4,16},{8,28},{12,24},{16,4},{20,0},{24,12},{28,8},{1,21},{... | collective-permute-start | bytes 147464 | tf_op jit(solution)/shard_map/ppermute | solution.py:74
  72.2 25.8 %collective-permute-start.7 = (bf16[64,384]{1,0:T(8,128)(2,1)S(1)}, bf16[64,384]{1,0:T(8,128)(2,1)S(1)}, u32[]{:S(2)}, u32[]{:S(2)}) collective-permute-start(bf16[64,384]{1,0:T(8,128)(2,1)S(1)} %bitcast.413), channel_id=1, source_target_pairs={{0,28},{4,24},{8,4},{12,0},{16,12},{20,8},{24,20},{28,16},{1,29},{... | collective-permute-start | bytes 147464 | tf_op jit(solution)/shard_map/ppermute | solution.py:74
  87.1 61.6 %collective-permute-start.34 = (bf16[64,2048]{1,0:T(8,128)(2,1)}, bf16[64,2048]{1,0:T(8,128)(2,1)}, u32[]{:S(2)}, u32[]{:S(2)}) collective-permute-start(bf16[64,2048]{1,0:T(8,128)(2,1)} %bitcast.321), channel_id=1, source_target_pairs={{0,16},{4,20},{8,24},{12,28},{16,0},{20,4},{24,8},{28,12},{1,17},{... | collective-permute-start | bytes 786440 | tf_op jit(solution)/shard_map/ppermute | solution.py:74
  87.1 63.7 %collective-permute-start.33 = (bf16[64,2048]{1,0:T(8,128)(2,1)}, bf16[64,2048]{1,0:T(8,128)(2,1)}, u32[]{:S(2)}, u32[]{:S(2)}) collective-permute-start(bf16[64,2048]{1,0:T(8,128)(2,1)} %bitcast.322), channel_id=1, source_target_pairs={{0,12},{4,8},{8,20},{12,16},{16,28},{20,24},{24,4},{28,0},{1,13},{... | collective-permute-start | bytes 786440 | tf_op jit(solution)/shard_map/ppermute | solution.py:74
  98.0 56.5 %collective-permute-start.32 = (bf16[64,2048]{1,0:T(8,128)(2,1)}, bf16[64,2048]{1,0:T(8,128)(2,1)}, u32[]{:S(2)}, u32[]{:S(2)}) collective-permute-start(bf16[64,2048]{1,0:T(8,128)(2,1)} %bitcast.323), channel_id=1, source_target_pairs={{0,8},{4,12},{8,16},{12,20},{16,24},{20,28},{24,0},{28,4},{1,9},{5... | collective-permute-start | bytes 786440 | tf_op jit(solution)/shard_map/ppermute | solution.py:74
  98.0 58.6 %collective-permute-start.31 = (bf16[64,2048]{1,0:T(8,128)(2,1)}, bf16[64,2048]{1,0:T(8,128)(2,1)}, u32[]{:S(2)}, u32[]{:S(2)}) collective-permute-start(bf16[64,2048]{1,0:T(8,128)(2,1)} %bitcast.324), channel_id=1, source_target_pairs={{0,4},{4,0},{8,12},{12,8},{16,20},{20,16},{24,28},{28,24},{1,5},{5... | collective-permute-start | bytes 786440 | tf_op jit(solution)/shard_map/ppermute | solution.py:74
  99.4 60.7 %collective-permute-start.37 = (bf16[64,2048]{1,0:T(8,128)(2,1)S(1)}, bf16[64,2048]{1,0:T(8,128)(2,1)}, u32[]{:S(2)}, u32[]{:S(2)}) collective-permute-start(bf16[64,2048]{1,0:T(8,128)(2,1)S(1)} %bitcast.408), channel_id=1, source_target_pairs={{0,28},{4,24},{8,4},{12,0},{16,12},{20,8},{24,20},{28,16},{1,29},{... | collective-permute-start | bytes 786440 | tf_op jit(solution)/shard_map/ppermute | solution.py:74
  148.6 91.3 %collective-permute-start.21 = (bf16[64,2048]{1,0:T(8,128)(2,1)}, bf16[64,2048]{1,0:T(8,128)(2,1)}, u32[]{:S(2)}, u32[]{:S(2)}) collective-permute-start(bf16[64,2048]{1,0:T(8,128)(2,1)} %param.24), channel_id=1, source_target_pairs={{0,1},{1,0},{2,3},{3,2},{4,5},{5,4},{6,7},{7,6},{8,9},{9,8},{10,11... | collective-permute-start | bytes 786440 | tf_op jit(solution)/shard_map/ppermute | solution.py:78
  150.8 87.4 %collective-permute-start.20 = (bf16[64,2048]{1,0:T(8,128)(2,1)}, bf16[64,2048]{1,0:T(8,128)(2,1)}, u32[]{:S(2)}, u32[]{:S(2)}) collective-permute-start(bf16[64,2048]{1,0:T(8,128)(2,1)} %param.24), channel_id=1, source_target_pairs={{0,2},{1,3},{2,0},{3,1},{4,6},{5,7},{6,4},{7,5},{8,10},{9,11},{10,... | collective-permute-start | bytes 786440 | tf_op jit(solution)/shard_map/ppermute | solution.py:78
  154.4 101.3 %collective-permute-start.14 = (bf16[128,2048]{1,0:T(8,128)(2,1)}, bf16[128,2048]{1,0:T(8,128)(2,1)}, u32[]{:S(2)}, u32[]{:S(2)}) collective-permute-start(bf16[128,2048]{1,0:T(8,128)(2,1)} %bitcast), channel_id=1, source_target_pairs={{0,8},{4,12},{8,16},{12,20},{16,24},{20,28},{24,0},{28,4},{1,9},{5... | collective-permute-start | bytes 1572872 | tf_op jit(solution)/shard_map/ppermute | solution.py:74
  156.6 95.2 %collective-permute-start = (bf16[128,2048]{1,0:T(8,128)(2,1)}, bf16[128,2048]{1,0:T(8,128)(2,1)}, u32[]{:S(2)}, u32[]{:S(2)}) collective-permute-start(bf16[128,2048]{1,0:T(8,128)(2,1)} %bitcast), channel_id=1, source_target_pairs={{0,4},{4,0},{8,12},{12,8},{16,20},{20,16},{24,28},{28,24},{1,5},{5... | collective-permute-start | bytes 1572872 | tf_op jit(solution)/shard_map/ppermute | solution.py:74
  160.0 147.4 %collective-permute-start.42 = (bf16[256,2048]{1,0:T(8,128)(2,1)}, bf16[256,2048]{1,0:T(8,128)(2,1)}, u32[]{:S(2)}, u32[]{:S(2)}) collective-permute-start(bf16[256,2048]{1,0:T(8,128)(2,1)} %param.27), channel_id=1, source_target_pairs={{0,1},{1,0},{2,3},{3,2},{4,5},{5,4},{6,7},{7,6},{8,9},{9,8},{10,11... | collective-permute-start | bytes 3145736 | tf_op jit(solution)/shard_map/ppermute | solution.py:78
  251.0 51.8 %collective-permute-start.41 = (bf16[256,2048]{1,0:T(8,128)(2,1)}, bf16[256,2048]{1,0:T(8,128)(2,1)}, u32[]{:S(2)}, u32[]{:S(2)}) collective-permute-start(bf16[256,2048]{1,0:T(8,128)(2,1)} %param.27), channel_id=1, source_target_pairs={{0,2},{1,3},{2,0},{3,1},{4,6},{5,7},{6,4},{7,5},{8,10},{9,11},{10,... | collective-permute-start | bytes 3145736 | tf_op jit(solution)/shard_map/ppermute | solution.py:78
  251.7 135.9 %collective-permute-start.39 = (bf16[8,64,2048]{2,0,1:T(8,128)(2,1)}, bf16[8,64,2048]{2,0,1:T(8,128)(2,1)}, u32[]{:S(2)}, u32[]{:S(2)}) collective-permute-start(bf16[8,64,2048]{2,0,1:T(8,128)(2,1)} %dynamic_update_slice.153), channel_id=1, source_target_pairs={{0,1},{1,0},{2,3},{3,2},{4,5},{5,4},{6,7},{7,6},{8,9},{9,8},{10,11... | collective-permute-start | bytes 6291464 | tf_op jit(solution)/shard_map/ppermute | solution.py:78
  255.8 106.5 %collective-permute-start.38 = (bf16[8,64,2048]{2,0,1:T(8,128)(2,1)}, bf16[8,64,2048]{2,0,1:T(8,128)(2,1)}, u32[]{:S(2)}, u32[]{:S(2)}) collective-permute-start(bf16[8,64,2048]{2,0,1:T(8,128)(2,1)} %dynamic_update_slice.153), channel_id=1, source_target_pairs={{0,2},{1,3},{2,0},{3,1},{4,6},{5,7},{6,4},{7,5},{8,10},{9,11},{10,... | collective-permute-start | bytes 6291464 | tf_op jit(solution)/shard_map/ppermute | solution.py:78
  261.2 25.0 %collective-permute-start.15 = (bf16[128,2048]{1,0:T(8,128)(2,1)}, bf16[128,2048]{1,0:T(8,128)(2,1)}, u32[]{:S(2)}, u32[]{:S(2)}) collective-permute-start(bf16[128,2048]{1,0:T(8,128)(2,1)} %collective-permute-done.14), channel_id=1, source_target_pairs={{0,4},{4,0},{8,12},{12,8},{16,20},{20,16},{24,28},{28,24},{1,5},{5... | collective-permute-start | bytes 1572872 | tf_op jit(solution)/shard_map/ppermute | solution.py:74
  286.2 16.4 %collective-permute-start.16 = (bf16[128,2048]{1,0:T(8,128)(2,1)}, bf16[128,2048]{1,0:T(8,128)(2,1)S(1)}, u32[]{:S(2)}, u32[]{:S(2)}) collective-permute-start(bf16[128,2048]{1,0:T(8,128)(2,1)} %collective-permute-done.14), channel_id=1, source_target_pairs={{0,8},{4,12},{8,16},{12,20},{16,24},{20,28},{24,0},{28,4},{1,9},{5... | collective-permute-start | bytes 1572872 | tf_op jit(solution)/shard_map/ppermute | solution.py:74
  302.7 16.3 %collective-permute-start.18 = (bf16[128,2048]{1,0:T(8,128)(2,1)S(1)}, bf16[128,2048]{1,0:T(8,128)(2,1)S(1)}, u32[]{:S(2)}, u32[]{:S(2)}) collective-permute-start(bf16[128,2048]{1,0:T(8,128)(2,1)S(1)} %collective-permute-done.16), channel_id=1, source_target_pairs={{0,8},{4,12},{8,16},{12,20},{16,24},{20,28},{24,0},{28,4},{1,9},{5... | collective-permute-start | bytes 1572872 | tf_op jit(solution)/shard_map/ppermute | solution.py:74
  307.4 52.5 %collective-permute-start.43 = (bf16[256,2048]{1,0:T(8,128)(2,1)}, bf16[256,2048]{1,0:T(8,128)(2,1)S(1)}, u32[]{:S(2)}, u32[]{:S(2)}) collective-permute-start(bf16[256,2048]{1,0:T(8,128)(2,1)} %collective-permute-done.41), channel_id=1, source_target_pairs={{0,1},{1,0},{2,3},{3,2},{4,5},{5,4},{6,7},{7,6},{8,9},{9,8},{10,11... | collective-permute-start | bytes 3145736 | tf_op jit(solution)/shard_map/ppermute | solution.py:78
  346.9 23.8 %collective-permute-start.25 = (bf16[128,2048]{1,0:T(8,128)(2,1)S(1)}, bf16[128,2048]{1,0:T(8,128)(2,1)S(1)}, u32[]{:S(2)}, u32[]{:S(2)}) collective-permute-start(bf16[128,2048]{1,0:T(8,128)(2,1)S(1)} %slice.739), channel_id=1, source_target_pairs={{0,4},{4,0},{8,12},{12,8},{16,20},{20,16},{24,28},{28,24},{1,5},{5... | collective-permute-start | bytes 1572872 | tf_op jit(solution)/shard_map/ppermute | solution.py:74
  359.9 22.1 %collective-permute-start.24 = (bf16[128,2048]{1,0:T(8,128)(2,1)S(1)}, bf16[128,2048]{1,0:T(8,128)(2,1)S(1)}, u32[]{:S(2)}, u32[]{:S(2)}) collective-permute-start(bf16[128,2048]{1,0:T(8,128)(2,1)S(1)} %slice.740), channel_id=1, source_target_pairs={{0,4},{4,0},{8,12},{12,8},{16,20},{20,16},{24,28},{28,24},{1,5},{5... | collective-permute-start | bytes 1572872 | tf_op jit(solution)/shard_map/ppermute | solution.py:74
  362.3 28.2 %collective-permute-start.23 = (bf16[128,2048]{1,0:T(8,128)(2,1)S(1)}, bf16[128,2048]{1,0:T(8,128)(2,1)S(1)}, u32[]{:S(2)}, u32[]{:S(2)}) collective-permute-start(bf16[128,2048]{1,0:T(8,128)(2,1)S(1)} %slice.741), channel_id=1, source_target_pairs={{0,4},{4,0},{8,12},{12,8},{16,20},{20,16},{24,28},{28,24},{1,5},{5... | collective-permute-start | bytes 1572872 | tf_op jit(solution)/shard_map/ppermute | solution.py:74
  370.7 35.8 %collective-permute-start.40 = (bf16[8,64,2048]{2,0,1:T(8,128)(2,1)}, bf16[8,64,2048]{2,0,1:T(8,128)(2,1)S(1)}, u32[]{:S(2)}, u32[]{:S(2)}) collective-permute-start(bf16[8,64,2048]{2,0,1:T(8,128)(2,1)} %collective-permute-done.38), channel_id=1, source_target_pairs={{0,1},{1,0},{2,3},{3,2},{4,5},{5,4},{6,7},{7,6},{8,9},{9,8},{10,11... | collective-permute-start | bytes 6291464 | tf_op jit(solution)/shard_map/ppermute | solution.py:78
  370.9 16.4 %collective-permute-start.28 = (bf16[128,2048]{1,0:T(8,128)(2,1)S(1)}, bf16[128,2048]{1,0:T(8,128)(2,1)S(1)}, u32[]{:S(2)}, u32[]{:S(2)}) collective-permute-start(bf16[128,2048]{1,0:T(8,128)(2,1)S(1)} %fusion.62), channel_id=1, source_target_pairs={{0,8},{4,12},{8,16},{12,20},{16,24},{20,28},{24,0},{28,4},{1,9},{5... | collective-permute-start | bytes 1572872 | tf_op jit(solution)/shard_map/ppermute | solution.py:74
  440.5 18.9 %collective-permute-start.53 = (bf16[128,2048]{1,0:T(8,128)(2,1)S(1)}, bf16[128,2048]{1,0:T(8,128)(2,1)S(1)}, u32[]{:S(2)}, u32[]{:S(2)}) collective-permute-start(bf16[128,2048]{1,0:T(8,128)(2,1)S(1)} %slice.734), channel_id=1, source_target_pairs={{0,4},{4,0},{8,12},{12,8},{16,20},{20,16},{24,28},{28,24},{1,5},{5... | collective-permute-start | bytes 1572872 | tf_op jit(solution)/shard_map/ppermute | solution.py:74
  453.9 16.4 %collective-permute-start.48 = (bf16[128,2048]{1,0:T(8,128)(2,1)S(1)}, bf16[128,2048]{1,0:T(8,128)(2,1)S(1)}, u32[]{:S(2)}, u32[]{:S(2)}) collective-permute-start(bf16[128,2048]{1,0:T(8,128)(2,1)S(1)} %collective-permute-done.47), channel_id=1, source_target_pairs={{0,4},{4,0},{8,12},{12,8},{16,20},{20,16},{24,28},{28,24},{1,5},{5... | collective-permute-start | bytes 1572872 | tf_op jit(solution)/shard_map/ppermute | solution.py:74
  458.1 23.4 %collective-permute-start.51 = (bf16[128,2048]{1,0:T(8,128)(2,1)S(1)}, bf16[128,2048]{1,0:T(8,128)(2,1)S(1)}, u32[]{:S(2)}, u32[]{:S(2)}) collective-permute-start(bf16[128,2048]{1,0:T(8,128)(2,1)S(1)} %slice.735), channel_id=1, source_target_pairs={{0,4},{4,0},{8,12},{12,8},{16,20},{20,16},{24,28},{28,24},{1,5},{5... | collective-permute-start | bytes 1572872 | tf_op jit(solution)/shard_map/ppermute | solution.py:74
  459.6 21.9 %collective-permute-start.54 = (bf16[128,2048]{1,0:T(8,128)(2,1)S(1)}, bf16[128,2048]{1,0:T(8,128)(2,1)S(1)}, u32[]{:S(2)}, u32[]{:S(2)}) collective-permute-start(bf16[128,2048]{1,0:T(8,128)(2,1)S(1)} %fusion.53), channel_id=1, source_target_pairs={{0,8},{4,12},{8,16},{12,20},{16,24},{20,28},{24,0},{28,4},{1,9},{5... | collective-permute-start | bytes 1572872 | tf_op jit(solution)/shard_map/ppermute | solution.py:74
  476.5 16.3 %collective-permute-start.49 = (bf16[128,2048]{1,0:T(8,128)(2,1)S(1)}, bf16[128,2048]{1,0:T(8,128)(2,1)S(1)}, u32[]{:S(2)}, u32[]{:S(2)}) collective-permute-start(bf16[128,2048]{1,0:T(8,128)(2,1)S(1)} %slice.736), channel_id=1, source_target_pairs={{0,4},{4,0},{8,12},{12,8},{16,20},{20,16},{24,28},{28,24},{1,5},{5... | collective-permute-start | bytes 1572872 | tf_op jit(solution)/shard_map/ppermute | solution.py:74
  509.9 26.6 %collective-permute-start.66 = (bf16[128,2048]{1,0:T(8,128)(2,1)S(1)}, bf16[128,2048]{1,0:T(8,128)(2,1)S(1)}, u32[]{:S(2)}, u32[]{:S(2)}) collective-permute-start(bf16[128,2048]{1,0:T(8,128)(2,1)S(1)} %get-tuple-element.25), channel_id=1, source_target_pairs={{0,8},{4,12},{8,16},{12,20},{16,24},{20,28},{24,0},{28,4},{1,9},{5... | collective-permute-start | bytes 1572872 | tf_op jit(solution)/shard_map/ppermute | solution.py:74
  510.3 27.0 %collective-permute-start.64 = (bf16[128,2048]{1,0:T(8,128)(2,1)S(1)}, bf16[128,2048]{1,0:T(8,128)(2,1)S(1)}, u32[]{:S(2)}, u32[]{:S(2)}) collective-permute-start(bf16[128,2048]{1,0:T(8,128)(2,1)S(1)} %get-tuple-element.25), channel_id=1, source_target_pairs={{0,4},{4,0},{8,12},{12,8},{16,20},{20,16},{24,28},{28,24},{1,5},{5... | collective-permute-start | bytes 1572872 | tf_op jit(solution)/shard_map/ppermute | solution.py:74
  546.7 85.8 %collective-permute-start.65 = (bf16[128,2048]{1,0:T(8,128)(2,1)}, bf16[128,2048]{1,0:T(8,128)(2,1)S(1)}, u32[]{:S(2)}, u32[]{:S(2)}) collective-permute-start(bf16[128,2048]{1,0:T(8,128)(2,1)} %slice.733), channel_id=1, source_target_pairs={{0,4},{4,0},{8,12},{12,8},{16,20},{20,16},{24,28},{28,24},{1,5},{5... | collective-permute-start | bytes 1572872 | tf_op jit(solution)/shard_map/ppermute | solution.py:74
  567.7 21.5 %collective-permute-start.74 = (bf16[128,2048]{1,0:T(8,128)(2,1)}, bf16[128,2048]{1,0:T(8,128)(2,1)}, u32[]{:S(2)}, u32[]{:S(2)}) collective-permute-start(bf16[128,2048]{1,0:T(8,128)(2,1)} %slice.730), channel_id=1, source_target_pairs={{0,4},{4,0},{8,12},{12,8},{16,20},{20,16},{24,28},{28,24},{1,5},{5... | collective-permute-start | bytes 1572872 | tf_op jit(solution)/shard_map/ppermute | solution.py:74
  582.7 17.5 %collective-permute-start.69 = (bf16[128,2048]{1,0:T(8,128)(2,1)}, bf16[128,2048]{1,0:T(8,128)(2,1)}, u32[]{:S(2)}, u32[]{:S(2)}) collective-permute-start(bf16[128,2048]{1,0:T(8,128)(2,1)} %collective-permute-done.68), channel_id=1, source_target_pairs={{0,4},{4,0},{8,12},{12,8},{16,20},{20,16},{24,28},{28,24},{1,5},{5... | collective-permute-start | bytes 1572872 | tf_op jit(solution)/shard_map/ppermute | solution.py:74
  588.0 23.4 %collective-permute-start.72 = (bf16[128,2048]{1,0:T(8,128)(2,1)}, bf16[128,2048]{1,0:T(8,128)(2,1)S(1)}, u32[]{:S(2)}, u32[]{:S(2)}) collective-permute-start(bf16[128,2048]{1,0:T(8,128)(2,1)} %slice.731), channel_id=1, source_target_pairs={{0,4},{4,0},{8,12},{12,8},{16,20},{20,16},{24,28},{28,24},{1,5},{5... | collective-permute-start | bytes 1572872 | tf_op jit(solution)/shard_map/ppermute | solution.py:74
  591.2 20.2 %collective-permute-start.75 = (bf16[128,2048]{1,0:T(8,128)(2,1)}, bf16[128,2048]{1,0:T(8,128)(2,1)S(1)}, u32[]{:S(2)}, u32[]{:S(2)}) collective-permute-start(bf16[128,2048]{1,0:T(8,128)(2,1)} %fusion.47), channel_id=1, source_target_pairs={{0,8},{4,12},{8,16},{12,20},{16,24},{20,28},{24,0},{28,4},{1,9},{5... | collective-permute-start | bytes 1572872 | tf_op jit(solution)/shard_map/ppermute | solution.py:74
  632.5 32.0 %collective-permute-start.112 = (bf16[2,256,2048]{2,1,0:T(8,128)(2,1)}, bf16[2,256,2048]{2,1,0:T(8,128)(2,1)}, u32[]{:S(2)}, u32[]{:S(2)}) collective-permute-start(bf16[2,256,2048]{2,1,0:T(8,128)(2,1)} %fusion.22), channel_id=1, source_target_pairs={{0,1},{1,0},{2,3},{3,2},{4,5},{5,4},{6,7},{7,6},{8,9},{9,8},{10,11... | collective-permute-start | bytes 6291464 | tf_op jit(solution)/shard_map/ppermute | solution.py:78
  637.1 23.8 %collective-permute-start.79 = (bf16[128,2048]{1,0:T(8,128)(2,1)S(1)}, bf16[128,2048]{1,0:T(8,128)(2,1)S(1)}, u32[]{:S(2)}, u32[]{:S(2)}) collective-permute-start(bf16[128,2048]{1,0:T(8,128)(2,1)S(1)} %get-tuple-element.30), channel_id=1, source_target_pairs={{0,8},{4,12},{8,16},{12,20},{16,24},{20,28},{24,0},{28,4},{1,9},{5... | collective-permute-start | bytes 1572872 | tf_op jit(solution)/shard_map/ppermute | solution.py:74
  637.5 24.8 %collective-permute-start.78 = (bf16[128,2048]{1,0:T(8,128)(2,1)S(1)}, bf16[128,2048]{1,0:T(8,128)(2,1)S(1)}, u32[]{:S(2)}, u32[]{:S(2)}) collective-permute-start(bf16[128,2048]{1,0:T(8,128)(2,1)S(1)} %get-tuple-element.30), channel_id=1, source_target_pairs={{0,4},{4,0},{8,12},{12,8},{16,20},{20,16},{24,28},{28,24},{1,5},{5... | collective-permute-start | bytes 1572872 | tf_op jit(solution)/shard_map/ppermute | solution.py:74
  661.0 136.4 %collective-permute-start.103 = (bf16[8,2,64,2048]{3,2,1,0:T(8,128)(2,1)}, bf16[8,2,64,2048]{3,2,1,0:T(8,128)(2,1)}, u32[]{:S(2)}, u32[]{:S(2)}) collective-permute-start(bf16[8,2,64,2048]{3,2,1,0:T(8,128)(2,1)} %fusion), channel_id=1, source_target_pairs={{0,1},{1,0},{2,3},{3,2},{4,5},{5,4},{6,7},{7,6},{8,9},{9,8},{10,11... | collective-permute-start | bytes 12582920 | tf_op jit(solution)/shard_map/ppermute | solution.py:78
  661.0 16.3 %collective-permute-start.81 = (bf16[128,2048]{1,0:T(8,128)(2,1)S(1)}, bf16[128,2048]{1,0:T(8,128)(2,1)S(1)}, u32[]{:S(2)}, u32[]{:S(2)}) collective-permute-start(bf16[128,2048]{1,0:T(8,128)(2,1)S(1)} %collective-permute-done.79), channel_id=1, source_target_pairs={{0,8},{4,12},{8,16},{12,20},{16,24},{20,28},{24,0},{28,4},{1,9},{5... | collective-permute-start | bytes 1572872 | tf_op jit(solution)/shard_map/ppermute | solution.py:74
  661.0 17.6 %collective-permute-start.80 = (bf16[128,2048]{1,0:T(8,128)(2,1)S(1)}, bf16[128,2048]{1,0:T(8,128)(2,1)S(1)}, u32[]{:S(2)}, u32[]{:S(2)}) collective-permute-start(bf16[128,2048]{1,0:T(8,128)(2,1)S(1)} %collective-permute-done.79), channel_id=1, source_target_pairs={{0,4},{4,0},{8,12},{12,8},{16,20},{20,16},{24,28},{28,24},{1,5},{5... | collective-permute-start | bytes 1572872 | tf_op jit(solution)/shard_map/ppermute | solution.py:74
  667.4 27.3 %collective-permute-start.113 = (bf16[1,256,2048]{2,1,0:T(8,128)(2,1)S(1)}, bf16[1,256,2048]{2,1,0:T(8,128)(2,1)S(1)}, u32[]{:S(2)}, u32[]{:S(2)}) collective-permute-start(bf16[1,256,2048]{2,1,0:T(8,128)(2,1)S(1)} %dynamic-slice_convert_fusion.2), channel_id=1, source_target_pairs={{0,2},{1,3},{2,0},{3,1},{4,6},{5,7},{6,4},{7,5},{8,10},{9,11},{10,... | collective-permute-start | bytes 3145736 | tf_op jit(solution)/shard_map/ppermute | solution.py:78
  677.3 16.8 %collective-permute-start.82 = (bf16[128,2048]{1,0:T(8,128)(2,1)S(1)}, bf16[128,2048]{1,0:T(8,128)(2,1)S(1)}, u32[]{:S(2)}, u32[]{:S(2)}) collective-permute-start(bf16[128,2048]{1,0:T(8,128)(2,1)S(1)} %collective-permute-done.81), channel_id=1, source_target_pairs={{0,4},{4,0},{8,12},{12,8},{16,20},{20,16},{24,28},{28,24},{1,5},{5... | collective-permute-start | bytes 1572872 | tf_op jit(solution)/shard_map/ppermute | solution.py:74
  707.9 61.2 %collective-permute-start.101 = (bf16[2,64,2048]{2,1,0:T(8,128)(2,1)}, bf16[2,64,2048]{2,1,0:T(8,128)(2,1)}, u32[]{:S(2)}, u32[]{:S(2)}) collective-permute-start(bf16[2,64,2048]{2,1,0:T(8,128)(2,1)} %fusion.137), channel_id=1, source_target_pairs={{0,1},{1,0},{2,3},{3,2},{4,5},{5,4},{6,7},{7,6},{8,9},{9,8},{10,11... | collective-permute-start | bytes 1572872 | tf_op jit(solution)/shard_map/ppermute | solution.py:78
  758.4 30.6 %collective-permute-start.92 = (bf16[8,2,64,384]{3,2,1,0:T(8,128)(2,1)S(1)}, bf16[8,2,64,384]{3,2,1,0:T(8,128)(2,1)S(1)}, u32[]{:S(2)}, u32[]{:S(2)}) collective-permute-start(bf16[8,2,64,384]{3,2,1,0:T(8,128)(2,1)S(1)} %fusion.133), channel_id=1, source_target_pairs={{0,1},{1,0},{2,3},{3,2},{4,5},{5,4},{6,7},{7,6},{8,9},{9,8},{10,11... | collective-permute-start | bytes 2359304 | tf_op jit(solution)/shard_map/ppermute | solution.py:78
  760.6 102.9 %collective-permute-start.85 = (bf16[128,2048]{1,0:T(8,128)(2,1)}, bf16[128,2048]{1,0:T(8,128)(2,1)}, u32[]{:S(2)}, u32[]{:S(2)}) collective-permute-start(bf16[128,2048]{1,0:T(8,128)(2,1)} %slice.729), channel_id=1, source_target_pairs={{0,4},{4,0},{8,12},{12,8},{16,20},{20,16},{24,28},{28,24},{1,5},{5... | collective-permute-start | bytes 1572872 | tf_op jit(solution)/shard_map/ppermute | solution.py:74
  763.2 23.6 %collective-permute-start.88 = (bf16[128,2048]{1,0:T(8,128)(2,1)S(1)}, bf16[128,2048]{1,0:T(8,128)(2,1)S(1)}, u32[]{:S(2)}, u32[]{:S(2)}) collective-permute-start(bf16[128,2048]{1,0:T(8,128)(2,1)S(1)} %slice.726), channel_id=1, source_target_pairs={{0,4},{4,0},{8,12},{12,8},{16,20},{20,16},{24,28},{28,24},{1,5},{5... | collective-permute-start | bytes 1572872 | tf_op jit(solution)/shard_map/ppermute | solution.py:74
  769.1 40.1 %collective-permute-start.87 = (bf16[128,2048]{1,0:T(8,128)(2,1)}, bf16[128,2048]{1,0:T(8,128)(2,1)}, u32[]{:S(2)}, u32[]{:S(2)}) collective-permute-start(bf16[128,2048]{1,0:T(8,128)(2,1)} %slice.727), channel_id=1, source_target_pairs={{0,4},{4,0},{8,12},{12,8},{16,20},{20,16},{24,28},{28,24},{1,5},{5... | collective-permute-start | bytes 1572872 | tf_op jit(solution)/shard_map/ppermute | solution.py:74
  786.8 72.4 %collective-permute-start.86 = (bf16[128,2048]{1,0:T(8,128)(2,1)}, bf16[128,2048]{1,0:T(8,128)(2,1)}, u32[]{:S(2)}, u32[]{:S(2)}) collective-permute-start(bf16[128,2048]{1,0:T(8,128)(2,1)} %slice.728), channel_id=1, source_target_pairs={{0,4},{4,0},{8,12},{12,8},{16,20},{20,16},{24,28},{28,24},{1,5},{5... | collective-permute-start | bytes 1572872 | tf_op jit(solution)/shard_map/ppermute | solution.py:74
  807.5 67.2 %collective-permute-start.104 = (bf16[8,1,64,2048]{3,2,1,0:T(8,128)(2,1)S(1)}, bf16[8,1,64,2048]{3,2,1,0:T(8,128)(2,1)}, u32[]{:S(2)}, u32[]{:S(2)}) collective-permute-start(bf16[8,1,64,2048]{3,2,1,0:T(8,128)(2,1)S(1)} %dynamic-slice_convert_fusion.1), channel_id=1, source_target_pairs={{0,2},{1,3},{2,0},{3,1},{4,6},{5,7},{6,4},{7,5},{8,10},{9,11},{10,... | collective-permute-start | bytes 6291464 | tf_op jit(solution)/shard_map/ppermute | solution.py:78
  812.5 46.6 %collective-permute-start.90 = (bf16[128,2048]{1,0:T(8,128)(2,1)}, bf16[128,2048]{1,0:T(8,128)(2,1)}, u32[]{:S(2)}, u32[]{:S(2)}) collective-permute-start(bf16[128,2048]{1,0:T(8,128)(2,1)} %fusion.43), channel_id=1, source_target_pairs={{0,8},{4,12},{8,16},{12,20},{16,24},{20,28},{24,0},{28,4},{1,9},{5... | collective-permute-start | bytes 1572872 | tf_op jit(solution)/shard_map/ppermute | solution.py:74
  882.1 37.4 %collective-permute-start.111 = (bf16[64,2048]{1,0:T(8,128)(2,1)S(1)}, bf16[64,2048]{1,0:T(8,128)(2,1)S(1)}, u32[]{:S(2)}, u32[]{:S(2)}) collective-permute-start(bf16[64,2048]{1,0:T(8,128)(2,1)S(1)} %get-tuple-element.51), channel_id=1, source_target_pairs={{0,28},{4,24},{8,4},{12,0},{16,12},{20,8},{24,20},{28,16},{1,29},{... | collective-permute-start | bytes 786440 | tf_op jit(solution)/shard_map/ppermute | solution.py:74
  884.6 34.8 %collective-permute-start.110 = (bf16[64,2048]{1,0:T(8,128)(2,1)S(1)}, bf16[64,2048]{1,0:T(8,128)(2,1)S(1)}, u32[]{:S(2)}, u32[]{:S(2)}) collective-permute-start(bf16[64,2048]{1,0:T(8,128)(2,1)S(1)} %get-tuple-element.52), channel_id=1, source_target_pairs={{0,24},{4,28},{8,0},{12,4},{16,8},{20,12},{24,16},{28,20},{1,25},{... | collective-permute-start | bytes 786440 | tf_op jit(solution)/shard_map/ppermute | solution.py:74
  884.6 34.8 %collective-permute-start.109 = (bf16[64,2048]{1,0:T(8,128)(2,1)S(1)}, bf16[64,2048]{1,0:T(8,128)(2,1)S(1)}, u32[]{:S(2)}, u32[]{:S(2)}) collective-permute-start(bf16[64,2048]{1,0:T(8,128)(2,1)S(1)} %get-tuple-element.53), channel_id=1, source_target_pairs={{0,20},{4,16},{8,28},{12,24},{16,4},{20,0},{24,12},{28,8},{1,21},{... | collective-permute-start | bytes 786440 | tf_op jit(solution)/shard_map/ppermute | solution.py:74
  886.5 32.9 %collective-permute-start.108 = (bf16[64,2048]{1,0:T(8,128)(2,1)S(1)}, bf16[64,2048]{1,0:T(8,128)(2,1)S(1)}, u32[]{:S(2)}, u32[]{:S(2)}) collective-permute-start(bf16[64,2048]{1,0:T(8,128)(2,1)S(1)} %get-tuple-element.54), channel_id=1, source_target_pairs={{0,16},{4,20},{8,24},{12,28},{16,0},{20,4},{24,8},{28,12},{1,17},{... | collective-permute-start | bytes 786440 | tf_op jit(solution)/shard_map/ppermute | solution.py:74
  887.9 16.9 %collective-permute-start.106 = (bf16[64,2048]{1,0:T(8,128)(2,1)S(1)}, bf16[64,2048]{1,0:T(8,128)(2,1)S(1)}, u32[]{:S(2)}, u32[]{:S(2)}) collective-permute-start(bf16[64,2048]{1,0:T(8,128)(2,1)S(1)} %get-tuple-element.56), channel_id=1, source_target_pairs={{0,8},{4,12},{8,16},{12,20},{16,24},{20,28},{24,0},{28,4},{1,9},{5... | collective-permute-start | bytes 786440 | tf_op jit(solution)/shard_map/ppermute | solution.py:74
  (131 other events, 1238.9 us)

commit v2 on v1

v2 whole, which is shorter than its diff:
```python
import functools
import math

import jax
import jax.numpy as jnp
import numpy as np
from jax import lax
from jax.experimental import pallas as pl
from jax.experimental.pallas import tpu as pltpu
from jax.sharding import PartitionSpec as P

HEADS = 32
KV_HEADS = 8
HEAD_DIM = 64
SPAN = 128
EPSILON = 1e-05
HIDE = -1e30
TWICE = ("bf", "bo")
BF = jnp.bfloat16
F32 = jnp.float32


def rope_rates(head_width):
    frequency = 1.0 / 500000.0 ** (np.arange(0, head_width, 2) / head_width)
    wavelength = 2.0 * np.pi / frequency
    blend_share = (8192.0 / wavelength - 1.0) / 3.0
    blended = (1.0 - blend_share) * frequency / 32.0 + blend_share * frequency
    frequency = np.where(
        wavelength < 2048.0, frequency, np.where(wavelength > 8192.0, frequency / 32.0, blended)
    )
    return np.concatenate([frequency, frequency]).astype(np.float32)


def mm(left, right):
    return jnp.dot(left, right, preferred_element_type=F32)


def mm_t(left, right):
    return lax.dot_general(left, right, (((0,), (0,)), ((), ())), preferred_element_type=F32)


def against(left, right):
    return lax.dot_general(left, right, (((1,), (1,)), ((), ())), preferred_element_type=F32)


def pick(array, index, axis=0):
    return lax.dynamic_index_in_dim(array, index, axis, keepdims=False)


def paired(blocks):
    rows = [jnp.concatenate(pieces, axis=1) if len(pieces) > 1 else pieces[0] for pieces in blocks]
    return jnp.concatenate(rows, axis=0)


def tie(value, *others):
    return lax.optimization_barrier((value, *others))[0]


class Links:
    def __init__(self):
        self.n = lax.axis_size("ctx")
        self.m = lax.axis_size("fsdp")
        self.ring = self.n // 2
        self.c = lax.axis_index("ctx")
        self.f = lax.axis_index("fsdp")
        self.a = self.c // 2
        self.b = self.c % 2
        self.box, self.jobs = {}, {}

    def shift(self, x, da, dq):
        perm = [
            (a * 2 + b, ((a + da) % self.ring) * 2 + (b ^ dq))
            for a in range(self.ring)
            for b in range(2)
        ]
        return lax.ppermute(x, "ctx", perm)

    def flip(self, x, axis, bit):
        size = self.n if axis == "ctx" else self.m
        return lax.ppermute(x, axis, [(i, i ^ bit) for i in range(size)])

    def slot(self, name, begun, mains):
        made = {key: job(begun) for key, job in self.jobs.pop(name, {}).items()}
        mains, made = lax.optimization_barrier((mains, made))
        self.box.update(made)
        return mains

    def cut(self, x, name):
        count = 2 if name in TWICE else 1
        step = x.shape[1] // count
        return [x[:, i * step : (i + 1) * step] for i in range(count)]

    def gather_ctx(self, x, name):
        out = []
        held = self.cut(x, name)
        for r in range(self.ring):
            pairs, moved = [], []
            for i, piece in enumerate(held):
                mains = [self.shift(piece, 0, 1)]
                if r < self.ring - 1:
                    mains.append(self.shift(piece, 1, 0))
                last = i == len(held) - 1
                mains = self.slot(f"{name}{r}" if last else "", piece, mains)
                pairs.append(mains[0])
                moved.append(mains[-1])
            out.append((held, pairs))
            held = moved
        return out

    def scatter_order(self):
        return list(range(1, self.ring)) + [0]

    def scatter_ctx(self, part, name):
        count = len(self.cut(jnp.zeros((1, 2)), name))
        held, got = [None] * count, [None] * count
        for i, r in enumerate(self.scatter_order()):
            mine, other = part(r)
            pieces = zip(self.cut(mine, name), self.cut(other.astype(BF), name))
            for k, (own, away) in enumerate(pieces):
                if i:
                    away = tie(away, got[k])
                mains = [self.shift(away, 0, 1)]
                if i:
                    mains.append(self.shift(held[k].astype(BF), 1, 0))
                mains = self.slot(f"{name}{i}" if k == count - 1 else "", away, mains)
                got[k] = mains[0]
                held[k] = own + sum(block.astype(F32) for block in mains)
        return held[0] if count == 1 else jnp.concatenate(held, axis=1)

    def direct(self):
        near = sorted(range(1, self.ring), key=lambda da: (min(da, self.ring - da), da))
        return [(0, 0)] + [(da, 0) for da in near] + [(0, 1)] + [(da, 1) for da in near]

    def dests(self, moves):
        spots = [((self.a + da) % self.ring) * 2 + (self.b ^ dq) for da, dq in moves]
        return jnp.stack(spots).astype(jnp.int32)

    def sources(self, moves):
        return self.dests([((self.ring - da) % self.ring, dq) for da, dq in moves])

    def routes(self):
        c = jnp.arange(self.n, dtype=jnp.int32)
        return ((c // 2 + self.ring - self.a) % self.ring) * 2 + (self.b ^ (c % 2))

    def origins(self):
        c = jnp.arange(self.n, dtype=jnp.int32)
        return ((self.a + self.ring - c // 2) % self.ring) * 2 + (self.b ^ (c % 2))

    def assemble(self, groups, spots, rows):
        sizes = [group[0].shape[0] for group in groups]
        count = sum(sizes)
        held_rows, width = groups[0][0].shape[1:]
        parts = max(1, min(width // 256, 8 // count))
        part = width // parts
        marks = self.f ^ jnp.arange(self.m, dtype=jnp.int32)
        specs, base = [], 0
        for size in sizes:

            def at(i, j, spots, base=base, size=size):
                return jnp.clip(i - base, 0, size - 1), 0, j

            specs += [pl.BlockSpec((1, held_rows, part), at)] * self.m
            base += size
        out = pl.pallas_call(
            functools.partial(place_kernel, sizes, self.m),
            grid_spec=pltpu.PrefetchScalarGridSpec(
                num_scalar_prefetch=1,
                grid=(count, parts),
                in_specs=specs,
                out_specs=pl.BlockSpec(
                    (1, self.m, rows, part), lambda i, j, spots: (spots[i], 0, 0, j)
                ),
            ),
            out_shape=jax.ShapeDtypeStruct((count, self.m, rows, width), BF),
            compiler_params=pltpu.CompilerParams(vmem_limit_bytes=24 << 20),
            cost_estimate=pl.CostEstimate(
                flops=0, bytes_accessed=4 * count * self.m * rows * width, transcendentals=0
            ),
        )(jnp.concatenate([spots, marks]), *[block for group in groups for block in group])
        return out.reshape(count * self.m * rows, width)


def place_kernel(sizes, m, spots, *refs):
    count = sum(sizes)
    out = refs[-1]
    base = 0
    for g, size in enumerate(sizes):

        @pl.when((pl.program_id(0) >= base) & (pl.program_id(0) < base + size))
        def _(g=g):
            for k in range(m):
                out[0, spots[count + k]] = refs[g * m + k][0, : out.shape[2]]

        base += size


def cut_qkv_kernel(n, spots, q_ref, k_ref, v_ref, gain_ref, span_ref, straight, across):
    rows = q_ref.shape[0]
    q_width = q_ref.shape[1] // n
    sharers = n // KV_HEADS
    gain = gain_ref[...]

    def folded(ref, i, width):
        return (ref[:, i * width : (i + 1) * width].astype(F32) * gain).astype(BF)

    for c in range(n):
        kv = c // sharers
        piece = jnp.concatenate(
            [
                folded(q_ref, c, q_width),
                folded(k_ref, kv, HEAD_DIM),
                folded(v_ref, kv, HEAD_DIM),
            ],
            axis=1,
        )
        move = spots[c]

        def fill(ref, piece=piece, move=move):
            ref[move // 2, :rows, :] = piece
            ref[move // 2, rows:, :] = jnp.broadcast_to(
                span_ref[0:16, : piece.shape[1]], (16, piece.shape[1])
            )

        pl.when(move % 2 == 0)(functools.partial(fill, straight))
        pl.when(move % 2 == 1)(functools.partial(fill, across))


def cut_qkv(n, spots, w_query, w_key, w_value, gain, span):
    rows = w_query.shape[0]
    width = w_query.shape[1] // n + 2 * HEAD_DIM
    vmem = pl.BlockSpec(memory_space=pltpu.VMEM)
    return pl.pallas_call(
        functools.partial(cut_qkv_kernel, n),
        in_specs=[pl.BlockSpec(memory_space=pltpu.SMEM)] + [vmem] * 5,
        out_specs=[vmem] * 2,
        out_shape=[jax.ShapeDtypeStruct((n // 2, rows + 16, width), BF)] * 2,
    )(spots, w_query, w_key, w_value, gain, span)


def cut_ffn_kernel(spots, gate, up, gain_ref, out):
    gain = gain_ref[...]
    width = gate.shape[1]
    out[0, :, :width] = (gate[...].astype(F32) * gain).astype(BF)
    out[0, :, width:] = (up[...].astype(F32) * gain).astype(BF)


def cut_ffn(dests, w_gate, w_up, gain):
    n = dests.shape[0]
    rows, width = w_gate.shape[0], w_gate.shape[1] // n
    block = pl.BlockSpec((rows, width), lambda i, dests: (0, dests[i]))
    return pl.pallas_call(
        cut_ffn_kernel,
        grid_spec=pltpu.PrefetchScalarGridSpec(
            num_scalar_prefetch=1,
            grid=(n,),
            in_specs=[block, block, pl.BlockSpec((rows, 1), lambda i, dests: (0, 0))],
            out_specs=pl.BlockSpec((1, rows, 2 * width), lambda i, dests: (i, 0, 0)),
        ),
        out_shape=jax.ShapeDtypeStruct((n, rows, 2 * width), BF),
    )(dests, w_gate, w_up, gain)


def term_kernel(count, m, spots, *refs):
    lefts, rights = refs[:count], refs[count : 2 * count]
    keep_ref, send_ref, held = refs[2 * count :]
    held[...] = sum(mm_t(z[...], g[...]) for z, g in zip(lefts, rights))
    rows = held.shape[0] // m
    core, side = spots[spots.shape[0] - 2], spots[spots.shape[0] - 1]
    for far in range(m // 2):
        for ref, choice in ((keep_ref, core), (send_ref, 1 - core)):
            owner = 2 * (side ^ far) + choice
            ref[far, 0] = held[pl.ds(pl.multiple_of(owner * rows, rows), rows), :].astype(BF)


def term(m, n, owners, f, lefts, rights):
    count = len(lefts)
    tokens, width = rights[0].shape
    block = lefts[0].shape[1] // n
    if n > 1 and block % 128:
        full = sum(mm_t(z, g) for z, g in zip(lefts, rights)).astype(BF)
        full = full.reshape(n, m // 2, 2, block // m, width)[owners].transpose(1, 2, 0, 3, 4)
        full = full[(f // 2) ^ jnp.arange(m // 2)]
        return pick(full, f % 2, 1), pick(full, 1 - f % 2, 1)
    out = pl.BlockSpec((m // 2, 1, block // m, width), lambda i, spots: (0, i, 0, 0))
    return pl.pallas_call(
        functools.partial(term_kernel, count, m),
        grid_spec=pltpu.PrefetchScalarGridSpec(
            num_scalar_prefetch=1,
            grid=(owners.shape[0],),
            in_specs=[pl.BlockSpec((tokens, block), lambda i, spots: (0, spots[i]))] * count
            + [pl.BlockSpec((tokens, width), lambda i, spots: (0, 0))] * count,
            out_specs=[out, out],
            scratch_shapes=[pltpu.VMEM((block, width), F32)],
        ),
        out_shape=[
            jax.ShapeDtypeStruct((m // 2, owners.shape[0], block // m, width), BF)
        ] * 2,
        compiler_params=pltpu.CompilerParams(vmem_limit_bytes=44 << 20),
        cost_estimate=pl.CostEstimate(
            flops=2 * count * tokens * owners.shape[0] * block * width,
            bytes_accessed=2 * owners.shape[0] * block * (count * tokens + width)
            + 2 * count * tokens * width,
            transcendentals=0,
        ),
    )(jnp.concatenate([owners, jnp.stack([f % 2, f // 2])]), *lefts, *rights)


def lanes(width):
    return lax.broadcasted_iota(jnp.int32, (1, width), 1)


def turned(x):
    half = HEAD_DIM // 2
    low = lanes(128) % HEAD_DIM < half
    return jnp.where(low, -pltpu.roll(x, 128 - half, 1), pltpu.roll(x, half, 1))


def in_halves(f, x):
    return jnp.concatenate([f(x[:, i : i + 128]) for i in range(0, x.shape[1], 128)], axis=1)


def fill_pads(heads, kv, row, kpad, vpad):
    width = kpad.shape[2]
    swapped = pltpu.roll(kv, HEAD_DIM, 1)
    first = lanes(128) < HEAD_DIM
    both_k = jnp.where(first, kv, swapped)
    both_v = jnp.where(first, swapped, kv)
    wide_k = jnp.concatenate([both_k] * (width // 128), axis=1)
    wide_v = jnp.concatenate([both_v] * (width // 128), axis=1)
    for h in range(heads):
        own = lanes(width) // HEAD_DIM == h
        kpad[h, row, :] = jnp.where(own, wide_k, 0.0).astype(BF)
        vpad[h, row, :] = jnp.where(own, wide_v, 0.0).astype(BF)


def key_rows(stream, each):
    step = 256

    @pl.loop(0, stream // step)
    def _(i):
        each(pl.ds(pl.multiple_of(i * step, step), step))


def hidden_bias(facts, table):
    seen = (facts[:, 64:65] == table[64:65, :]) & (table[65:66, :] <= facts[:, 65:66])
    return jnp.where(seen, 0.0, HIDE)


def spread_lanes(x):
    x = jnp.where(lanes(128) < 32, x, 0.0)
    x = x + pltpu.roll(x, 32, 1)
    return x + pltpu.roll(x, 64, 1)


def waves(facts):
    return spread_lanes(facts), spread_lanes(pltpu.roll(facts, 96, 1))


def attend_kernel(
    heads, base, act_ref, table_ref, facts_in, o_ref, lse_ref, q_ref, kv_ref, *rest
):
    kpad, vpad = rest[-2:]
    facts_ref = rest[0] if base == 0 else facts_in
    rows, width = q_ref.shape
    stream = act_ref.shape[0]

    @pl.when(pl.program_id(0) == 0)
    def _():
        def each(row):
            if base == 0:
                facts_ref[row, :] = table_ref[:, row].T
            cos, sin = waves(facts_ref[row, :])
            kv = act_ref[row, width : width + 128]
            rot = kv * cos + turned(kv) * sin
            kv = jnp.where(lanes(128) < HEAD_DIM, rot, kv)
            kv_ref[row, :] = kv.astype(BF)
            fill_pads(heads, kv, row, kpad, vpad)

        key_rows(stream, each)

    here = pl.ds(pl.multiple_of(base + pl.program_id(0) * rows, rows), rows)
    facts = facts_ref[here, :]
    cos, sin = waves(facts)
    q = in_halves(lambda x: x * cos + turned(x) * sin, act_ref[here, :width])
    q = (q * (1.0 / math.sqrt(HEAD_DIM))).astype(BF)
    q_ref[...] = q
    bias = hidden_bias(facts, table_ref)
    out = jnp.zeros((rows, width), F32)
    lse = jnp.zeros((rows, 128), F32)
    for h in range(heads):
        s = against(q, kpad[h]) + bias
        top = jnp.max(s, axis=1, keepdims=True)
        p = jnp.exp(s - top)
        total = jnp.sum(p, axis=1, keepdims=True)
        out = out + mm(p.astype(BF), vpad[h]) / total
        lse = jnp.where(lanes(128) == h, top + jnp.log(total), lse)
    o_ref[...] = out.astype(BF)
    lse_ref[...] = lse


def attend_back_kernel(
    heads, base, first, q_ref, g_ref, kv_ref, table_ref, facts_ref, inv_ref, lse_ref, *rest
):
    if first:
        ga_ref, gs_ref, dk_out, dv_out, kpad, vpad, dk, dv = rest
    else:
        dk_in, dv_in, ga_ref, gs_ref, kv_ga, kv_gs, kpad, vpad, dk, dv = rest
    rows, width = q_ref.shape
    stream = kv_ref.shape[0]

    @pl.when(pl.program_id(0) == 0)
    def _():
        key_rows(stream, lambda row: fill_pads(heads, kv_ref[row, :].astype(F32), row, kpad, vpad))
        dk[...] = jnp.zeros_like(dk) if first else dk_in[...]
        dv[...] = jnp.zeros_like(dv) if first else dv_in[...]

    here = pl.ds(pl.multiple_of(base + pl.program_id(0) * rows, rows), rows)
    bias = hidden_bias(facts_ref[here, :], table_ref)
    q = q_ref[...]
    g = g_ref[...]
    dq = jnp.zeros((rows, width), F32)
    for h in range(heads):
        p = jnp.exp(against(q, kpad[h]) + (bias - lse_ref[:, h : h + 1]))
        dp = against(g, vpad[h])
        delta = jnp.sum(p * dp, axis=1, keepdims=True)
        ds = (p * (dp - delta)).astype(BF)
        dq = dq + mm(ds, kpad[h])
        own = lanes(width) // HEAD_DIM == h
        dk[...] += mm_t(ds, jnp.where(own, q, 0).astype(BF))
        dv[...] += mm_t(p.astype(BF), jnp.where(own, g, 0).astype(BF))
    dq = dq * (1.0 / math.sqrt(HEAD_DIM))

    def turn_back(row, x):
        cos, sin = waves(facts_ref[row, :])
        return x * cos - turned(x * sin)

    ga = in_halves(lambda x: turn_back(here, x), dq)
    ga_ref[...] = ga.astype(BF)
    gs_ref[...] = (ga * inv_ref[here, :]).astype(BF)

    @pl.when(pl.program_id(0) == pl.num_programs(0) - 1)
    def _():
        if first:
            dk_out[...] = dk[...]
            dv_out[...] = dv[...]
            return

        def folded(x):
            x = sum(x[:, i : i + 128] for i in range(0, width, 128))
            return x + pltpu.roll(x, HEAD_DIM, 1)

        def each(row):
            gk = turn_back(row, folded(dk[row, :]))
            gkv = jnp.where(lanes(128) < HEAD_DIM, gk, folded(dv[row, :]))
            kv_ga[row, :] = gkv.astype(BF)
            kv_gs[row, :] = (gkv * inv_ref[row, :]).astype(BF)

        key_rows(stream, each)


def attend_specs(rows, stream, base):
    def part(width):
        return pl.BlockSpec((rows, width), lambda i: (i, 0))

    def by_row(width):
        return pl.BlockSpec((rows, width), lambda i: (i + base // rows, 0))

    def whole(width):
        return pl.BlockSpec((stream, width), lambda i: (0, 0))

    return part, by_row, whole


def attend(heads, half, act, table, facts=None):
    stream, width = act.shape
    width, count = width - 128, stream // 2
    base = half * count
    rows = 256 if stream <= 1024 else 128
    part, by_row, whole = attend_specs(rows, stream, base)
    first = half == 0
    return pl.pallas_call(
        functools.partial(attend_kernel, heads, base),
        grid=(count // rows,),
        in_specs=[
            whole(width + 128),
            pl.BlockSpec((128, stream), lambda i: (0, 0)),
            pl.BlockSpec((8, 128), lambda i: (0, 0)) if first else whole(128),
        ],
        out_specs=[part(width), part(128), part(width), whole(128)] + [whole(128)] * first,
        out_shape=[
            jax.ShapeDtypeStruct((count, width), BF),
            jax.ShapeDtypeStruct((count, 128), F32),
            jax.ShapeDtypeStruct((count, width), BF),
            jax.ShapeDtypeStruct((stream, 128), BF),
        ]
        + [jax.ShapeDtypeStruct((stream, 128), F32)] * first,
        scratch_shapes=[pltpu.VMEM((heads, stream, width), BF)] * 2,
        compiler_params=pltpu.CompilerParams(vmem_limit_bytes=44 << 20),
        cost_estimate=pl.CostEstimate(
            flops=4 * stream * count * heads * 256,
            bytes_accessed=8 * stream * width,
            transcendentals=stream * count * heads,
        ),
    )(act, table, jnp.zeros((8, 128), F32) if first else facts)


def attend_back(heads, half, q, g, kv, table, facts, inverse, lse, sums=()):
    count, width = q.shape
    stream = kv.shape[0]
    base = half * count
    rows = 256 if stream <= 1024 else 128
    part, by_row, whole = attend_specs(rows, stream, base)
    first = half == 0
    last_width, last_type = (width, F32) if first else (128, BF)
    return pl.pallas_call(
        functools.partial(attend_back_kernel, heads, base, first),
        grid=(count // rows,),
        in_specs=[
            part(width), part(width), whole(128),
            pl.BlockSpec((128, stream), lambda i: (0, 0)), whole(128), whole(1), part(128),
        ] + [whole(width)] * len(sums),
        out_specs=[part(width)] * 2 + [whole(last_width)] * 2,
        out_shape=[jax.ShapeDtypeStruct((count, width), BF)] * 2
        + [jax.ShapeDtypeStruct((stream, last_width), last_type)] * 2,
        scratch_shapes=[
            *([pltpu.VMEM((heads, stream, width), BF)] * 2),
            *([pltpu.VMEM((stream, width), F32)] * 2),
        ],
        compiler_params=pltpu.CompilerParams(vmem_limit_bytes=48 << 20),
        cost_estimate=pl.CostEstimate(
            flops=10 * stream * count * heads * 256,
            bytes_accessed=20 * stream * width,
            transcendentals=stream * count * heads,
        ),
    )(q, g, kv, table, facts, inverse, lse, *sums)


def finish_ffn_kernel(n, spots, *refs):
    gate_ref, up_ref, gain_ref, og_ref, ou_ref, gg_ref = refs[n:]
    width = gate_ref.shape[1]
    gain = gain_ref[...]
    step = pl.program_id(0)

    @pl.when(step == 0)
    def _():
        gg_ref[...] = jnp.zeros_like(gg_ref)

    for k in range(n):

        @pl.when(step == k)
        def _(piece=refs[k]):
            gate = piece[:, :width].astype(F32)
            up = piece[:, width:].astype(F32)
            og_ref[...] = gate * gain
            ou_ref[...] = up * gain
            term = jnp.sum(
                gate * gate_ref[...].astype(F32) + up * up_ref[...].astype(F32),
                axis=1,
                keepdims=True,
            )
            gg_ref[...] += jnp.broadcast_to(term, gg_ref.shape)


def finish_ffn(pieces, spots, w_gate, w_up, gain):
    n = len(pieces)
    rows, both = pieces[0].shape
    width = both // 2
    block = pl.BlockSpec((rows, width), lambda i, spots: (0, spots[i]))
    return pl.pallas_call(
        functools.partial(finish_ffn_kernel, n),
        grid_spec=pltpu.PrefetchScalarGridSpec(
            num_scalar_prefetch=1,
            grid=(n,),
            in_specs=[pl.BlockSpec((rows, both), lambda i, spots: (0, 0))] * n
            + [block, block, pl.BlockSpec((rows, 1), lambda i, spots: (0, 0))],
            out_specs=[block, block, pl.BlockSpec((rows, 128), lambda i, spots: (0, 0))],
        ),
        out_shape=[
            jax.ShapeDtypeStruct(w_gate.shape, F32),
            jax.ShapeDtypeStruct(w_gate.shape, F32),
            jax.ShapeDtypeStruct((rows, 128), F32),
        ],
        compiler_params=pltpu.CompilerParams(vmem_limit_bytes=24 << 20),
    )(spots, *pieces, w_gate, w_up, gain)


def finish_qkv_kernel(n, spots, pieces, q_ref, k_ref, v_ref, gain_ref, oq, ok, ov, gg_ref):
    q_width = q_ref.shape[1] // n
    sharers = n // KV_HEADS
    gain = gain_ref[...]
    term = jnp.zeros((q_ref.shape[0], 1), F32)
    for kv in range(KV_HEADS):
        held = 0.0
        for j in range(sharers):
            c = kv * sharers + j
            piece = pieces[spots[c]].astype(F32)
            here = slice(c * q_width, (c + 1) * q_width)
            q = piece[:, :q_width]
            held = held + piece[:, q_width:]
            oq[:, here] = q * gain
            term += jnp.sum(q * q_ref[:, here].astype(F32), axis=1, keepdims=True)
        here = slice(kv * HEAD_DIM, (kv + 1) * HEAD_DIM)
        k, v = held[:, :HEAD_DIM], held[:, HEAD_DIM:]
        ok[:, here] = k * gain
        ov[:, here] = v * gain
        term += jnp.sum(
            k * k_ref[:, here].astype(F32) + v * v_ref[:, here].astype(F32), axis=1, keepdims=True
        )
    gg_ref[...] = jnp.broadcast_to(term, gg_ref.shape)


def finish_qkv(pieces, spots, w_query, w_key, w_value, gain):
    n, rows, _ = pieces.shape
    vmem = pl.BlockSpec(memory_space=pltpu.VMEM)
    return pl.pallas_call(
        functools.partial(finish_qkv_kernel, n),
        in_specs=[pl.BlockSpec(memory_space=pltpu.SMEM)] + [vmem] * 5,
        out_specs=[vmem] * 4,
        out_shape=[
            jax.ShapeDtypeStruct(w_query.shape, F32),
            jax.ShapeDtypeStruct(w_key.shape, F32),
            jax.ShapeDtypeStruct(w_value.shape, F32),
            jax.ShapeDtypeStruct((rows, 128), F32),
        ],
    )(spots, pieces, w_query, w_key, w_value, gain)


def norm_back(grad_scaled, unit_rows, inverse):
    return inverse * (
        grad_scaled - unit_rows * jnp.mean(grad_scaled * unit_rows, axis=1, keepdims=True)
    )


def rms_inverse(values):
    return lax.rsqrt(jnp.mean(values * values, axis=1, keepdims=True) + EPSILON)


def body(
    tokens,
    teacher,
    valid_mask,
    lengths,
    span_order,
    w_query,
    w_key,
    w_value,
    w_out,
    w_gate,
    w_up,
    w_down,
    gain_attn,
    gain_ffn,
):
    net = Links()
    n, m, ring = net.n, net.m, net.ring
    x_low = tokens[0]
    tok_rows, width = x_low.shape
    rows = w_query.shape[0]
    heads = HEADS // n
    q_width = heads * HEAD_DIM
    sharers = n // KV_HEADS
    ff_slice = w_gate.shape[1] // n
    stream = tok_rows * n
    spans = tok_rows // SPAN

    jobs, box = net.jobs, net.box

    def later(name, key, job):
        jobs.setdefault(name, {})[key] = job

    def core(x):
        return net.flip(x, "fsdp", 1)

    def side(x):
        return net.flip(x, "fsdp", 2)

    gain_a = gain_attn.astype(F32)[:, None]
    gain_f = gain_ffn.astype(F32)[:, None]
    routes, origins = net.routes(), net.origins()
    pair_moves = [(da, dq) for da in range(ring) for dq in range(2)]
    dests, sources = net.dests(pair_moves), net.sources(pair_moves)
    span_row = jnp.broadcast_to(
        jnp.pad(span_order[0].astype(BF), (0, q_width + 2 * HEAD_DIM - spans))[None, :],
        (16, q_width + 2 * HEAD_DIM),
    )
    straight, across = cut_qkv(n, routes, w_query, w_key, w_value, gain_a, span_row)

    def along(first, other):
        def job(begun):
            ready = tie(jnp.stack([first, box[other]], axis=1), begun)
            return [net.shift(ready[da], da, 0) if da else ready[da] for da in range(ring)]

        return job

    half_rows = w_down.shape[0] // 2
    later("ax0", "q_across", lambda begun: net.shift(across, 0, 1))
    later("ax1", "out_side", lambda begun: side(tie(w_out, begun)))
    later("ax0", "down_side_0", lambda begun: side(w_down[:half_rows]))
    later("ax1", "q_came", along(straight, "q_across"))

    def q_side(begun):
        came = jnp.concatenate(box["q_came"], axis=0)
        return came, side(came)

    later("ax2", "q_sides", q_side)
    later("ax2", "out_core", lambda begun: [core(tie(w_out, begun)), core(box["out_side"])])
    later("ax3", "down_side_1", lambda begun: side(tie(w_down[half_rows:], begun)))
    token_blocks = net.gather_ctx(x_low, "ax")
    q_came, q_other = box["q_sides"]
    qkv_w = net.assemble([[q_came, core(q_came), q_other, core(q_other)]], sources, rows)
    spans_here = tie(q_came, qkv_w)[:, rows, :spans].astype(jnp.int32).reshape(n * spans)
    padding = (-q_width) % 128

    def with_padding(array):
        if not padding:
            return array
        return jnp.concatenate(
            [
                jnp.pad(array[:, :q_width], ((0, 0), (0, padding))),
                array[:, q_width:],
            ],
            axis=1,
        )

    def no_padding(array):
        if not padding:
            return array
        return jnp.concatenate([array[:, :q_width], array[:, q_width + padding :]], axis=1)

    qkv_w = with_padding(qkv_w)
    alone = jnp.zeros((1,), jnp.int32)
    out_w = net.assemble(
        [[x[None] for x in (w_out, box["out_core"][0], box["out_side"], box["out_core"][1])]],
        alone,
        rows,
    )

    direct = net.direct()
    quarter = n // 4
    gate_in, up_in = tie((w_gate, w_up), token_blocks[1][0][0])
    gate_up_cut = cut_ffn(net.dests(direct), gate_in, up_in, gain_f)
    came_ffn = [gate_up_cut[0]]

    def send(pieces, begun, start, stop):
        pieces = tie(pieces, begun)
        return [net.shift(pieces[i], *direct[i]) for i in range(start, stop)]

    place = (
        spans_here[:, None] * SPAN + lax.broadcasted_iota(jnp.int32, (n * spans, SPAN), 1)
    ).reshape(stream)
    seq_ends = jnp.cumsum(lengths[0])
    passed = seq_ends[None, :] <= place[:, None]
    segment = jnp.sum(passed.astype(jnp.int32), axis=1)
    seq_begin = jnp.sum(jnp.where(passed, lengths[0][None, :], 0), axis=1)
    rates = jnp.asarray(rope_rates(HEAD_DIM)[: HEAD_DIM // 2])
    angles = rates[:, None] * (place - seq_begin).astype(F32)[None, :]
    table = jnp.concatenate(
        [
            jnp.cos(angles),
            jnp.sin(angles),
            segment.astype(F32)[None, :],
            place.astype(F32)[None, :],
            jnp.zeros((128 - 66, stream), F32),
        ],
        axis=0,
    )

    x_pairs, inverses, acts_attn = [], [], []
    pair_rows = 2 * tok_rows
    for r in range(ring):
        x_pair = paired(token_blocks[r])
        inverse = rms_inverse(x_pair.astype(F32))
        x_pairs.append(x_pair)
        inverses.append(inverse)
        acts_attn.append(mm(x_pair, qkv_w) * inverse)
    inverse_all = jnp.concatenate(inverses, axis=0)
    act_all = jnp.concatenate(acts_attn, axis=0)
    cuts = [1, max(1, 0 * n // 8), 4 * n // 8, 6 * n // 8, 7 * n // 8, n]
    first = attend(heads, 0, act_all, table)
    sent = send(gate_up_cut, qkv_w, cuts[1], cuts[2])
    act_all, sent = lax.optimization_barrier((act_all, sent))
    came_ffn += sent
    facts = first[4]
    second = attend(heads, 1, act_all, table, facts)
    kv_rot = second[3]
    attended_halves = first[0], second[0]

    def split_pair(block):
        return block[:tok_rows], block[tok_rows:]

    def pair_of(array, r):
        return array[r * pair_rows : (r + 1) * pair_rows]

    inputs = x_low.astype(F32)

    def of_halves(halves, r):
        which, start = divmod(r * pair_rows, stream // 2)
        return halves[which][start : start + pair_rows]

    for i in range(3):
        later(f"ro{i}", f"f_{i}", lambda begun, i=i: send(gate_up_cut, begun, cuts[2 + i], cuts[3 + i]))
    for g in range(4):

        def g_side(begun, g=g):
            pieces = came_ffn + sum((box[f"f_{i}"] for i in range(g)), [])
            block = tie(jnp.stack(pieces[g * quarter : (g + 1) * quarter]), begun)
            return block, side(block)

        def g_core(begun, g=g):
            return [core(x) for x in box[f"g_side{g}"]]

        later(f"ro{g}", f"g_side{g}", g_side)
        later(f"ro{g + 1}" if g < 3 else "ff0", f"g_core{g}", g_core)
    later("ro0", "down_core", lambda begun: core(tie(w_down, begun)))

    def down_far(begun):
        return core(jnp.concatenate([box["down_side_0"], box["down_side_1"]], axis=0))

    later("ff0", "down_far", down_far)
    middle = inputs + net.scatter_ctx(
        lambda r: split_pair(mm(of_halves(attended_halves, r)[:, :q_width], out_w)), "ro"
    )

    inverse_ffn = rms_inverse(middle)
    unit_ffn = middle * inverse_ffn
    unit_blocks = net.gather_ctx(unit_ffn.astype(BF), "ff")
    gate_up_w = net.assemble(
        [
            [box[f"g_side{g}"][0], box[f"g_core{g}"][0], box[f"g_side{g}"][1], box[f"g_core{g}"][1]]
            for g in range(4)
        ],
        net.sources(direct),
        rows,
    )
    down_sides = jnp.concatenate([box["down_side_0"], box["down_side_1"]], axis=0)
    down_w = net.assemble(
        [[x[None] for x in (w_down, box["down_core"], down_sides, box["down_far"])]],
        alone,
        w_down.shape[0],
    )
    z_pairs = [paired(blocks) for blocks in unit_blocks]
    acts, hiddens = {}, {}

    def down_part(r):
        both = mm(z_pairs[r], gate_up_w)
        gate, up = both[:, :ff_slice], both[:, ff_slice:]
        acts[r] = (gate, up)
        hiddens[r] = (gate * jax.nn.sigmoid(gate) * up).astype(BF)
        return split_pair(mm(hiddens[r], down_w))

    out_full = middle + net.scatter_ctx(down_part, "fo")

    valid_f = valid_mask[0].astype(F32)[:, None]
    missed = (out_full - teacher[0].astype(F32)) * valid_f
    sums = jnp.stack([jnp.sum(missed * missed), jnp.sum(valid_f)]).reshape(1, 2)
    grad_out = missed

    grad_blocks = net.gather_ctx(grad_out.astype(BF), "bf")
    grad_pairs = [paired(blocks) for blocks in grad_blocks]
    grad_acts = {}

    def unit_part(r):
        gate, up = acts[r]
        grad_hidden = against(grad_pairs[r], down_w)
        share = jax.nn.sigmoid(gate)
        grad_gate = grad_hidden * up * share * (1.0 + gate * (1.0 - share))
        grad_up = grad_hidden * (gate * share)
        grad_acts[r] = jnp.concatenate([grad_gate.astype(BF), grad_up.astype(BF)], axis=1)
        return split_pair(against(grad_acts[r], gate_up_w))

    owners = net.dests(direct)
    term_slots = ["bo2", "bo3", "am0", "am1", "am2", "am3", "ar0"]

    def listed(items):
        return [items[r] for r in range(ring)]

    for g in range(4):

        def g_term(begun, g=g):
            lefts, rights = tie((z_pairs, listed(grad_acts)), begun)
            return term(m, n, owners[g * quarter : (g + 1) * quarter], net.f, lefts, rights)

        def g_cross(begun, g=g):
            return core(box[f"t{g}"][1])

        def g_far(begun, g=g):
            keep, got = box[f"t{g}"][0], box[f"tc{g}"]
            return side((keep[1].astype(F32) + got[1]).astype(BF))

        later(term_slots[g], f"t{g}", g_term)
        later(term_slots[g + 1], f"tc{g}", g_cross)
        later(term_slots[g + 2], f"ts{g}", g_far)

    def d_term(begun):
        lefts, rights = tie((listed(hiddens), grad_pairs), begun)
        return term(m, 1, alone, net.f, lefts, rights)

    later("am2", "d", d_term)
    later("am3", "dc", lambda begun: core(box["d"][1]))

    def d_far(begun):
        block = (tie(box["d"][0], begun)[1, 0].astype(F32) + box["dc"][1, 0]).astype(BF)
        return block[half_rows:], side(block[:half_rows])


    axes = [("ctx", 1 << i) for i in range((n - 1).bit_length())]
    axes += [("fsdp", 1 << i) for i in range((m - 1).bit_length())]
    spots = [f"am{r}" for r in range(ring)] + [f"ar{r}" for r in range(ring)]
    box["sums"] = sums
    for name, (axis, bit) in zip(spots, axes):
        later(name, "sums", lambda begun, a=axis, b=bit: box["sums"] + net.flip(tie(box["sums"], begun), a, b))

    unit_parts = {r: unit_part(r) for r in net.scatter_order()}
    grad_unit = net.scatter_ctx(unit_parts.get, "bo")
    grad_middle = grad_out + norm_back(grad_unit, unit_ffn, inverse_ffn)
    middle_low = grad_middle.astype(BF)

    middle_blocks = net.gather_ctx(middle_low, "am")
    middle_pairs = [paired(blocks) for blocks in middle_blocks]

    def summed(i):
        g, at = divmod(i, quarter)
        keep, got, far = box[f"t{g}"][0], box[f"tc{g}"], box[f"ts{g}"]
        return (keep[0, at].astype(F32) + got[0, at] + far[at]).astype(BF)

    def send_sum(begun, start, stop):
        return [net.shift(tie(summed(i), begun), *direct[i]) for i in range(start, stop)]

    def back_half(half):
        parts = [
            against(middle_pairs[r], out_w).astype(BF)
            for r in range(half * ring // 2, (half + 1) * ring // 2)
        ]
        grads = jnp.concatenate(parts, axis=0)
        return jnp.pad(grads, ((0, 0), (0, padding))) if padding else grads

    grads_first, grads_second = back_half(0), back_half(1)
    came_sums = [summed(0)]
    cuts = [1, 3 * n // 8, 5 * n // 8, 7 * n // 8, n]
    sent = send_sum(middle_blocks[-1][0][0], cuts[0], cuts[1])
    grads_first, grads_second, sent = lax.optimization_barrier((grads_first, grads_second, sent))
    came_sums += sent
    fixed = kv_rot, table, facts, inverse_all
    sent, box["ds0"] = send_sum(grads_first, cuts[1], cuts[2]), d_far(grads_first)
    backed = attend_back(heads, 0, first[2], grads_first, *fixed, first[1])
    backed, grads_second, sent, box["ds0"] = lax.optimization_barrier(
        (backed, grads_second, sent, box["ds0"])
    )
    came_sums += sent
    gq_first, gs_first, sum_k, sum_v = backed
    sent = send_sum(grads_second, cuts[2], cuts[3])
    box["ds1"] = side(tie(box["ds0"][0], grads_second))
    backed = attend_back(heads, 1, second[2], grads_second, *fixed, second[1], (sum_k, sum_v))
    (gq_second, gs_second, g_kv, gs_kv), sent, box["ds1"] = lax.optimization_barrier(
        (backed, sent, box["ds1"])
    )
    came_sums += sent

    def attn_part(r):
        rows_q = of_halves((gq_first, gq_second), r)
        grads = jnp.concatenate([rows_q, pair_of(g_kv, r)], axis=1)
        return split_pair(against(grads, qkv_w))

    def q_term(begun):
        grads = [
            jnp.concatenate([of_halves((gs_first, gs_second), r), pair_of(gs_kv, r)], axis=1)
            for r in range(ring)
        ]
        lefts, grads = tie((x_pairs, grads), begun)
        return term(m, n, dests, net.f, lefts, grads)

    def q_back(begun):
        (keep, _), got = box["qt"], box["qc"]
        block = keep[0].astype(F32) + got[0] + box["qs"]
        if padding:
            block = jnp.concatenate([block[..., :q_width], block[..., q_width + padding :]], axis=2)
        block = block.astype(BF).reshape(ring, 2, rows, q_width + 2 * HEAD_DIM)
        return block[:, 0], net.shift(block[:, 1], 0, 1)

    def q_along(begun):
        ready = tie(jnp.stack(box["qb"], axis=1), begun)
        return [net.shift(ready[da], da, 0) if da else ready[da] for da in range(ring)]

    def o_term(begun):
        lefts = [of_halves(attended_halves, r)[:, :q_width] for r in range(ring)]
        lefts, grads = tie((lefts, middle_pairs), begun)
        return term(m, 1, alone, net.f, lefts, grads)

    def crossed(key, made):
        return lambda begun: core(tie(box[made][1], begun))

    def farther(made, got):
        return lambda begun: side((box[made][0][1].astype(F32) + box[got][1]).astype(BF))

    def ends(begun):
        square_sum, valid_count = box["sums"][0, 0], box["sums"][0, 1]
        box["loss"] = 0.5 * square_sum / (width * valid_count)
        box["spread"] = (tok_rows * n * m) / valid_count
        pieces = tie(came_sums + box["c_last"], begun)
        return finish_ffn(pieces, net.sources(direct), w_gate, w_up, gain_f * box["spread"])

    later("ar0", "ot", o_term)
    later("ar0", "qt", q_term)
    later("ar0", "c_last", lambda begun: send_sum(begun, cuts[3], n))
    later("ar1", "qc", crossed("qc", "qt"))
    later("ar1", "oc", crossed("oc", "ot"))
    later("ar2", "qs", farther("qt", "qc"))
    later("ar2", "os", farther("ot", "oc"))
    later("ar3", "qb", q_back)
    later(f"ar{max(2, len(axes) - ring)}", "ffn", ends)
    grad_attn = net.scatter_ctx(attn_part, "ar")
    spread = box["spread"]
    inverse_attn = rms_inverse(inputs)
    grad_input = grad_middle + norm_back(grad_attn, inputs * inverse_attn, inverse_attn)
    grad_w_query, grad_w_key, grad_w_value, gain_sum_attn = finish_qkv(
        jnp.concatenate(q_along(grad_attn), axis=0), origins, w_query, w_key, w_value, gain_a * spread
    )
    grad_w_out = (box["ot"][0][0, 0].astype(F32) + box["oc"][0, 0] + box["os"][0]) * spread
    down_keep = box["d"][0][0, 0].astype(F32) + box["dc"][0, 0]
    down_far = jnp.concatenate([box["ds0"][1], box["ds1"]], axis=0)
    grad_down = down_keep + down_far
    grad_w_gate, grad_w_up, gain_sum_ffn = box["ffn"]
    loss_value = box["loss"]
    return (
        out_full.astype(BF)[None],
        loss_value,
        (grad_input * spread)[None],
        grad_w_query,
        grad_w_key,
        grad_w_value,
        grad_w_out,
        grad_w_gate,
        grad_w_up,
        grad_down * spread,
        gain_sum_attn[:, 0] * spread,
        gain_sum_ffn[:, 0] * spread,
    )


def solution(mesh):
    token_spec = P("fsdp", "ctx", None)
    row_spec = P(("ctx", "fsdp"), None)
    gain_spec = P(("ctx", "fsdp"))
    in_specs = (
        token_spec,
        token_spec,
        P("fsdp", "ctx"),
        P("fsdp", None),
        P("fsdp", "ctx"),
        *([row_spec] * 7),
        gain_spec,
        gain_spec,
    )
    out_specs = (token_spec, P(), token_spec, *([row_spec] * 7), gain_spec, gain_spec)
    return jax.shard_map(body, mesh=mesh, in_specs=in_specs, out_specs=out_specs, check_vma=False)
```

time: 941 us -> 618 us (0.66)
  local copies, waits for them, and re-layouts: 248 us -> 51.7 us
  waiting for transfers between devices: 334 us -> 202 us
  Pallas kernels: 26.5 us -> 100 us
  matrix products: 108 us -> 52.4 us
  other arithmetic: 80.4 us -> 68.3 us
    ppermute x84 -> x92, waiting for transfers between devices: 301 us -> 168 us  [shift(): return lax.ppermute(x, 'ctx', perm)]
    dynamic_update_slice x44 -> x0, local copies, waits for them, and re-layouts: 110 us -> none  [the longest x28 88.7 us: exchange_ctx(): out = lax.dynamic_update_slice(out, got[None], (src,) + zeros)]
    pallas_call x2 -> x19, Pallas kernels: 26.5 us -> 100 us  [the longest x7 34.7 us: term(): pl.pallas_call(functools.partial(term_kernel, count, m), grid_spec=pltpu....]
    dot_general x4 -> x0, matrix products: 27.9 us -> none  [mm_t(): lax.dot_general(left, right, (((0,), (0,)), ((), ())), preferred_element_...]
    unnamed x209 -> x438, local copies, waits for them, and re-layouts: 51.4 us -> 26.3 us
    broadcast_in_dim x18 -> x5, local copies, waits for them, and re-layouts: 22.8 us -> 2.05 us  [the longest x1 0.71 us: body(): gain_f = gain_ffn.astype(F32)[:, None]]
    another operation x23 -> x2, local copies, waits for them, and re-layouts: 17.8 us -> 0.69 us  [dests(): return jnp.stack(spots).astype(jnp.int32)]
    dot_general x18 -> x16, matrix products: 44.6 us -> 29.7 us  [against(): lax.dot_general(left, right, (((1,), (1,)), ((), ())), preferred_element_...]
  transfers between devices with their start and end apart: 114 -> 134, of which waited for: 53 -> 46; matrix products, arithmetic and copies ran while one was open for 44% -> 22% of each run, Pallas kernels for 3% -> 16%
where the time goes in v2:
time: 618 us; the launch traced here: 608 us
  waiting for transfers between devices  202 us (33%)
  starting transfers between devices  125 us (20%)
  Pallas kernels  100 us (16%)
  other arithmetic  68.3 us (11%)
  matrix products  52.4 us (8%)
  local copies, waits for them, and re-layouts  51.7 us (8%)
  between operations  8.3 us (1%)
    ppermute x92, waiting for transfers between devices, shift(): return lax.ppermute(x, 'ctx', perm)  168 us
    ppermute x92, starting transfers between devices, shift(): return lax.ppermute(x, 'ctx', perm)  96 us
    pallas_call x7, Pallas kernels, term(): pl.pallas_call(functools.partial(term_kernel, count, m), grid_spec=pltpu....  34.7 us
    ppermute x42, waiting for transfers between devices, flip(): return lax.ppermute(x, axis, [(i, i ^ bit) for i in range(size)])  33.8 us
    dot_general x16, matrix products, against(): lax.dot_general(left, right, (((1,), (1,)), ((), ())), preferred_element_...  29.7 us
    ppermute x42, starting transfers between devices, flip(): return lax.ppermute(x, axis, [(i, i ^ bit) for i in range(size)])  29.3 us
    unnamed x438, local copies, waits for them, and re-layouts  26.3 us
    dot_general x16, matrix products, mm(): return jnp.dot(left, right, preferred_element_type=F32)  22.7 us
  transfers between devices with their start and end apart: 134, of which 46 were waited for; matrix products, arithmetic and copies ran while one was open for 22% of the time, Pallas kernels for 16%

profile of v2, /device:TPU:0, one launch (start us, length us, event | category | flops | bytes accessed | tf_op | source)
XLA Modules:
  0.0 607.6 jit_solution(7591070687553574648)
XLA Ops:
  0.7 3.0 collective-permute-start
  11.4 2.5 shard_map.238
  16.1 5.0 collective-permute-done.3
  31.7 6.8 %shard_map.242 = bf16[8,64,2048]{2,1,0:T(8,128)(2,1)} custom-call(s32[8]{0:T(128)} %stack.75.spots, bf16[64,8192]{1,0:T(8,128)(2,1)} %refs_8_.1, bf16[64,8192]{1,0:T(8,128)(2,1)} %refs_9_.1, f32[64,1]{1,0:T(8,128)} %copy.51.gain_ref), custom_call_target="tpu_custom_call" | custom-call | tf_op jit(solution)/shard_map/pallas_call | solution.py:251
  38.8 3.4 collective-permute-done.7
  54.9 5.6 collective-permute-done.14.refs_2_
  70.7 3.8 collective-permute-start.20
  85.3 7.6 %shard_map.240 = (bf16[512,256]{1,0:T(8,128)(2,1)S(1)}, f32[512,128]{1,0:T(8,128)S(1)}, bf16[512,256]{1,0:T(8,128)(2,1)S(1)}, bf16[1024,128]{1,0:T(8,128)(2,1)}, f32[1024,128]{1,0:T(8,128)S(1)}) custom-call(f32[1024,384]{1,0:T(8,128)S(1)} %pad_maximum_fusion.act_ref, f32[128,1024]{1,0:T(8,128)S(1)} %concatenate.181.table_ref, ...), custom_call_target="tpu_custom_call" | custom-call | flops 2147483648 | bytes 2097152 | tf_op jit(solution)/shard_map/pallas_call | solution.py:481
  99.4 7.1 %shard_map.243 = (bf16[512,256]{1,0:T(8,128)(2,1)S(1)}, f32[512,128]{1,0:T(8,128)S(1)}, bf16[512,256]{1,0:T(8,128)(2,1)S(1)}, bf16[1024,128]{1,0:T(8,128)(2,1)S(1)}) custom-call(f32[1024,384]{1,0:T(8,128)S(1)} %pad_maximum_fusion.act_ref, f32[128,1024]{1,0:T(8,128)S(1)} %copy-done.68, f32[1024,128]{1,0:T(8,128)S(1)} %get-tuple-element.352.facts_in.facts_ref), custom_call_target="tpu_custom_call" | custom-call | flops 2147483648 | bytes 2097152 | tf_op jit(solution)/shard_map/pallas_call | solution.py:481
  108.4 9.3 %collective-permute-done.24 = bf16[64,2048]{1,0:T(8,128)(2,1)S(1)} collective-permute-done((bf16[64,2048]{1,0:T(8,128)(2,1)S(1)}, bf16[64,2048]{1,0:T(8,128)(2,1)S(1)}, u32[]{:S(2)}, u32[]{:S(2)}) %collective-permute-start.24) | collective-permute-done | bytes 262176 | tf_op jit(solution)/shard_map/ppermute | solution.py:76
  122.1 7.0 %collective-permute-done.29 = bf16[64,2048]{1,0:T(8,128)(2,1)S(1)} collective-permute-done((bf16[64,2048]{1,0:T(8,128)(2,1)S(1)}, bf16[64,2048]{1,0:T(8,128)(2,1)S(1)}, u32[]{:S(2)}, u32[]{:S(2)}) %collective-permute-start.29) | collective-permute-done | bytes 262176 | tf_op jit(solution)/shard_map/ppermute | solution.py:76
  129.9 8.7 %collective-permute-done.28 = bf16[128,2048]{1,0:T(8,128)(2,1)S(1)} collective-permute-done((bf16[128,2048]{1,0:T(8,128)(2,1)S(1)}, bf16[128,2048]{1,0:T(8,128)(2,1)S(1)}, u32[]{:S(2)}, u32[]{:S(2)}) %collective-permute-start.28) | collective-permute-done | bytes 524320 | tf_op jit(solution)/shard_map/ppermute | solution.py:76
  143.1 20.3 %collective-permute-done.35 = bf16[64,2048]{1,0:T(8,128)(2,1)S(1)} collective-permute-done((bf16[64,2048]{1,0:T(8,128)(2,1)S(1)}, bf16[64,2048]{1,0:T(8,128)(2,1)S(1)}, u32[]{:S(2)}, u32[]{:S(2)}) %collective-permute-start.35) | collective-permute-done | bytes 262176 | tf_op jit(solution)/shard_map/ppermute | solution.py:76
  171.5 9.9 %collective-permute-done.43.refs_14_ = bf16[2,64,2048]{2,1,0:T(8,128)(2,1)} collective-permute-done((bf16[2,64,2048]{2,1,0:T(8,128)(2,1)}, bf16[2,64,2048]{2,1,0:T(8,128)(2,1)}, u32[]{:S(2)}, u32[]{:S(2)}) %collective-permute-start.43) | collective-permute-done | bytes 524320 | tf_op jit(solution)/shard_map/ppermute | solution.py:80
  189.1 9.1 %collective-permute-done.44 = bf16[128,2048]{1,0:T(8,128)(2,1)} collective-permute-done((bf16[128,2048]{1,0:T(8,128)(2,1)}, bf16[128,2048]{1,0:T(8,128)(2,1)}, u32[]{:S(2)}, u32[]{:S(2)}) %collective-permute-start.44) | collective-permute-done | bytes 524320 | tf_op jit(solution)/shard_map/ppermute | solution.py:76
  198.3 2.4 collective-permute-done.45
  205.4 5.7 shard_map.245
  211.2 4.6 shard_map.244
  217.4 2.4 fusion.122
  226.7 10.6 %collective-permute-done.54 = bf16[128,2048]{1,0:T(8,128)(2,1)S(1)} collective-permute-done((bf16[128,2048]{1,0:T(8,128)(2,1)S(1)}, bf16[128,2048]{1,0:T(8,128)(2,1)S(1)}, u32[]{:S(2)}, u32[]{:S(2)}) %collective-permute-start.54) | collective-permute-done | bytes 524320 | tf_op jit(solution)/shard_map/ppermute | solution.py:76
  237.4 7.2 %collective-permute-done.51 = bf16[128,2048]{1,0:T(8,128)(2,1)S(1)} collective-permute-done((bf16[128,2048]{1,0:T(8,128)(2,1)S(1)}, bf16[128,2048]{1,0:T(8,128)(2,1)S(1)}, u32[]{:S(2)}, u32[]{:S(2)}) %collective-permute-start.51) | collective-permute-done | bytes 524320 | tf_op jit(solution)/shard_map/ppermute | solution.py:76
  244.7 2.4 fusion.120
  250.9 3.6 fusion.92
  254.6 9.2 %collective-permute-done.55 = bf16[128,2048]{1,0:T(8,128)(2,1)S(1)} collective-permute-done((bf16[128,2048]{1,0:T(8,128)(2,1)S(1)}, bf16[128,2048]{1,0:T(8,128)(2,1)S(1)}, u32[]{:S(2)}, u32[]{:S(2)}) %collective-permute-start.55) | collective-permute-done | bytes 524320 | tf_op jit(solution)/shard_map/ppermute | solution.py:76
  264.0 6.2 %collective-permute-done.53 = bf16[128,2048]{1,0:T(8,128)(2,1)S(1)} collective-permute-done((bf16[128,2048]{1,0:T(8,128)(2,1)S(1)}, bf16[128,2048]{1,0:T(8,128)(2,1)S(1)}, u32[]{:S(2)}, u32[]{:S(2)}) %collective-permute-start.53) | collective-permute-done | bytes 524320 | tf_op jit(solution)/shard_map/ppermute | solution.py:76
  270.2 2.4 fusion.91
  278.5 6.5 %collective-permute-done.57 = bf16[128,2048]{1,0:T(8,128)(2,1)S(1)} collective-permute-done((bf16[128,2048]{1,0:T(8,128)(2,1)S(1)}, bf16[128,2048]{1,0:T(8,128)(2,1)S(1)}, u32[]{:S(2)}, u32[]{:S(2)}) %collective-permute-start.57) | collective-permute-done | bytes 524320 | tf_op jit(solution)/shard_map/ppermute | solution.py:76
  288.4 8.8 %collective-permute-done.60 = bf16[128,2048]{1,0:T(8,128)(2,1)} collective-permute-done((bf16[128,2048]{1,0:T(8,128)(2,1)}, bf16[128,2048]{1,0:T(8,128)(2,1)}, u32[]{:S(2)}, u32[]{:S(2)}) %collective-permute-start.60) | collective-permute-done | bytes 524320 | tf_op jit(solution)/shard_map/ppermute | solution.py:76
  297.3 3.2 multiply_reduce_fusion.4
  302.8 5.5 collective-permute-start.64
  314.1 2.6 collective-permute-done.64
  319.5 4.0 fusion.114
  329.9 2.6 multiply_convert_fusion.1
  332.6 3.7 fusion.117
  338.6 2.3 collective-permute-done.71
  343.0 2.7 multiply_convert_fusion.3
  345.7 4.1 fusion.116
  358.9 3.9 collective-permute-done.74
  362.8 2.6 multiply_convert_fusion.5
  365.4 2.4 fusion.115
  377.2 4.9 shard_map.246
  391.0 4.9 shard_map.247
  395.9 5.3 collective-permute-done.81
  411.4 4.9 shard_map.248
  416.3 2.4 collective-permute-done.92
  428.1 5.6 shard_map.249
  435.5 3.9 collective-permute-done.99
  448.0 4.1 collective-permute-start.102
  452.1 6.9 %shard_map.250 = (bf16[2,1,256,2048]{3,2,1,0:T(8,128)(2,1)S(1)}, bf16[2,1,256,2048]{3,2,1,0:T(8,128)(2,1)}) custom-call(s32[3]{0:T(128)S(1)} %pad_add_fusion.1.spots, bf16[256,1024]{1,0:T(8,128)(2,1)S(1)} %copy-done.48, bf16[256,1024]{1,0:T(8,128)(2,1)S(1)} %copy-done.42, bf16[256,1024]{1,0:T(8,128)(2,1)S(1)} %copy-done.44, ...), custom_call_target="tpu_custom_call" | custom-call | flops 4294967296 | bytes 10485760 | tf_op jit(solution)/shard_map/pallas_call | solution.py:285
  466.5 2.2 fusion.40
  468.9 9.4 %collective-permute-done.108 = bf16[2,64,2048]{2,1,0:T(8,128)(2,1)S(1)} collective-permute-done((bf16[2,64,2048]{2,1,0:T(8,128)(2,1)S(1)}, bf16[2,64,2048]{2,1,0:T(8,128)(2,1)S(1)}, u32[]{:S(2)}, u32[]{:S(2)}) %collective-permute-start.108) | collective-permute-done | bytes 524320 | tf_op jit(solution)/shard_map/ppermute | solution.py:80
  483.8 9.6 %shard_map.251 = (bf16[512,256]{1,0:T(8,128)(2,1)S(1)}, bf16[512,256]{1,0:T(8,128)(2,1)S(1)}, f32[1024,256]{1,0:T(8,128)S(1)}, f32[1024,256]{1,0:T(8,128)S(1)}) custom-call(bf16[512,256]{1,0:T(8,128)(2,1)S(1)} %copy-done.102, bf16[512,256]{1,0:T(8,128)(2,1)S(1)} %pad_maximum_fusion.17.g_ref, bf16[1024,128]{1,0:T(8,128)(2,1)S(1)} %copy-done.98, ...), custom_call_target="tpu_custom_call" | custom-call | flops 5368709120 | bytes 5242880 | tf_op jit(solution)/shard_map/pallas_call | solution.py:515
  494.4 2.5 fusion.38
  498.2 3.1 collective-permute-start.115
  504.0 11.7 %shard_map.252 = (bf16[512,256]{1,0:T(8,128)(2,1)S(1)}, bf16[512,256]{1,0:T(8,128)(2,1)S(1)}, bf16[1024,128]{1,0:T(8,128)(2,1)S(1)}, bf16[1024,128]{1,0:T(8,128)(2,1)S(1)}) custom-call(bf16[512,256]{1,0:T(8,128)(2,1)S(1)} %copy-done.96, bf16[512,256]{1,0:T(8,128)(2,1)S(1)} %pad_maximum_fusion.18.g_ref, bf16[1024,128]{1,0:T(8,128)(2,1)S(1)} %copy-done.98, ...), custom_call_target="tpu_custom_call" | custom-call | flops 5368709120 | bytes 5242880 | tf_op jit(solution)/shard_map/pallas_call | solution.py:515
  520.4 3.0 collective-permute-start.118
  529.5 5.7 shard_map.254
  539.5 3.0 fusion
  542.6 11.1 %collective-permute-done.121 = bf16[128,2048]{1,0:T(8,128)(2,1)S(1)} collective-permute-done((bf16[128,2048]{1,0:T(8,128)(2,1)S(1)}, bf16[128,2048]{1,0:T(8,128)(2,1)S(1)}, u32[]{:S(2)}, u32[]{:S(2)}) %collective-permute-start.121) | collective-permute-done | bytes 524320 | tf_op jit(solution)/shard_map/ppermute | solution.py:76
  566.9 4.9 shard_map.255
  581.4 9.0 %collective-permute-done.129 = bf16[128,2048]{1,0:T(8,128)(2,1)S(1)} collective-permute-done((bf16[128,2048]{1,0:T(8,128)(2,1)S(1)}, bf16[128,2048]{1,0:T(8,128)(2,1)S(1)}, u32[]{:S(2)}, u32[]{:S(2)}) %collective-permute-start.129) | collective-permute-done | bytes 524320 | tf_op jit(solution)/shard_map/ppermute | solution.py:76
  591.2 3.8 collective-permute-start.132
  598.1 2.8 collective-permute-done.132
  601.7 2.9 shard_map.256
  (860 shorter events, 250.9 us)
Async XLA Ops:
  0.7 20.4 %collective-permute-start = (bf16[128,2048]{1,0:T(8,128)(2,1)}, bf16[128,2048]{1,0:T(8,128)(2,1)S(1)}, u32[]{:S(2)}, u32[]{:S(2)}) collective-permute-start(bf16[128,2048]{1,0:T(8,128)(2,1)} %bitcast.277), channel_id=1, source_target_pairs={{0,4},{4,0},{8,12},{12,8},{16,20},{20,16},{24,28},{28,24},{1,5},{5... | collective-permute-start | bytes 1572872 | tf_op jit(solution)/shard_map/ppermute | solution.py:76
  3.7 17.4 %collective-permute-start.1 = (bf16[128,2048]{1,0:T(8,128)(2,1)}, bf16[128,2048]{1,0:T(8,128)(2,1)}, u32[]{:S(2)}, u32[]{:S(2)}) collective-permute-start(bf16[128,2048]{1,0:T(8,128)(2,1)} %bitcast.278), channel_id=1, source_target_pairs={{0,8},{4,12},{8,16},{12,20},{16,24},{20,28},{24,0},{28,4},{1,9},{5... | collective-permute-start | bytes 1572872 | tf_op jit(solution)/shard_map/ppermute | solution.py:76
  21.1 26.1 %collective-permute-start.4 = (bf16[128,2048]{1,0:T(8,128)(2,1)}, bf16[128,2048]{1,0:T(8,128)(2,1)}, u32[]{:S(2)}, u32[]{:S(2)}) collective-permute-start(bf16[128,2048]{1,0:T(8,128)(2,1)} %collective-permute-done.1), channel_id=1, source_target_pairs={{0,4},{4,0},{8,12},{12,8},{16,20},{20,16},{24,28},{28,24},{1,5},{5... | collective-permute-start | bytes 1572872 | tf_op jit(solution)/shard_map/ppermute | solution.py:76
  22.9 24.3 %collective-permute-start.5 = (bf16[128,2048]{1,0:T(8,128)(2,1)}, bf16[128,2048]{1,0:T(8,128)(2,1)}, u32[]{:S(2)}, u32[]{:S(2)}) collective-permute-start(bf16[128,2048]{1,0:T(8,128)(2,1)} %collective-permute-done.1), channel_id=1, source_target_pairs={{0,8},{4,12},{8,16},{12,20},{16,24},{20,28},{24,0},{28,4},{1,9},{5... | collective-permute-start | bytes 1572872 | tf_op jit(solution)/shard_map/ppermute | solution.py:76
  26.3 16.0 %collective-permute-start.7 = (bf16[2,80,384]{2,1,0:T(8,128)(2,1)}, bf16[2,80,384]{2,1,0:T(8,128)(2,1)S(1)}, u32[]{:S(2)}, u32[]{:S(2)}) collective-permute-start(bf16[2,80,384]{2,1,0:T(8,128)(2,1)} %get-tuple-element.691), channel_id=1, source_target_pairs={{0,8},{4,12},{8,16},{12,20},{16,24},{20,28},{24,0},{28,4},{1,9},{5... | collective-permute-start | bytes 368648 | tf_op jit(solution)/shard_map/ppermute | solution.py:76
  29.0 16.6 %collective-permute-start.8 = (bf16[2,80,384]{2,1,0:T(8,128)(2,1)}, bf16[2,80,384]{2,1,0:T(8,128)(2,1)S(1)}, u32[]{:S(2)}, u32[]{:S(2)}) collective-permute-start(bf16[2,80,384]{2,1,0:T(8,128)(2,1)} %get-tuple-element.690), channel_id=1, source_target_pairs={{0,16},{4,20},{8,24},{12,28},{16,0},{20,4},{24,8},{28,12},{1,17},{... | collective-permute-start | bytes 368648 | tf_op jit(solution)/shard_map/ppermute | solution.py:76
  30.3 17.0 %collective-permute-start.6 = (bf16[64,2048]{1,0:T(8,128)(2,1)S(1)}, bf16[64,2048]{1,0:T(8,128)(2,1)S(1)}, u32[]{:S(2)}, u32[]{:S(2)}) collective-permute-start(bf16[64,2048]{1,0:T(8,128)(2,1)S(1)} %copy-done.72), channel_id=1, source_target_pairs={{0,2},{1,3},{2,0},{3,1},{4,6},{5,7},{6,4},{7,5},{8,10},{9,11},{10,... | collective-permute-start | bytes 786440 | tf_op jit(solution)/shard_map/ppermute | solution.py:80
  62.7 19.2 %collective-permute-start.17 = (bf16[128,2048]{1,0:T(8,128)(2,1)}, bf16[128,2048]{1,0:T(8,128)(2,1)}, u32[]{:S(2)}, u32[]{:S(2)}) collective-permute-start(bf16[128,2048]{1,0:T(8,128)(2,1)} %collective-permute-done.11), channel_id=1, source_target_pairs={{0,4},{4,0},{8,12},{12,8},{16,20},{20,16},{24,28},{28,24},{1,5},{5... | collective-permute-start | bytes 1572872 | tf_op jit(solution)/shard_map/ppermute | solution.py:76
  64.2 17.6 %collective-permute-start.18 = (bf16[128,2048]{1,0:T(8,128)(2,1)}, bf16[128,2048]{1,0:T(8,128)(2,1)}, u32[]{:S(2)}, u32[]{:S(2)}) collective-permute-start(bf16[128,2048]{1,0:T(8,128)(2,1)} %get-tuple-element.342), channel_id=1, source_target_pairs={{0,2},{1,3},{2,0},{3,1},{4,6},{5,7},{6,4},{7,5},{8,10},{9,11},{10,... | collective-permute-start | bytes 1572872 | tf_op jit(solution)/shard_map/ppermute | solution.py:80
  70.7 24.7 %collective-permute-start.19 = (bf16[64,2048]{1,0:T(8,128)(2,1)}, bf16[64,2048]{1,0:T(8,128)(2,1)}, u32[]{:S(2)}, u32[]{:S(2)}) collective-permute-start(bf16[64,2048]{1,0:T(8,128)(2,1)} %get-tuple-element.672), channel_id=1, source_target_pairs={{0,8},{4,12},{8,16},{12,20},{16,24},{20,28},{24,0},{28,4},{1,9},{5... | collective-permute-start | bytes 786440 | tf_op jit(solution)/shard_map/ppermute | solution.py:76
  70.7 25.4 %collective-permute-start.20 = (bf16[64,2048]{1,0:T(8,128)(2,1)}, bf16[64,2048]{1,0:T(8,128)(2,1)}, u32[]{:S(2)}, u32[]{:S(2)}) collective-permute-start(bf16[64,2048]{1,0:T(8,128)(2,1)} %get-tuple-element.671), channel_id=1, source_target_pairs={{0,24},{4,28},{8,0},{12,4},{16,8},{20,12},{24,16},{28,20},{1,25},{... | collective-permute-start | bytes 786440 | tf_op jit(solution)/shard_map/ppermute | solution.py:76
  74.5 23.2 %collective-permute-start.21 = (bf16[64,2048]{1,0:T(8,128)(2,1)}, bf16[64,2048]{1,0:T(8,128)(2,1)}, u32[]{:S(2)}, u32[]{:S(2)}) collective-permute-start(bf16[64,2048]{1,0:T(8,128)(2,1)} %get-tuple-element.670), channel_id=1, source_target_pairs={{0,16},{4,20},{8,24},{12,28},{16,0},{20,4},{24,8},{28,12},{1,17},{... | collective-permute-start | bytes 786440 | tf_op jit(solution)/shard_map/ppermute | solution.py:76
  93.8 24.0 %collective-permute-start.22 = (bf16[128,2048]{1,0:T(8,128)(2,1)S(1)}, bf16[128,2048]{1,0:T(8,128)(2,1)S(1)}, u32[]{:S(2)}, u32[]{:S(2)}) collective-permute-start(bf16[128,2048]{1,0:T(8,128)(2,1)S(1)} %slice.860), channel_id=1, source_target_pairs={{0,4},{4,0},{8,12},{12,8},{16,20},{20,16},{24,28},{28,24},{1,5},{5... | collective-permute-start | bytes 1572872 | tf_op jit(solution)/shard_map/ppermute | solution.py:76
  94.7 23.1 %collective-permute-start.23 = (bf16[256,2048]{1,0:T(8,128)(2,1)S(1)}, bf16[256,2048]{1,0:T(8,128)(2,1)S(1)}, u32[]{:S(2)}, u32[]{:S(2)}) collective-permute-start(bf16[256,2048]{1,0:T(8,128)(2,1)S(1)} %copy-done.16), channel_id=1, source_target_pairs={{0,1},{1,0},{2,3},{3,2},{4,5},{5,4},{6,7},{7,6},{8,9},{9,8},{10,11... | collective-permute-start | bytes 3145736 | tf_op jit(solution)/shard_map/ppermute | solution.py:80
  95.4 22.3 %collective-permute-start.24 = (bf16[64,2048]{1,0:T(8,128)(2,1)S(1)}, bf16[64,2048]{1,0:T(8,128)(2,1)S(1)}, u32[]{:S(2)}, u32[]{:S(2)}) collective-permute-start(bf16[64,2048]{1,0:T(8,128)(2,1)S(1)} %get-tuple-element.669), channel_id=1, source_target_pairs={{0,4},{4,0},{8,12},{12,8},{16,20},{20,16},{24,28},{28,24},{1,5},{5... | collective-permute-start | bytes 786440 | tf_op jit(solution)/shard_map/ppermute | solution.py:76
  96.1 21.6 %collective-permute-start.25 = (bf16[64,2048]{1,0:T(8,128)(2,1)S(1)}, bf16[64,2048]{1,0:T(8,128)(2,1)S(1)}, u32[]{:S(2)}, u32[]{:S(2)}) collective-permute-start(bf16[64,2048]{1,0:T(8,128)(2,1)S(1)} %get-tuple-element.668), channel_id=1, source_target_pairs={{0,12},{4,8},{8,20},{12,16},{16,28},{20,24},{24,4},{28,0},{1,13},{... | collective-permute-start | bytes 786440 | tf_op jit(solution)/shard_map/ppermute | solution.py:76
  98.8 19.0 %collective-permute-start.26 = (bf16[2,64,2048]{2,1,0:T(8,128)(2,1)S(1)}, bf16[2,64,2048]{2,1,0:T(8,128)(2,1)S(1)}, u32[]{:S(2)}, u32[]{:S(2)}) collective-permute-start(bf16[2,64,2048]{2,1,0:T(8,128)(2,1)S(1)} %pad_maximum_fusion.10.refs_0_), channel_id=1, source_target_pairs={{0,2},{1,3},{2,0},{3,1},{4,6},{5,7},{6,4},{7,5},{8,10},{9,11},{10,... | collective-permute-start | bytes 1572872 | tf_op jit(solution)/shard_map/ppermute | solution.py:80
  117.8 20.9 %collective-permute-start.27 = (bf16[128,2048]{1,0:T(8,128)(2,1)S(1)}, bf16[128,2048]{1,0:T(8,128)(2,1)S(1)}, u32[]{:S(2)}, u32[]{:S(2)}) collective-permute-start(bf16[128,2048]{1,0:T(8,128)(2,1)S(1)} %slice.861), channel_id=1, source_target_pairs={{0,4},{4,0},{8,12},{12,8},{16,20},{20,16},{24,28},{28,24},{1,5},{5... | collective-permute-start | bytes 1572872 | tf_op jit(solution)/shard_map/ppermute | solution.py:76
  120.6 18.1 %collective-permute-start.28 = (bf16[128,2048]{1,0:T(8,128)(2,1)S(1)}, bf16[128,2048]{1,0:T(8,128)(2,1)S(1)}, u32[]{:S(2)}, u32[]{:S(2)}) collective-permute-start(bf16[128,2048]{1,0:T(8,128)(2,1)S(1)} %fusion.19), channel_id=1, source_target_pairs={{0,8},{4,12},{8,16},{12,20},{16,24},{20,28},{24,0},{28,4},{1,9},{5... | collective-permute-start | bytes 1572872 | tf_op jit(solution)/shard_map/ppermute | solution.py:76
  122.1 16.6 %collective-permute-start.30 = (bf16[2,64,2048]{2,1,0:T(8,128)(2,1)S(1)}, bf16[2,64,2048]{2,1,0:T(8,128)(2,1)S(1)}, u32[]{:S(2)}, u32[]{:S(2)}) collective-permute-start(bf16[2,64,2048]{2,1,0:T(8,128)(2,1)S(1)} %pad_maximum_fusion.10.refs_0_), channel_id=1, source_target_pairs={{0,1},{1,0},{2,3},{3,2},{4,5},{5,4},{6,7},{7,6},{8,9},{9,8},{10,11... | collective-permute-start | bytes 1572872 | tf_op jit(solution)/shard_map/ppermute | solution.py:80
  138.7 25.4 %collective-permute-start.33 = (bf16[128,2048]{1,0:T(8,128)(2,1)S(1)}, bf16[128,2048]{1,0:T(8,128)(2,1)S(1)}, u32[]{:S(2)}, u32[]{:S(2)}) collective-permute-start(bf16[128,2048]{1,0:T(8,128)(2,1)S(1)} %slice.862), channel_id=1, source_target_pairs={{0,4},{4,0},{8,12},{12,8},{16,20},{20,16},{24,28},{28,24},{1,5},{5... | collective-permute-start | bytes 1572872 | tf_op jit(solution)/shard_map/ppermute | solution.py:76
  139.4 24.6 %collective-permute-start.38 = (bf16[2,64,2048]{2,1,0:T(8,128)(2,1)S(1)}, bf16[2,64,2048]{2,1,0:T(8,128)(2,1)S(1)}, u32[]{:S(2)}, u32[]{:S(2)}) collective-permute-start(bf16[2,64,2048]{2,1,0:T(8,128)(2,1)S(1)} %pad_maximum_fusion.12.refs_8_), channel_id=1, source_target_pairs={{0,2},{1,3},{2,0},{3,1},{4,6},{5,7},{6,4},{7,5},{8,10},{9,11},{10,... | collective-permute-start | bytes 1572872 | tf_op jit(solution)/shard_map/ppermute | solution.py:80
  140.8 22.6 %collective-permute-start.35 = (bf16[64,2048]{1,0:T(8,128)(2,1)S(1)}, bf16[64,2048]{1,0:T(8,128)(2,1)S(1)}, u32[]{:S(2)}, u32[]{:S(2)}) collective-permute-start(bf16[64,2048]{1,0:T(8,128)(2,1)S(1)} %slice_bitcast_fusion.2), channel_id=1, source_target_pairs={{0,20},{4,16},{8,28},{12,24},{16,4},{20,0},{24,12},{28,8},{1,21},{... | collective-permute-start | bytes 786440 | tf_op jit(solution)/shard_map/ppermute | solution.py:76
  141.5 22.5 %collective-permute-start.34 = (bf16[128,2048]{1,0:T(8,128)(2,1)S(1)}, bf16[128,2048]{1,0:T(8,128)(2,1)S(1)}, u32[]{:S(2)}, u32[]{:S(2)}) collective-permute-start(bf16[128,2048]{1,0:T(8,128)(2,1)S(1)} %fusion.18), channel_id=1, source_target_pairs={{0,8},{4,12},{8,16},{12,20},{16,24},{20,28},{24,0},{28,4},{1,9},{5... | collective-permute-start | bytes 1572872 | tf_op jit(solution)/shard_map/ppermute | solution.py:76
  143.1 21.0 %collective-permute-start.36 = (bf16[2,64,2048]{2,1,0:T(8,128)(2,1)S(1)}, bf16[2,64,2048]{2,1,0:T(8,128)(2,1)S(1)}, u32[]{:S(2)}, u32[]{:S(2)}) collective-permute-start(bf16[2,64,2048]{2,1,0:T(8,128)(2,1)S(1)} %pad_maximum_fusion.11.refs_4_), channel_id=1, source_target_pairs={{0,1},{1,0},{2,3},{3,2},{4,5},{5,4},{6,7},{7,6},{8,9},{9,8},{10,11... | collective-permute-start | bytes 1572872 | tf_op jit(solution)/shard_map/ppermute | solution.py:80
  165.4 18.0 %collective-permute-start.39 = (bf16[128,2048]{1,0:T(8,128)(2,1)S(1)}, bf16[128,2048]{1,0:T(8,128)(2,1)S(1)}, u32[]{:S(2)}, u32[]{:S(2)}) collective-permute-start(bf16[128,2048]{1,0:T(8,128)(2,1)S(1)} %slice.863), channel_id=1, source_target_pairs={{0,4},{4,0},{8,12},{12,8},{16,20},{20,16},{24,28},{28,24},{1,5},{5... | collective-permute-start | bytes 1572872 | tf_op jit(solution)/shard_map/ppermute | solution.py:76
  168.1 15.3 %collective-permute-start.40 = (bf16[128,2048]{1,0:T(8,128)(2,1)S(1)}, bf16[128,2048]{1,0:T(8,128)(2,1)S(1)}, u32[]{:S(2)}, u32[]{:S(2)}) collective-permute-start(bf16[128,2048]{1,0:T(8,128)(2,1)S(1)} %fusion.17), channel_id=1, source_target_pairs={{0,8},{4,12},{8,16},{12,20},{16,24},{20,28},{24,0},{28,4},{1,9},{5... | collective-permute-start | bytes 1572872 | tf_op jit(solution)/shard_map/ppermute | solution.py:76
  168.2 15.2 %collective-permute-start.41 = (bf16[2,64,2048]{2,1,0:T(8,128)(2,1)S(1)}, bf16[2,64,2048]{2,1,0:T(8,128)(2,1)S(1)}, u32[]{:S(2)}, u32[]{:S(2)}) collective-permute-start(bf16[2,64,2048]{2,1,0:T(8,128)(2,1)S(1)} %pad_maximum_fusion.12.refs_8_), channel_id=1, source_target_pairs={{0,1},{1,0},{2,3},{3,2},{4,5},{5,4},{6,7},{7,6},{8,9},{9,8},{10,11... | collective-permute-start | bytes 1572872 | tf_op jit(solution)/shard_map/ppermute | solution.py:80
  168.3 15.1 %collective-permute-start.42 = (bf16[2,64,2048]{2,1,0:T(8,128)(2,1)S(1)}, bf16[2,64,2048]{2,1,0:T(8,128)(2,1)S(1)}, u32[]{:S(2)}, u32[]{:S(2)}) collective-permute-start(bf16[2,64,2048]{2,1,0:T(8,128)(2,1)S(1)} %collective-permute-done.38.refs_10_), channel_id=1, source_target_pairs={{0,1},{1,0},{2,3},{3,2},{4,5},{5,4},{6,7},{7,6},{8,9},{9,8},{10,11... | collective-permute-start | bytes 1572872 | tf_op jit(solution)/shard_map/ppermute | solution.py:80
  200.7 16.6 %collective-permute-start.49 = (bf16[128,2048]{1,0:T(8,128)(2,1)}, bf16[128,2048]{1,0:T(8,128)(2,1)S(1)}, u32[]{:S(2)}, u32[]{:S(2)}) collective-permute-start(bf16[128,2048]{1,0:T(8,128)(2,1)} %collective-permute-done.45), channel_id=1, source_target_pairs={{0,4},{4,0},{8,12},{12,8},{16,20},{20,16},{24,28},{28,24},{1,5},{5... | collective-permute-start | bytes 1572872 | tf_op jit(solution)/shard_map/ppermute | solution.py:76
  201.8 15.5 %collective-permute-start.50 = (bf16[128,2048]{1,0:T(8,128)(2,1)}, bf16[128,2048]{1,0:T(8,128)(2,1)S(1)}, u32[]{:S(2)}, u32[]{:S(2)}) collective-permute-start(bf16[128,2048]{1,0:T(8,128)(2,1)} %collective-permute-done.45), channel_id=1, source_target_pairs={{0,8},{4,12},{8,16},{12,20},{16,24},{20,28},{24,0},{28,4},{1,9},{5... | collective-permute-start | bytes 1572872 | tf_op jit(solution)/shard_map/ppermute | solution.py:76
  225.0 19.6 %collective-permute-start.51 = (bf16[128,2048]{1,0:T(8,128)(2,1)S(1)}, bf16[128,2048]{1,0:T(8,128)(2,1)S(1)}, u32[]{:S(2)}, u32[]{:S(2)}) collective-permute-start(bf16[128,2048]{1,0:T(8,128)(2,1)S(1)} %collective-permute-done.50), channel_id=1, source_target_pairs={{0,4},{4,0},{8,12},{12,8},{16,20},{20,16},{24,28},{28,24},{1,5},{5... | collective-permute-start | bytes 1572872 | tf_op jit(solution)/shard_map/ppermute | solution.py:76
  226.1 18.5 %collective-permute-start.52 = (bf16[128,2048]{1,0:T(8,128)(2,1)S(1)}, bf16[128,2048]{1,0:T(8,128)(2,1)S(1)}, u32[]{:S(2)}, u32[]{:S(2)}) collective-permute-start(bf16[128,2048]{1,0:T(8,128)(2,1)S(1)} %collective-permute-done.50), channel_id=1, source_target_pairs={{0,8},{4,12},{8,16},{12,20},{16,24},{20,28},{24,0},{28,4},{1,9},{5... | collective-permute-start | bytes 1572872 | tf_op jit(solution)/shard_map/ppermute | solution.py:76
  237.4 17.2 %collective-permute-start.56 = (bf16[128,2048]{1,0:T(8,128)(2,1)S(1)}, bf16[128,2048]{1,0:T(8,128)(2,1)S(1)}, u32[]{:S(2)}, u32[]{:S(2)}) collective-permute-start(bf16[128,2048]{1,0:T(8,128)(2,1)S(1)} %fusion.15), channel_id=1, source_target_pairs={{0,8},{4,12},{8,16},{12,20},{16,24},{20,28},{24,0},{28,4},{1,9},{5... | collective-permute-start | bytes 1572872 | tf_op jit(solution)/shard_map/ppermute | solution.py:76
  249.8 20.4 %collective-permute-start.53 = (bf16[128,2048]{1,0:T(8,128)(2,1)S(1)}, bf16[128,2048]{1,0:T(8,128)(2,1)S(1)}, u32[]{:S(2)}, u32[]{:S(2)}) collective-permute-start(bf16[128,2048]{1,0:T(8,128)(2,1)S(1)} %collective-permute-done.52), channel_id=1, source_target_pairs={{0,4},{4,0},{8,12},{12,8},{16,20},{20,16},{24,28},{28,24},{1,5},{5... | collective-permute-start | bytes 1572872 | tf_op jit(solution)/shard_map/ppermute | solution.py:76
  337.7 15.3 %collective-permute-start.75 = (bf16[128,1024]{1,0:T(8,128)(2,1)S(1)}, bf16[128,1024]{1,0:T(8,128)(2,1)S(1)}, u32[]{:S(2)}, u32[]{:S(2)}) collective-permute-start(bf16[128,1024]{1,0:T(8,128)(2,1)S(1)} %get-tuple-element.676), channel_id=1, source_target_pairs={{0,4},{4,0},{8,12},{12,8},{16,20},{20,16},{24,28},{28,24},{1,5},{5... | collective-permute-start | bytes 786440 | tf_op jit(solution)/shard_map/ppermute | solution.py:76
  340.9 16.8 %collective-permute-start.73 = (bf16[128,1024]{1,0:T(8,128)(2,1)S(1)}, bf16[128,1024]{1,0:T(8,128)(2,1)S(1)}, u32[]{:S(2)}, u32[]{:S(2)}) collective-permute-start(bf16[128,1024]{1,0:T(8,128)(2,1)S(1)} %collective-permute-done.68), channel_id=1, source_target_pairs={{0,4},{4,0},{8,12},{12,8},{16,20},{20,16},{24,28},{28,24},{1,5},{5... | collective-permute-start | bytes 786440 | tf_op jit(solution)/shard_map/ppermute | solution.py:76
  342.1 20.7 %collective-permute-start.74 = (bf16[128,1024]{1,0:T(8,128)(2,1)S(1)}, bf16[128,1024]{1,0:T(8,128)(2,1)}, u32[]{:S(2)}, u32[]{:S(2)}) collective-permute-start(bf16[128,1024]{1,0:T(8,128)(2,1)S(1)} %collective-permute-done.72), channel_id=1, source_target_pairs={{0,4},{4,0},{8,12},{12,8},{16,20},{20,16},{24,28},{28,24},{1,5},{5... | collective-permute-start | bytes 786440 | tf_op jit(solution)/shard_map/ppermute | solution.py:76
  351.8 16.0 %collective-permute-start.83 = (bf16[128,1024]{1,0:T(8,128)(2,1)}, bf16[128,1024]{1,0:T(8,128)(2,1)S(1)}, u32[]{:S(2)}, u32[]{:S(2)}) collective-permute-start(bf16[128,1024]{1,0:T(8,128)(2,1)} %get-tuple-element.436), channel_id=1, source_target_pairs={{0,4},{4,0},{8,12},{12,8},{16,20},{20,16},{24,28},{28,24},{1,5},{5... | collective-permute-start | bytes 786440 | tf_op jit(solution)/shard_map/ppermute | solution.py:76
  382.1 19.1 %collective-permute-start.89 = (bf16[2,2,64,2048]{3,2,1,0:T(8,128)(2,1)S(1)}, bf16[2,2,64,2048]{3,2,1,0:T(8,128)(2,1)S(1)}, u32[]{:S(2)}, u32[]{:S(2)}) collective-permute-start(bf16[2,2,64,2048]{3,2,1,0:T(8,128)(2,1)S(1)} %get-tuple-element.463), channel_id=1, source_target_pairs={{0,1},{1,0},{2,3},{3,2},{4,5},{5,4},{6,7},{7,6},{8,9},{9,8},{10,11... | collective-permute-start | bytes 3145736 | tf_op jit(solution)/shard_map/ppermute | solution.py:80
  384.1 17.1 %collective-permute-start.87 = (bf16[128,1024]{1,0:T(8,128)(2,1)}, bf16[128,1024]{1,0:T(8,128)(2,1)S(1)}, u32[]{:S(2)}, u32[]{:S(2)}) collective-permute-start(bf16[128,1024]{1,0:T(8,128)(2,1)} %get-tuple-element.451), channel_id=1, source_target_pairs={{0,4},{4,0},{8,12},{12,8},{16,20},{20,16},{24,28},{28,24},{1,5},{5... | collective-permute-start | bytes 786440 | tf_op jit(solution)/shard_map/ppermute | solution.py:76
  385.3 15.9 %collective-permute-start.88 = (bf16[128,1024]{1,0:T(8,128)(2,1)S(1)}, bf16[128,1024]{1,0:T(8,128)(2,1)S(1)}, u32[]{:S(2)}, u32[]{:S(2)}) collective-permute-start(bf16[128,1024]{1,0:T(8,128)(2,1)S(1)} %get-tuple-element.663), channel_id=1, source_target_pairs={{0,8},{4,12},{8,16},{12,20},{16,24},{20,28},{24,0},{28,4},{1,9},{5... | collective-permute-start | bytes 786440 | tf_op jit(solution)/shard_map/ppermute | solution.py:76
  405.2 15.9 %collective-permute-start.90 = (bf16[128,2048]{1,0:T(8,128)(2,1)}, bf16[128,2048]{1,0:T(8,128)(2,1)S(1)}, u32[]{:S(2)}, u32[]{:S(2)}) collective-permute-start(bf16[128,2048]{1,0:T(8,128)(2,1)} %get-tuple-element.640), channel_id=1, source_target_pairs={{0,4},{4,0},{8,12},{12,8},{16,20},{20,16},{24,28},{28,24},{1,5},{5... | collective-permute-start | bytes 1572872 | tf_op jit(solution)/shard_map/ppermute | solution.py:76
  406.3 14.9 %collective-permute-start.91 = (bf16[128,2048]{1,0:T(8,128)(2,1)}, bf16[128,2048]{1,0:T(8,128)(2,1)S(1)}, u32[]{:S(2)}, u32[]{:S(2)}) collective-permute-start(bf16[128,2048]{1,0:T(8,128)(2,1)} %get-tuple-element.640), channel_id=1, source_target_pairs={{0,8},{4,12},{8,16},{12,20},{16,24},{20,28},{24,0},{28,4},{1,9},{5... | collective-permute-start | bytes 1572872 | tf_op jit(solution)/shard_map/ppermute | solution.py:76
  421.2 18.3 %collective-permute-start.95 = (bf16[128,2048]{1,0:T(8,128)(2,1)S(1)}, bf16[128,2048]{1,0:T(8,128)(2,1)}, u32[]{:S(2)}, u32[]{:S(2)}) collective-permute-start(bf16[128,2048]{1,0:T(8,128)(2,1)S(1)} %collective-permute-done.91), channel_id=1, source_target_pairs={{0,4},{4,0},{8,12},{12,8},{16,20},{20,16},{24,28},{28,24},{1,5},{5... | collective-permute-start | bytes 1572872 | tf_op jit(solution)/shard_map/ppermute | solution.py:76
  422.1 17.3 %collective-permute-start.96 = (bf16[128,2048]{1,0:T(8,128)(2,1)S(1)}, bf16[128,2048]{1,0:T(8,128)(2,1)}, u32[]{:S(2)}, u32[]{:S(2)}) collective-permute-start(bf16[128,2048]{1,0:T(8,128)(2,1)S(1)} %collective-permute-done.91), channel_id=1, source_target_pairs={{0,8},{4,12},{8,16},{12,20},{16,24},{20,28},{24,0},{28,4},{1,9},{5... | collective-permute-start | bytes 1572872 | tf_op jit(solution)/shard_map/ppermute | solution.py:76
  423.6 15.9 %collective-permute-start.98 = (bf16[2,2,64,2048]{3,2,1,0:T(8,128)(2,1)S(1)}, bf16[2,2,64,2048]{3,2,1,0:T(8,128)(2,1)}, u32[]{:S(2)}, u32[]{:S(2)}) collective-permute-start(bf16[2,2,64,2048]{3,2,1,0:T(8,128)(2,1)S(1)} %get-tuple-element.494), channel_id=1, source_target_pairs={{0,1},{1,0},{2,3},{3,2},{4,5},{5,4},{6,7},{7,6},{8,9},{9,8},{10,11... | collective-permute-start | bytes 3145736 | tf_op jit(solution)/shard_map/ppermute | solution.py:80
  439.5 19.6 %collective-permute-start.100 = (bf16[128,2048]{1,0:T(8,128)(2,1)}, bf16[128,2048]{1,0:T(8,128)(2,1)S(1)}, u32[]{:S(2)}, u32[]{:S(2)}) collective-permute-start(bf16[128,2048]{1,0:T(8,128)(2,1)} %collective-permute-done.96), channel_id=1, source_target_pairs={{0,4},{4,0},{8,12},{12,8},{16,20},{20,16},{24,28},{28,24},{1,5},{5... | collective-permute-start | bytes 1572872 | tf_op jit(solution)/shard_map/ppermute | solution.py:76
  440.7 18.3 %collective-permute-start.101 = (bf16[128,2048]{1,0:T(8,128)(2,1)}, bf16[128,2048]{1,0:T(8,128)(2,1)S(1)}, u32[]{:S(2)}, u32[]{:S(2)}) collective-permute-start(bf16[128,2048]{1,0:T(8,128)(2,1)} %collective-permute-done.96), channel_id=1, source_target_pairs={{0,8},{4,12},{8,16},{12,20},{16,24},{20,28},{24,0},{28,4},{1,9},{5... | collective-permute-start | bytes 1572872 | tf_op jit(solution)/shard_map/ppermute | solution.py:76
  443.0 16.1 %collective-permute-start.104 = (bf16[2,64,2048]{2,1,0:T(8,128)(2,1)S(1)}, bf16[2,64,2048]{2,1,0:T(8,128)(2,1)}, u32[]{:S(2)}, u32[]{:S(2)}) collective-permute-start(bf16[2,64,2048]{2,1,0:T(8,128)(2,1)S(1)} %fusion.28), channel_id=1, source_target_pairs={{0,2},{1,3},{2,0},{3,1},{4,6},{5,7},{6,4},{7,5},{8,10},{9,11},{10,... | collective-permute-start | bytes 1572872 | tf_op jit(solution)/shard_map/ppermute | solution.py:80
  459.1 19.2 %collective-permute-start.106 = (bf16[2,1,256,2048]{3,2,1,0:T(8,128)(2,1)}, bf16[2,1,256,2048]{3,2,1,0:T(8,128)(2,1)S(1)}, u32[]{:S(2)}, u32[]{:S(2)}) collective-permute-start(bf16[2,1,256,2048]{3,2,1,0:T(8,128)(2,1)} %get-tuple-element.516), channel_id=1, source_target_pairs={{0,1},{1,0},{2,3},{3,2},{4,5},{5,4},{6,7},{7,6},{8,9},{9,8},{10,11... | collective-permute-start | bytes 6291464 | tf_op jit(solution)/shard_map/ppermute | solution.py:80
  461.4 16.9 %collective-permute-start.105 = (bf16[128,2048]{1,0:T(8,128)(2,1)S(1)}, bf16[128,2048]{1,0:T(8,128)(2,1)S(1)}, u32[]{:S(2)}, u32[]{:S(2)}) collective-permute-start(bf16[128,2048]{1,0:T(8,128)(2,1)S(1)} %collective-permute-done.101), channel_id=1, source_target_pairs={{0,4},{4,0},{8,12},{12,8},{16,20},{20,16},{24,28},{28,24},{1,5},{5... | collective-permute-start | bytes 1572872 | tf_op jit(solution)/shard_map/ppermute | solution.py:76
  462.3 16.6 %collective-permute-start.110 = (bf16[64,2048]{1,0:T(8,128)(2,1)S(1)}, bf16[64,2048]{1,0:T(8,128)(2,1)S(1)}, u32[]{:S(2)}, u32[]{:S(2)}) collective-permute-start(bf16[64,2048]{1,0:T(8,128)(2,1)S(1)} %get-tuple-element.525), channel_id=1, source_target_pairs={{0,24},{4,28},{8,0},{12,4},{16,8},{20,12},{24,16},{28,20},{1,25},{... | collective-permute-start | bytes 786440 | tf_op jit(solution)/shard_map/ppermute | solution.py:76
  480.8 16.9 %collective-permute-start.113 = (bf16[128,2048]{1,0:T(8,128)(2,1)}, bf16[128,2048]{1,0:T(8,128)(2,1)}, u32[]{:S(2)}, u32[]{:S(2)}) collective-permute-start(bf16[128,2048]{1,0:T(8,128)(2,1)} %get-tuple-element.673), channel_id=1, source_target_pairs={{0,2},{1,3},{2,0},{3,1},{4,6},{5,7},{6,4},{7,5},{8,10},{9,11},{10,... | collective-permute-start | bytes 1572872 | tf_op jit(solution)/shard_map/ppermute | solution.py:80
  497.7 18.1 %collective-permute-start.116 = (bf16[128,2048]{1,0:T(8,128)(2,1)}, bf16[128,2048]{1,0:T(8,128)(2,1)S(1)}, u32[]{:S(2)}, u32[]{:S(2)}) collective-permute-start(bf16[128,2048]{1,0:T(8,128)(2,1)} %get-tuple-element.554), channel_id=1, source_target_pairs={{0,2},{1,3},{2,0},{3,1},{4,6},{5,7},{6,4},{7,5},{8,10},{9,11},{10,... | collective-permute-start | bytes 1572872 | tf_op jit(solution)/shard_map/ppermute | solution.py:80
  498.2 17.6 %collective-permute-start.115 = (bf16[64,2048]{1,0:T(8,128)(2,1)}, bf16[64,2048]{1,0:T(8,128)(2,1)S(1)}, u32[]{:S(2)}, u32[]{:S(2)}) collective-permute-start(bf16[64,2048]{1,0:T(8,128)(2,1)} %get-tuple-element.552), channel_id=1, source_target_pairs={{0,28},{4,24},{8,4},{12,0},{16,12},{20,8},{24,20},{28,16},{1,29},{... | collective-permute-start | bytes 786440 | tf_op jit(solution)/shard_map/ppermute | solution.py:76
  518.1 18.3 %collective-permute-start.117 = (bf16[128,2048]{1,0:T(8,128)(2,1)S(1)}, bf16[128,2048]{1,0:T(8,128)(2,1)S(1)}, u32[]{:S(2)}, u32[]{:S(2)}) collective-permute-start(bf16[128,2048]{1,0:T(8,128)(2,1)S(1)} %slice.855), channel_id=1, source_target_pairs={{0,4},{4,0},{8,12},{12,8},{16,20},{20,16},{24,28},{28,24},{1,5},{5... | collective-permute-start | bytes 1572872 | tf_op jit(solution)/shard_map/ppermute | solution.py:76
  519.3 15.9 %collective-permute-start.119 = (f32[1,2]{1,0:T(1,128)S(1)}, f32[1,2]{1,0:T(1,128)S(1)}, u32[]{:S(2)}, u32[]{:S(2)}) collective-permute-start(f32[1,2]{1,0:T(1,128)S(1)} %add.672), channel_id=1, source_target_pairs={{0,2},{1,3},{2,0},{3,1},{4,6},{5,7},{6,4},{7,5},{8,10},{9,11},{10,... | collective-permute-start | bytes 32 | tf_op jit(solution)/shard_map/ppermute | solution.py:80
  536.4 17.2 %collective-permute-start.123 = (bf16[2,8,64,384]{3,2,1,0:T(8,128)(2,1)S(1)}, bf16[2,8,64,384]{3,2,1,0:T(8,128)(2,1)S(1)}, u32[]{:S(2)}, u32[]{:S(2)}) collective-permute-start(bf16[2,8,64,384]{3,2,1,0:T(8,128)(2,1)S(1)} %get-tuple-element.589), channel_id=1, source_target_pairs={{0,1},{1,0},{2,3},{3,2},{4,5},{5,4},{6,7},{7,6},{8,9},{9,8},{10,11... | collective-permute-start | bytes 2359304 | tf_op jit(solution)/shard_map/ppermute | solution.py:80
  536.6 17.1 %collective-permute-start.120 = (bf16[128,2048]{1,0:T(8,128)(2,1)S(1)}, bf16[128,2048]{1,0:T(8,128)(2,1)S(1)}, u32[]{:S(2)}, u32[]{:S(2)}) collective-permute-start(bf16[128,2048]{1,0:T(8,128)(2,1)S(1)} %slice.852), channel_id=1, source_target_pairs={{0,4},{4,0},{8,12},{12,8},{16,20},{20,16},{24,28},{28,24},{1,5},{5... | collective-permute-start | bytes 1572872 | tf_op jit(solution)/shard_map/ppermute | solution.py:76
  537.8 15.9 %collective-permute-start.121 = (bf16[128,2048]{1,0:T(8,128)(2,1)S(1)}, bf16[128,2048]{1,0:T(8,128)(2,1)S(1)}, u32[]{:S(2)}, u32[]{:S(2)}) collective-permute-start(bf16[128,2048]{1,0:T(8,128)(2,1)S(1)} %fusion.12), channel_id=1, source_target_pairs={{0,8},{4,12},{8,16},{12,20},{16,24},{20,28},{24,0},{28,4},{1,9},{5... | collective-permute-start | bytes 1572872 | tf_op jit(solution)/shard_map/ppermute | solution.py:76
  554.7 17.1 %collective-permute-start.127 = (bf16[8,64,384]{2,1,0:T(8,128)(2,1)}, bf16[8,64,384]{2,1,0:T(8,128)(2,1)}, u32[]{:S(2)}, u32[]{:S(2)}) collective-permute-start(bf16[8,64,384]{2,1,0:T(8,128)(2,1)} %fusion.45), channel_id=1, source_target_pairs={{0,2},{1,3},{2,0},{3,1},{4,6},{5,7},{6,4},{7,5},{8,10},{9,11},{10,... | collective-permute-start | bytes 1179656 | tf_op jit(solution)/shard_map/ppermute | solution.py:80
  556.7 15.7 %collective-permute-start.125 = (bf16[128,2048]{1,0:T(8,128)(2,1)}, bf16[128,2048]{1,0:T(8,128)(2,1)}, u32[]{:S(2)}, u32[]{:S(2)}) collective-permute-start(bf16[128,2048]{1,0:T(8,128)(2,1)} %fusion.11), channel_id=1, source_target_pairs={{0,8},{4,12},{8,16},{12,20},{16,24},{20,28},{24,0},{28,4},{1,9},{5... | collective-permute-start | bytes 1572872 | tf_op jit(solution)/shard_map/ppermute | solution.py:76
  557.0 15.4 %collective-permute-start.124 = (bf16[128,2048]{1,0:T(8,128)(2,1)}, bf16[128,2048]{1,0:T(8,128)(2,1)}, u32[]{:S(2)}, u32[]{:S(2)}) collective-permute-start(bf16[128,2048]{1,0:T(8,128)(2,1)} %slice.853), channel_id=1, source_target_pairs={{0,4},{4,0},{8,12},{12,8},{16,20},{20,16},{24,28},{28,24},{1,5},{5... | collective-permute-start | bytes 1572872 | tf_op jit(solution)/shard_map/ppermute | solution.py:76
  (284 other events, 2543.6 us)

commit v3 on v2

--- a/solution.py
+++ b/solution.py
@@ -295,7 +295,7 @@
         out_shape=[
             jax.ShapeDtypeStruct((m // 2, owners.shape[0], block // m, width), BF)
         ] * 2,
-        compiler_params=pltpu.CompilerParams(vmem_limit_bytes=44 << 20),
+        compiler_params=pltpu.CompilerParams(vmem_limit_bytes=(24 if n > 1 else 44) << 20),
         cost_estimate=pl.CostEstimate(
             flops=2 * count * tokens * owners.shape[0] * block * width,
             bytes_accessed=2 * owners.shape[0] * block * (count * tokens + width)
@@ -495,7 +495,7 @@
         ]
         + [jax.ShapeDtypeStruct((stream, 128), F32)] * first,
         scratch_shapes=[pltpu.VMEM((heads, stream, width), BF)] * 2,
-        compiler_params=pltpu.CompilerParams(vmem_limit_bytes=44 << 20),
+        compiler_params=pltpu.CompilerParams(vmem_limit_bytes=28 << 20),
         cost_estimate=pl.CostEstimate(
             flops=4 * stream * count * heads * 256,
             bytes_accessed=8 * stream * width,
@@ -526,7 +526,7 @@
             *([pltpu.VMEM((heads, stream, width), BF)] * 2),
             *([pltpu.VMEM((stream, width), F32)] * 2),
         ],
-        compiler_params=pltpu.CompilerParams(vmem_limit_bytes=48 << 20),
+        compiler_params=pltpu.CompilerParams(vmem_limit_bytes=32 << 20),
         cost_estimate=pl.CostEstimate(
             flops=10 * stream * count * heads * 256,
             bytes_accessed=20 * stream * width,

time: 618 us -> 615 us (level)
  other arithmetic: 68.3 us -> 57.3 us
  waiting for transfers between devices: 202 us -> 211 us
    ppermute x42, waiting for transfers between devices: 33.8 us -> 43.1 us  [flip(): return lax.ppermute(x, axis, [(i, i ^ bit) for i in range(size)])]
    unnamed x438 -> x380, local copies, waits for them, and re-layouts: 26.3 us -> 28.8 us
  transfers between devices with their start and end apart: 134 -> 134, of which waited for: 46 -> 47; matrix products, arithmetic and copies ran while one was open for 22% -> 21% of each run, Pallas kernels for 16% -> 15%
where the time goes in v3:
time: 615 us; the launch traced here: 605 us
  waiting for transfers between devices  211 us (34%)
  starting transfers between devices  123 us (20%)
  Pallas kernels  94.8 us (15%)
  other arithmetic  57.3 us (9%)
  matrix products  56.6 us (9%)
  local copies, waits for them, and re-layouts  53.7 us (9%)
  between operations  8.14 us (1%)
    ppermute x92, waiting for transfers between devices, shift(): return lax.ppermute(x, 'ctx', perm)  168 us
    ppermute x92, starting transfers between devices, shift(): return lax.ppermute(x, 'ctx', perm)  100 us
    ppermute x42, waiting for transfers between devices, flip(): return lax.ppermute(x, axis, [(i, i ^ bit) for i in range(size)])  43.1 us
    dot_general x16, matrix products, against(): lax.dot_general(left, right, (((1,), (1,)), ((), ())), preferred_element_...  33.9 us
    pallas_call x7, Pallas kernels, term(): pl.pallas_call(functools.partial(term_kernel, count, m), grid_spec=pltpu....  29.4 us
    unnamed x380, local copies, waits for them, and re-layouts  28.8 us
    ppermute x42, starting transfers between devices, flip(): return lax.ppermute(x, axis, [(i, i ^ bit) for i in range(size)])  23.4 us
    dot_general x16, matrix products, mm(): return jnp.dot(left, right, preferred_element_type=F32)  22.7 us
  transfers between devices with their start and end apart: 134, of which 47 were waited for; matrix products, arithmetic and copies ran while one was open for 21% of the time, Pallas kernels for 15%

profile of v3, /device:TPU:0, one launch (start us, length us, event | category | flops | bytes accessed | tf_op | source)
XLA Modules:
  0.0 604.8 jit_solution(13902029700937586569)
XLA Ops:
  0.7 3.0 collective-permute-start
  11.4 2.5 shard_map.238
  16.1 5.0 collective-permute-done.3
  31.7 6.8 %shard_map.242 = bf16[8,64,2048]{2,1,0:T(8,128)(2,1)} custom-call(s32[8]{0:T(128)} %stack.75.spots, bf16[64,8192]{1,0:T(8,128)(2,1)} %refs_8_.1, bf16[64,8192]{1,0:T(8,128)(2,1)} %refs_9_.1, f32[64,1]{1,0:T(8,128)} %copy.51.gain_ref), custom_call_target="tpu_custom_call" | custom-call | tf_op jit(solution)/shard_map/pallas_call | solution.py:251
  38.8 3.4 collective-permute-done.7
  54.9 5.6 collective-permute-done.14.refs_2_
  70.7 3.8 collective-permute-start.20
  85.3 7.6 %shard_map.240 = (bf16[512,256]{1,0:T(8,128)(2,1)S(1)}, f32[512,128]{1,0:T(8,128)S(1)}, bf16[512,256]{1,0:T(8,128)(2,1)S(1)}, bf16[1024,128]{1,0:T(8,128)(2,1)}, f32[1024,128]{1,0:T(8,128)S(1)}) custom-call(f32[1024,384]{1,0:T(8,128)S(1)} %pad_maximum_fusion.act_ref, f32[128,1024]{1,0:T(8,128)S(1)} %concatenate.181.table_ref, ...), custom_call_target="tpu_custom_call" | custom-call | flops 2147483648 | bytes 2097152 | tf_op jit(solution)/shard_map/pallas_call | solution.py:481
  99.4 7.1 %shard_map.243 = (bf16[512,256]{1,0:T(8,128)(2,1)S(1)}, f32[512,128]{1,0:T(8,128)S(1)}, bf16[512,256]{1,0:T(8,128)(2,1)S(1)}, bf16[1024,128]{1,0:T(8,128)(2,1)S(1)}) custom-call(f32[1024,384]{1,0:T(8,128)S(1)} %pad_maximum_fusion.act_ref, f32[128,1024]{1,0:T(8,128)S(1)} %copy-done.58, f32[1024,128]{1,0:T(8,128)S(1)} %get-tuple-element.352.facts_in.facts_ref), custom_call_target="tpu_custom_call" | custom-call | flops 2147483648 | bytes 2097152 | tf_op jit(solution)/shard_map/pallas_call | solution.py:481
  108.4 9.3 %collective-permute-done.24 = bf16[64,2048]{1,0:T(8,128)(2,1)S(1)} collective-permute-done((bf16[64,2048]{1,0:T(8,128)(2,1)S(1)}, bf16[64,2048]{1,0:T(8,128)(2,1)S(1)}, u32[]{:S(2)}, u32[]{:S(2)}) %collective-permute-start.24) | collective-permute-done | bytes 262176 | tf_op jit(solution)/shard_map/ppermute | solution.py:76
  122.1 7.0 %collective-permute-done.29 = bf16[64,2048]{1,0:T(8,128)(2,1)S(1)} collective-permute-done((bf16[64,2048]{1,0:T(8,128)(2,1)S(1)}, bf16[64,2048]{1,0:T(8,128)(2,1)S(1)}, u32[]{:S(2)}, u32[]{:S(2)}) %collective-permute-start.29) | collective-permute-done | bytes 262176 | tf_op jit(solution)/shard_map/ppermute | solution.py:76
  129.9 8.7 %collective-permute-done.28 = bf16[128,2048]{1,0:T(8,128)(2,1)S(1)} collective-permute-done((bf16[128,2048]{1,0:T(8,128)(2,1)S(1)}, bf16[128,2048]{1,0:T(8,128)(2,1)S(1)}, u32[]{:S(2)}, u32[]{:S(2)}) %collective-permute-start.28) | collective-permute-done | bytes 524320 | tf_op jit(solution)/shard_map/ppermute | solution.py:76
  144.7 20.3 %collective-permute-done.35 = bf16[64,2048]{1,0:T(8,128)(2,1)S(1)} collective-permute-done((bf16[64,2048]{1,0:T(8,128)(2,1)S(1)}, bf16[64,2048]{1,0:T(8,128)(2,1)S(1)}, u32[]{:S(2)}, u32[]{:S(2)}) %collective-permute-start.35) | collective-permute-done | bytes 262176 | tf_op jit(solution)/shard_map/ppermute | solution.py:76
  173.8 9.9 %collective-permute-done.43.refs_14_ = bf16[2,64,2048]{2,1,0:T(8,128)(2,1)} collective-permute-done((bf16[2,64,2048]{2,1,0:T(8,128)(2,1)}, bf16[2,64,2048]{2,1,0:T(8,128)(2,1)}, u32[]{:S(2)}, u32[]{:S(2)}) %collective-permute-start.43) | collective-permute-done | bytes 524320 | tf_op jit(solution)/shard_map/ppermute | solution.py:80
  192.9 9.2 %collective-permute-done.44 = bf16[128,2048]{1,0:T(8,128)(2,1)} collective-permute-done((bf16[128,2048]{1,0:T(8,128)(2,1)}, bf16[128,2048]{1,0:T(8,128)(2,1)}, u32[]{:S(2)}, u32[]{:S(2)}) %collective-permute-start.44) | collective-permute-done | bytes 524320 | tf_op jit(solution)/shard_map/ppermute | solution.py:76
  202.1 2.4 collective-permute-done.45
  209.2 5.7 shard_map.245
  215.0 4.6 shard_map.244
  221.2 2.4 fusion.122
  230.6 10.5 %collective-permute-done.54 = bf16[128,2048]{1,0:T(8,128)(2,1)S(1)} collective-permute-done((bf16[128,2048]{1,0:T(8,128)(2,1)S(1)}, bf16[128,2048]{1,0:T(8,128)(2,1)S(1)}, u32[]{:S(2)}, u32[]{:S(2)}) %collective-permute-start.54) | collective-permute-done | bytes 524320 | tf_op jit(solution)/shard_map/ppermute | solution.py:76
  241.3 7.2 %collective-permute-done.51 = bf16[128,2048]{1,0:T(8,128)(2,1)S(1)} collective-permute-done((bf16[128,2048]{1,0:T(8,128)(2,1)S(1)}, bf16[128,2048]{1,0:T(8,128)(2,1)S(1)}, u32[]{:S(2)}, u32[]{:S(2)}) %collective-permute-start.51) | collective-permute-done | bytes 524320 | tf_op jit(solution)/shard_map/ppermute | solution.py:76
  248.5 2.4 fusion.120
  254.8 3.6 fusion.92
  258.4 9.2 %collective-permute-done.55 = bf16[128,2048]{1,0:T(8,128)(2,1)S(1)} collective-permute-done((bf16[128,2048]{1,0:T(8,128)(2,1)S(1)}, bf16[128,2048]{1,0:T(8,128)(2,1)S(1)}, u32[]{:S(2)}, u32[]{:S(2)}) %collective-permute-start.55) | collective-permute-done | bytes 524320 | tf_op jit(solution)/shard_map/ppermute | solution.py:76
  267.9 6.2 %collective-permute-done.53 = bf16[128,2048]{1,0:T(8,128)(2,1)S(1)} collective-permute-done((bf16[128,2048]{1,0:T(8,128)(2,1)S(1)}, bf16[128,2048]{1,0:T(8,128)(2,1)S(1)}, u32[]{:S(2)}, u32[]{:S(2)}) %collective-permute-start.53) | collective-permute-done | bytes 524320 | tf_op jit(solution)/shard_map/ppermute | solution.py:76
  274.1 2.4 fusion.91
  282.3 5.1 collective-permute-done.57
  288.5 2.5 collective-permute-start.60
  294.4 6.5 %collective-permute-done.60 = bf16[128,2048]{1,0:T(8,128)(2,1)} collective-permute-done((bf16[128,2048]{1,0:T(8,128)(2,1)}, bf16[128,2048]{1,0:T(8,128)(2,1)}, u32[]{:S(2)}, u32[]{:S(2)}) %collective-permute-start.60) | collective-permute-done | bytes 524320 | tf_op jit(solution)/shard_map/ppermute | solution.py:76
  300.9 3.2 multiply_reduce_fusion.4
  306.6 4.6 collective-permute-start.64
  314.1 2.2 collective-permute-done.62
  317.8 4.2 collective-permute-done.64
  323.8 4.1 fusion.114
  335.0 2.7 multiply_convert_fusion.1
  337.7 4.1 fusion.117
  348.4 3.6 multiply_convert_fusion.3
  352.0 5.2 fusion.116
  359.6 2.3 fusion.35
  361.9 2.8 collective-permute-start.84
  367.4 3.8 multiply_convert_fusion.5
  371.2 3.7 fusion.115
  382.3 3.7 shard_map.246
  395.5 3.7 shard_map.247
  399.2 7.8 %collective-permute-done.81 = bf16[128,1024]{1,0:T(8,128)(2,1)S(1)} collective-permute-done((bf16[128,1024]{1,0:T(8,128)(2,1)S(1)}, bf16[128,1024]{1,0:T(8,128)(2,1)S(1)}, u32[]{:S(2)}, u32[]{:S(2)}) %collective-permute-start.81) | collective-permute-done | bytes 262176 | tf_op jit(solution)/shard_map/ppermute | solution.py:76
  412.9 3.7 shard_map.248
  416.6 6.0 collective-permute-done.92
  428.6 3.7 shard_map.249
  432.5 4.7 collective-permute-done.97
  437.2 4.9 collective-permute-done.99
  447.3 3.4 collective-permute-start.102
  450.8 6.9 %shard_map.250 = (bf16[2,1,256,2048]{3,2,1,0:T(8,128)(2,1)S(1)}, bf16[2,1,256,2048]{3,2,1,0:T(8,128)(2,1)}) custom-call(s32[3]{0:T(128)S(1)} %pad_add_fusion.1.spots, bf16[256,1024]{1,0:T(8,128)(2,1)S(1)} %copy-done.38, bf16[256,1024]{1,0:T(8,128)(2,1)S(1)} %copy-done.32, bf16[256,1024]{1,0:T(8,128)(2,1)S(1)} %copy-done.34, ...), custom_call_target="tpu_custom_call" | custom-call | flops 4294967296 | bytes 10485760 | tf_op jit(solution)/shard_map/pallas_call | solution.py:285
  462.0 2.7 collective-permute-start.110
  470.5 9.3 %collective-permute-done.108 = bf16[2,64,2048]{2,1,0:T(8,128)(2,1)S(1)} collective-permute-done((bf16[2,64,2048]{2,1,0:T(8,128)(2,1)S(1)}, bf16[2,64,2048]{2,1,0:T(8,128)(2,1)S(1)}, u32[]{:S(2)}, u32[]{:S(2)}) %collective-permute-start.108) | collective-permute-done | bytes 524320 | tf_op jit(solution)/shard_map/ppermute | solution.py:80
  484.0 9.6 %shard_map.251 = (bf16[512,256]{1,0:T(8,128)(2,1)S(1)}, bf16[512,256]{1,0:T(8,128)(2,1)S(1)}, f32[1024,256]{1,0:T(8,128)S(1)}, f32[1024,256]{1,0:T(8,128)S(1)}) custom-call(bf16[512,256]{1,0:T(8,128)(2,1)S(1)} %copy-done.89, bf16[512,256]{1,0:T(8,128)(2,1)S(1)} %pad_maximum_fusion.17.g_ref, bf16[1024,128]{1,0:T(8,128)(2,1)S(1)} %copy-done.85, ...), custom_call_target="tpu_custom_call" | custom-call | flops 5368709120 | bytes 5242880 | tf_op jit(solution)/shard_map/pallas_call | solution.py:515
  497.1 3.3 collective-permute-start.115
  500.6 11.7 %shard_map.252 = (bf16[512,256]{1,0:T(8,128)(2,1)S(1)}, bf16[512,256]{1,0:T(8,128)(2,1)S(1)}, bf16[1024,128]{1,0:T(8,128)(2,1)S(1)}, bf16[1024,128]{1,0:T(8,128)(2,1)S(1)}) custom-call(bf16[512,256]{1,0:T(8,128)(2,1)S(1)} %copy-done.83, bf16[512,256]{1,0:T(8,128)(2,1)S(1)} %pad_maximum_fusion.18.g_ref, bf16[1024,128]{1,0:T(8,128)(2,1)S(1)} %copy-done.85, ...), custom_call_target="tpu_custom_call" | custom-call | flops 5368709120 | bytes 5242880 | tf_op jit(solution)/shard_map/pallas_call | solution.py:515
  526.2 5.7 shard_map.254
  539.2 12.1 %collective-permute-done.121 = bf16[128,2048]{1,0:T(8,128)(2,1)S(1)} collective-permute-done((bf16[128,2048]{1,0:T(8,128)(2,1)S(1)}, bf16[128,2048]{1,0:T(8,128)(2,1)S(1)}, u32[]{:S(2)}, u32[]{:S(2)}) %collective-permute-start.121) | collective-permute-done | bytes 524320 | tf_op jit(solution)/shard_map/ppermute | solution.py:76
  564.0 4.9 shard_map.255
  579.3 8.5 %collective-permute-done.129 = bf16[128,2048]{1,0:T(8,128)(2,1)S(1)} collective-permute-done((bf16[128,2048]{1,0:T(8,128)(2,1)S(1)}, bf16[128,2048]{1,0:T(8,128)(2,1)S(1)}, u32[]{:S(2)}, u32[]{:S(2)}) %collective-permute-start.129) | collective-permute-done | bytes 524320 | tf_op jit(solution)/shard_map/ppermute | solution.py:76
  588.8 3.4 collective-permute-start.132
  595.5 2.6 collective-permute-done.132
  598.9 2.9 shard_map.256
  (802 shorter events, 244.9 us)
Async XLA Ops:
  0.7 20.4 %collective-permute-start = (bf16[128,2048]{1,0:T(8,128)(2,1)}, bf16[128,2048]{1,0:T(8,128)(2,1)S(1)}, u32[]{:S(2)}, u32[]{:S(2)}) collective-permute-start(bf16[128,2048]{1,0:T(8,128)(2,1)} %bitcast.277), channel_id=1, source_target_pairs={{0,4},{4,0},{8,12},{12,8},{16,20},{20,16},{24,28},{28,24},{1,5},{5... | collective-permute-start | bytes 1572872 | tf_op jit(solution)/shard_map/ppermute | solution.py:76
  3.7 17.4 %collective-permute-start.1 = (bf16[128,2048]{1,0:T(8,128)(2,1)}, bf16[128,2048]{1,0:T(8,128)(2,1)}, u32[]{:S(2)}, u32[]{:S(2)}) collective-permute-start(bf16[128,2048]{1,0:T(8,128)(2,1)} %bitcast.278), channel_id=1, source_target_pairs={{0,8},{4,12},{8,16},{12,20},{16,24},{20,28},{24,0},{28,4},{1,9},{5... | collective-permute-start | bytes 1572872 | tf_op jit(solution)/shard_map/ppermute | solution.py:76
  21.1 26.1 %collective-permute-start.4 = (bf16[128,2048]{1,0:T(8,128)(2,1)}, bf16[128,2048]{1,0:T(8,128)(2,1)}, u32[]{:S(2)}, u32[]{:S(2)}) collective-permute-start(bf16[128,2048]{1,0:T(8,128)(2,1)} %collective-permute-done.1), channel_id=1, source_target_pairs={{0,4},{4,0},{8,12},{12,8},{16,20},{20,16},{24,28},{28,24},{1,5},{5... | collective-permute-start | bytes 1572872 | tf_op jit(solution)/shard_map/ppermute | solution.py:76
  22.9 24.3 %collective-permute-start.5 = (bf16[128,2048]{1,0:T(8,128)(2,1)}, bf16[128,2048]{1,0:T(8,128)(2,1)}, u32[]{:S(2)}, u32[]{:S(2)}) collective-permute-start(bf16[128,2048]{1,0:T(8,128)(2,1)} %collective-permute-done.1), channel_id=1, source_target_pairs={{0,8},{4,12},{8,16},{12,20},{16,24},{20,28},{24,0},{28,4},{1,9},{5... | collective-permute-start | bytes 1572872 | tf_op jit(solution)/shard_map/ppermute | solution.py:76
  26.3 16.0 %collective-permute-start.7 = (bf16[2,80,384]{2,1,0:T(8,128)(2,1)}, bf16[2,80,384]{2,1,0:T(8,128)(2,1)S(1)}, u32[]{:S(2)}, u32[]{:S(2)}) collective-permute-start(bf16[2,80,384]{2,1,0:T(8,128)(2,1)} %get-tuple-element.691), channel_id=1, source_target_pairs={{0,8},{4,12},{8,16},{12,20},{16,24},{20,28},{24,0},{28,4},{1,9},{5... | collective-permute-start | bytes 368648 | tf_op jit(solution)/shard_map/ppermute | solution.py:76
  29.0 16.6 %collective-permute-start.8 = (bf16[2,80,384]{2,1,0:T(8,128)(2,1)}, bf16[2,80,384]{2,1,0:T(8,128)(2,1)S(1)}, u32[]{:S(2)}, u32[]{:S(2)}) collective-permute-start(bf16[2,80,384]{2,1,0:T(8,128)(2,1)} %get-tuple-element.690), channel_id=1, source_target_pairs={{0,16},{4,20},{8,24},{12,28},{16,0},{20,4},{24,8},{28,12},{1,17},{... | collective-permute-start | bytes 368648 | tf_op jit(solution)/shard_map/ppermute | solution.py:76
  30.3 17.0 %collective-permute-start.6 = (bf16[64,2048]{1,0:T(8,128)(2,1)S(1)}, bf16[64,2048]{1,0:T(8,128)(2,1)S(1)}, u32[]{:S(2)}, u32[]{:S(2)}) collective-permute-start(bf16[64,2048]{1,0:T(8,128)(2,1)S(1)} %copy-done.62), channel_id=1, source_target_pairs={{0,2},{1,3},{2,0},{3,1},{4,6},{5,7},{6,4},{7,5},{8,10},{9,11},{10,... | collective-permute-start | bytes 786440 | tf_op jit(solution)/shard_map/ppermute | solution.py:80
  62.7 19.2 %collective-permute-start.17 = (bf16[128,2048]{1,0:T(8,128)(2,1)}, bf16[128,2048]{1,0:T(8,128)(2,1)}, u32[]{:S(2)}, u32[]{:S(2)}) collective-permute-start(bf16[128,2048]{1,0:T(8,128)(2,1)} %collective-permute-done.11), channel_id=1, source_target_pairs={{0,4},{4,0},{8,12},{12,8},{16,20},{20,16},{24,28},{28,24},{1,5},{5... | collective-permute-start | bytes 1572872 | tf_op jit(solution)/shard_map/ppermute | solution.py:76
  64.2 17.6 %collective-permute-start.18 = (bf16[128,2048]{1,0:T(8,128)(2,1)}, bf16[128,2048]{1,0:T(8,128)(2,1)}, u32[]{:S(2)}, u32[]{:S(2)}) collective-permute-start(bf16[128,2048]{1,0:T(8,128)(2,1)} %get-tuple-element.342), channel_id=1, source_target_pairs={{0,2},{1,3},{2,0},{3,1},{4,6},{5,7},{6,4},{7,5},{8,10},{9,11},{10,... | collective-permute-start | bytes 1572872 | tf_op jit(solution)/shard_map/ppermute | solution.py:80
  70.7 24.7 %collective-permute-start.19 = (bf16[64,2048]{1,0:T(8,128)(2,1)}, bf16[64,2048]{1,0:T(8,128)(2,1)}, u32[]{:S(2)}, u32[]{:S(2)}) collective-permute-start(bf16[64,2048]{1,0:T(8,128)(2,1)} %get-tuple-element.672), channel_id=1, source_target_pairs={{0,8},{4,12},{8,16},{12,20},{16,24},{20,28},{24,0},{28,4},{1,9},{5... | collective-permute-start | bytes 786440 | tf_op jit(solution)/shard_map/ppermute | solution.py:76
  70.7 25.4 %collective-permute-start.20 = (bf16[64,2048]{1,0:T(8,128)(2,1)}, bf16[64,2048]{1,0:T(8,128)(2,1)}, u32[]{:S(2)}, u32[]{:S(2)}) collective-permute-start(bf16[64,2048]{1,0:T(8,128)(2,1)} %get-tuple-element.671), channel_id=1, source_target_pairs={{0,24},{4,28},{8,0},{12,4},{16,8},{20,12},{24,16},{28,20},{1,25},{... | collective-permute-start | bytes 786440 | tf_op jit(solution)/shard_map/ppermute | solution.py:76
  74.5 23.3 %collective-permute-start.21 = (bf16[64,2048]{1,0:T(8,128)(2,1)}, bf16[64,2048]{1,0:T(8,128)(2,1)}, u32[]{:S(2)}, u32[]{:S(2)}) collective-permute-start(bf16[64,2048]{1,0:T(8,128)(2,1)} %get-tuple-element.670), channel_id=1, source_target_pairs={{0,16},{4,20},{8,24},{12,28},{16,0},{20,4},{24,8},{28,12},{1,17},{... | collective-permute-start | bytes 786440 | tf_op jit(solution)/shard_map/ppermute | solution.py:76
  93.8 24.0 %collective-permute-start.22 = (bf16[128,2048]{1,0:T(8,128)(2,1)S(1)}, bf16[128,2048]{1,0:T(8,128)(2,1)S(1)}, u32[]{:S(2)}, u32[]{:S(2)}) collective-permute-start(bf16[128,2048]{1,0:T(8,128)(2,1)S(1)} %slice.860), channel_id=1, source_target_pairs={{0,4},{4,0},{8,12},{12,8},{16,20},{20,16},{24,28},{28,24},{1,5},{5... | collective-permute-start | bytes 1572872 | tf_op jit(solution)/shard_map/ppermute | solution.py:76
  94.7 23.1 %collective-permute-start.23 = (bf16[256,2048]{1,0:T(8,128)(2,1)S(1)}, bf16[256,2048]{1,0:T(8,128)(2,1)S(1)}, u32[]{:S(2)}, u32[]{:S(2)}) collective-permute-start(bf16[256,2048]{1,0:T(8,128)(2,1)S(1)} %copy-done.16), channel_id=1, source_target_pairs={{0,1},{1,0},{2,3},{3,2},{4,5},{5,4},{6,7},{7,6},{8,9},{9,8},{10,11... | collective-permute-start | bytes 3145736 | tf_op jit(solution)/shard_map/ppermute | solution.py:80
  95.4 22.3 %collective-permute-start.24 = (bf16[64,2048]{1,0:T(8,128)(2,1)S(1)}, bf16[64,2048]{1,0:T(8,128)(2,1)S(1)}, u32[]{:S(2)}, u32[]{:S(2)}) collective-permute-start(bf16[64,2048]{1,0:T(8,128)(2,1)S(1)} %get-tuple-element.669), channel_id=1, source_target_pairs={{0,4},{4,0},{8,12},{12,8},{16,20},{20,16},{24,28},{28,24},{1,5},{5... | collective-permute-start | bytes 786440 | tf_op jit(solution)/shard_map/ppermute | solution.py:76
  96.1 21.6 %collective-permute-start.25 = (bf16[64,2048]{1,0:T(8,128)(2,1)S(1)}, bf16[64,2048]{1,0:T(8,128)(2,1)S(1)}, u32[]{:S(2)}, u32[]{:S(2)}) collective-permute-start(bf16[64,2048]{1,0:T(8,128)(2,1)S(1)} %get-tuple-element.668), channel_id=1, source_target_pairs={{0,12},{4,8},{8,20},{12,16},{16,28},{20,24},{24,4},{28,0},{1,13},{... | collective-permute-start | bytes 786440 | tf_op jit(solution)/shard_map/ppermute | solution.py:76
  98.8 19.0 %collective-permute-start.26 = (bf16[2,64,2048]{2,1,0:T(8,128)(2,1)S(1)}, bf16[2,64,2048]{2,1,0:T(8,128)(2,1)S(1)}, u32[]{:S(2)}, u32[]{:S(2)}) collective-permute-start(bf16[2,64,2048]{2,1,0:T(8,128)(2,1)S(1)} %pad_maximum_fusion.10.refs_0_), channel_id=1, source_target_pairs={{0,2},{1,3},{2,0},{3,1},{4,6},{5,7},{6,4},{7,5},{8,10},{9,11},{10,... | collective-permute-start | bytes 1572872 | tf_op jit(solution)/shard_map/ppermute | solution.py:80
  117.8 20.9 %collective-permute-start.27 = (bf16[128,2048]{1,0:T(8,128)(2,1)S(1)}, bf16[128,2048]{1,0:T(8,128)(2,1)S(1)}, u32[]{:S(2)}, u32[]{:S(2)}) collective-permute-start(bf16[128,2048]{1,0:T(8,128)(2,1)S(1)} %slice.861), channel_id=1, source_target_pairs={{0,4},{4,0},{8,12},{12,8},{16,20},{20,16},{24,28},{28,24},{1,5},{5... | collective-permute-start | bytes 1572872 | tf_op jit(solution)/shard_map/ppermute | solution.py:76
  120.6 18.1 %collective-permute-start.28 = (bf16[128,2048]{1,0:T(8,128)(2,1)S(1)}, bf16[128,2048]{1,0:T(8,128)(2,1)S(1)}, u32[]{:S(2)}, u32[]{:S(2)}) collective-permute-start(bf16[128,2048]{1,0:T(8,128)(2,1)S(1)} %fusion.19), channel_id=1, source_target_pairs={{0,8},{4,12},{8,16},{12,20},{16,24},{20,28},{24,0},{28,4},{1,9},{5... | collective-permute-start | bytes 1572872 | tf_op jit(solution)/shard_map/ppermute | solution.py:76
  122.1 16.5 %collective-permute-start.30 = (bf16[2,64,2048]{2,1,0:T(8,128)(2,1)S(1)}, bf16[2,64,2048]{2,1,0:T(8,128)(2,1)S(1)}, u32[]{:S(2)}, u32[]{:S(2)}) collective-permute-start(bf16[2,64,2048]{2,1,0:T(8,128)(2,1)S(1)} %pad_maximum_fusion.10.refs_0_), channel_id=1, source_target_pairs={{0,1},{1,0},{2,3},{3,2},{4,5},{5,4},{6,7},{7,6},{8,9},{9,8},{10,11... | collective-permute-start | bytes 1572872 | tf_op jit(solution)/shard_map/ppermute | solution.py:80
  140.2 25.3 %collective-permute-start.33 = (bf16[128,2048]{1,0:T(8,128)(2,1)S(1)}, bf16[128,2048]{1,0:T(8,128)(2,1)S(1)}, u32[]{:S(2)}, u32[]{:S(2)}) collective-permute-start(bf16[128,2048]{1,0:T(8,128)(2,1)S(1)} %slice.862), channel_id=1, source_target_pairs={{0,4},{4,0},{8,12},{12,8},{16,20},{20,16},{24,28},{28,24},{1,5},{5... | collective-permute-start | bytes 1572872 | tf_op jit(solution)/shard_map/ppermute | solution.py:76
  141.0 24.6 %collective-permute-start.38 = (bf16[2,64,2048]{2,1,0:T(8,128)(2,1)S(1)}, bf16[2,64,2048]{2,1,0:T(8,128)(2,1)S(1)}, u32[]{:S(2)}, u32[]{:S(2)}) collective-permute-start(bf16[2,64,2048]{2,1,0:T(8,128)(2,1)S(1)} %pad_maximum_fusion.12.refs_8_), channel_id=1, source_target_pairs={{0,2},{1,3},{2,0},{3,1},{4,6},{5,7},{6,4},{7,5},{8,10},{9,11},{10,... | collective-permute-start | bytes 1572872 | tf_op jit(solution)/shard_map/ppermute | solution.py:80
  142.3 22.6 %collective-permute-start.35 = (bf16[64,2048]{1,0:T(8,128)(2,1)S(1)}, bf16[64,2048]{1,0:T(8,128)(2,1)S(1)}, u32[]{:S(2)}, u32[]{:S(2)}) collective-permute-start(bf16[64,2048]{1,0:T(8,128)(2,1)S(1)} %slice_bitcast_fusion.2), channel_id=1, source_target_pairs={{0,20},{4,16},{8,28},{12,24},{16,4},{20,0},{24,12},{28,8},{1,21},{... | collective-permute-start | bytes 786440 | tf_op jit(solution)/shard_map/ppermute | solution.py:76
  143.0 22.5 %collective-permute-start.34 = (bf16[128,2048]{1,0:T(8,128)(2,1)S(1)}, bf16[128,2048]{1,0:T(8,128)(2,1)S(1)}, u32[]{:S(2)}, u32[]{:S(2)}) collective-permute-start(bf16[128,2048]{1,0:T(8,128)(2,1)S(1)} %fusion.18), channel_id=1, source_target_pairs={{0,8},{4,12},{8,16},{12,20},{16,24},{20,28},{24,0},{28,4},{1,9},{5... | collective-permute-start | bytes 1572872 | tf_op jit(solution)/shard_map/ppermute | solution.py:76
  144.7 20.9 %collective-permute-start.36 = (bf16[2,64,2048]{2,1,0:T(8,128)(2,1)S(1)}, bf16[2,64,2048]{2,1,0:T(8,128)(2,1)S(1)}, u32[]{:S(2)}, u32[]{:S(2)}) collective-permute-start(bf16[2,64,2048]{2,1,0:T(8,128)(2,1)S(1)} %pad_maximum_fusion.11.refs_4_), channel_id=1, source_target_pairs={{0,1},{1,0},{2,3},{3,2},{4,5},{5,4},{6,7},{7,6},{8,9},{9,8},{10,11... | collective-permute-start | bytes 1572872 | tf_op jit(solution)/shard_map/ppermute | solution.py:80
  167.7 18.0 %collective-permute-start.39 = (bf16[128,2048]{1,0:T(8,128)(2,1)S(1)}, bf16[128,2048]{1,0:T(8,128)(2,1)S(1)}, u32[]{:S(2)}, u32[]{:S(2)}) collective-permute-start(bf16[128,2048]{1,0:T(8,128)(2,1)S(1)} %slice.863), channel_id=1, source_target_pairs={{0,4},{4,0},{8,12},{12,8},{16,20},{20,16},{24,28},{28,24},{1,5},{5... | collective-permute-start | bytes 1572872 | tf_op jit(solution)/shard_map/ppermute | solution.py:76
  170.4 15.3 %collective-permute-start.40 = (bf16[128,2048]{1,0:T(8,128)(2,1)S(1)}, bf16[128,2048]{1,0:T(8,128)(2,1)S(1)}, u32[]{:S(2)}, u32[]{:S(2)}) collective-permute-start(bf16[128,2048]{1,0:T(8,128)(2,1)S(1)} %fusion.17), channel_id=1, source_target_pairs={{0,8},{4,12},{8,16},{12,20},{16,24},{20,28},{24,0},{28,4},{1,9},{5... | collective-permute-start | bytes 1572872 | tf_op jit(solution)/shard_map/ppermute | solution.py:76
  170.5 15.2 %collective-permute-start.41 = (bf16[2,64,2048]{2,1,0:T(8,128)(2,1)S(1)}, bf16[2,64,2048]{2,1,0:T(8,128)(2,1)S(1)}, u32[]{:S(2)}, u32[]{:S(2)}) collective-permute-start(bf16[2,64,2048]{2,1,0:T(8,128)(2,1)S(1)} %pad_maximum_fusion.12.refs_8_), channel_id=1, source_target_pairs={{0,1},{1,0},{2,3},{3,2},{4,5},{5,4},{6,7},{7,6},{8,9},{9,8},{10,11... | collective-permute-start | bytes 1572872 | tf_op jit(solution)/shard_map/ppermute | solution.py:80
  170.6 15.9 %collective-permute-start.42 = (bf16[2,64,2048]{2,1,0:T(8,128)(2,1)S(1)}, bf16[2,64,2048]{2,1,0:T(8,128)(2,1)S(1)}, u32[]{:S(2)}, u32[]{:S(2)}) collective-permute-start(bf16[2,64,2048]{2,1,0:T(8,128)(2,1)S(1)} %collective-permute-done.38.refs_10_), channel_id=1, source_target_pairs={{0,1},{1,0},{2,3},{3,2},{4,5},{5,4},{6,7},{7,6},{8,9},{9,8},{10,11... | collective-permute-start | bytes 1572872 | tf_op jit(solution)/shard_map/ppermute | solution.py:80
  204.5 16.6 %collective-permute-start.49 = (bf16[128,2048]{1,0:T(8,128)(2,1)}, bf16[128,2048]{1,0:T(8,128)(2,1)S(1)}, u32[]{:S(2)}, u32[]{:S(2)}) collective-permute-start(bf16[128,2048]{1,0:T(8,128)(2,1)} %collective-permute-done.45), channel_id=1, source_target_pairs={{0,4},{4,0},{8,12},{12,8},{16,20},{20,16},{24,28},{28,24},{1,5},{5... | collective-permute-start | bytes 1572872 | tf_op jit(solution)/shard_map/ppermute | solution.py:76
  205.6 15.5 %collective-permute-start.50 = (bf16[128,2048]{1,0:T(8,128)(2,1)}, bf16[128,2048]{1,0:T(8,128)(2,1)S(1)}, u32[]{:S(2)}, u32[]{:S(2)}) collective-permute-start(bf16[128,2048]{1,0:T(8,128)(2,1)} %collective-permute-done.45), channel_id=1, source_target_pairs={{0,8},{4,12},{8,16},{12,20},{16,24},{20,28},{24,0},{28,4},{1,9},{5... | collective-permute-start | bytes 1572872 | tf_op jit(solution)/shard_map/ppermute | solution.py:76
  228.9 19.6 %collective-permute-start.51 = (bf16[128,2048]{1,0:T(8,128)(2,1)S(1)}, bf16[128,2048]{1,0:T(8,128)(2,1)S(1)}, u32[]{:S(2)}, u32[]{:S(2)}) collective-permute-start(bf16[128,2048]{1,0:T(8,128)(2,1)S(1)} %collective-permute-done.50), channel_id=1, source_target_pairs={{0,4},{4,0},{8,12},{12,8},{16,20},{20,16},{24,28},{28,24},{1,5},{5... | collective-permute-start | bytes 1572872 | tf_op jit(solution)/shard_map/ppermute | solution.py:76
  230.1 18.4 %collective-permute-start.52 = (bf16[128,2048]{1,0:T(8,128)(2,1)S(1)}, bf16[128,2048]{1,0:T(8,128)(2,1)S(1)}, u32[]{:S(2)}, u32[]{:S(2)}) collective-permute-start(bf16[128,2048]{1,0:T(8,128)(2,1)S(1)} %collective-permute-done.50), channel_id=1, source_target_pairs={{0,8},{4,12},{8,16},{12,20},{16,24},{20,28},{24,0},{28,4},{1,9},{5... | collective-permute-start | bytes 1572872 | tf_op jit(solution)/shard_map/ppermute | solution.py:76
  241.2 17.2 %collective-permute-start.56 = (bf16[128,2048]{1,0:T(8,128)(2,1)S(1)}, bf16[128,2048]{1,0:T(8,128)(2,1)S(1)}, u32[]{:S(2)}, u32[]{:S(2)}) collective-permute-start(bf16[128,2048]{1,0:T(8,128)(2,1)S(1)} %fusion.15), channel_id=1, source_target_pairs={{0,8},{4,12},{8,16},{12,20},{16,24},{20,28},{24,0},{28,4},{1,9},{5... | collective-permute-start | bytes 1572872 | tf_op jit(solution)/shard_map/ppermute | solution.py:76
  253.6 20.4 %collective-permute-start.53 = (bf16[128,2048]{1,0:T(8,128)(2,1)S(1)}, bf16[128,2048]{1,0:T(8,128)(2,1)S(1)}, u32[]{:S(2)}, u32[]{:S(2)}) collective-permute-start(bf16[128,2048]{1,0:T(8,128)(2,1)S(1)} %collective-permute-done.52), channel_id=1, source_target_pairs={{0,4},{4,0},{8,12},{12,8},{16,20},{20,16},{24,28},{28,24},{1,5},{5... | collective-permute-start | bytes 1572872 | tf_op jit(solution)/shard_map/ppermute | solution.py:76
  306.6 15.4 %collective-permute-start.64 = (bf16[128,1024]{1,0:T(8,128)(2,1)S(1)}, bf16[128,1024]{1,0:T(8,128)(2,1)S(1)}, u32[]{:S(2)}, u32[]{:S(2)}) collective-permute-start(bf16[128,1024]{1,0:T(8,128)(2,1)S(1)} %get-tuple-element.688), channel_id=1, source_target_pairs={{0,8},{4,12},{8,16},{12,20},{16,24},{20,28},{24,0},{28,4},{1,9},{5... | collective-permute-start | bytes 786440 | tf_op jit(solution)/shard_map/ppermute | solution.py:76
  329.1 15.5 %collective-permute-start.67 = (bf16[128,1024]{1,0:T(8,128)(2,1)}, bf16[128,1024]{1,0:T(8,128)(2,1)}, u32[]{:S(2)}, u32[]{:S(2)}) collective-permute-start(bf16[128,1024]{1,0:T(8,128)(2,1)} %collective-permute-done.66), channel_id=1, source_target_pairs={{0,4},{4,0},{8,12},{12,8},{16,20},{20,16},{24,28},{28,24},{1,5},{5... | collective-permute-start | bytes 786440 | tf_op jit(solution)/shard_map/ppermute | solution.py:76
  331.2 15.1 %collective-permute-start.68 = (bf16[128,1024]{1,0:T(8,128)(2,1)}, bf16[128,1024]{1,0:T(8,128)(2,1)}, u32[]{:S(2)}, u32[]{:S(2)}) collective-permute-start(bf16[128,1024]{1,0:T(8,128)(2,1)} %collective-permute-done.66), channel_id=1, source_target_pairs={{0,8},{4,12},{8,16},{12,20},{16,24},{20,28},{24,0},{28,4},{1,9},{5... | collective-permute-start | bytes 786440 | tf_op jit(solution)/shard_map/ppermute | solution.py:76
  344.5 15.1 %collective-permute-start.75 = (bf16[128,1024]{1,0:T(8,128)(2,1)S(1)}, bf16[128,1024]{1,0:T(8,128)(2,1)}, u32[]{:S(2)}, u32[]{:S(2)}) collective-permute-start(bf16[128,1024]{1,0:T(8,128)(2,1)S(1)} %get-tuple-element.676), channel_id=1, source_target_pairs={{0,4},{4,0},{8,12},{12,8},{16,20},{20,16},{24,28},{28,24},{1,5},{5... | collective-permute-start | bytes 786440 | tf_op jit(solution)/shard_map/ppermute | solution.py:76
  346.3 18.9 %collective-permute-start.73 = (bf16[128,1024]{1,0:T(8,128)(2,1)}, bf16[128,1024]{1,0:T(8,128)(2,1)}, u32[]{:S(2)}, u32[]{:S(2)}) collective-permute-start(bf16[128,1024]{1,0:T(8,128)(2,1)} %collective-permute-done.68), channel_id=1, source_target_pairs={{0,4},{4,0},{8,12},{12,8},{16,20},{20,16},{24,28},{28,24},{1,5},{5... | collective-permute-start | bytes 786440 | tf_op jit(solution)/shard_map/ppermute | solution.py:76
  346.7 20.7 %collective-permute-start.74 = (bf16[128,1024]{1,0:T(8,128)(2,1)}, bf16[128,1024]{1,0:T(8,128)(2,1)}, u32[]{:S(2)}, u32[]{:S(2)}) collective-permute-start(bf16[128,1024]{1,0:T(8,128)(2,1)} %collective-permute-done.72), channel_id=1, source_target_pairs={{0,4},{4,0},{8,12},{12,8},{16,20},{20,16},{24,28},{28,24},{1,5},{5... | collective-permute-start | bytes 786440 | tf_op jit(solution)/shard_map/ppermute | solution.py:76
  359.2 15.7 %collective-permute-start.83 = (bf16[128,1024]{1,0:T(8,128)(2,1)}, bf16[128,1024]{1,0:T(8,128)(2,1)S(1)}, u32[]{:S(2)}, u32[]{:S(2)}) collective-permute-start(bf16[128,1024]{1,0:T(8,128)(2,1)} %get-tuple-element.436), channel_id=1, source_target_pairs={{0,4},{4,0},{8,12},{12,8},{16,20},{20,16},{24,28},{28,24},{1,5},{5... | collective-permute-start | bytes 786440 | tf_op jit(solution)/shard_map/ppermute | solution.py:76
  387.6 19.5 %collective-permute-start.89 = (bf16[2,2,64,2048]{3,2,1,0:T(8,128)(2,1)S(1)}, bf16[2,2,64,2048]{3,2,1,0:T(8,128)(2,1)S(1)}, u32[]{:S(2)}, u32[]{:S(2)}) collective-permute-start(bf16[2,2,64,2048]{3,2,1,0:T(8,128)(2,1)S(1)} %get-tuple-element.463), channel_id=1, source_target_pairs={{0,1},{1,0},{2,3},{3,2},{4,5},{5,4},{6,7},{7,6},{8,9},{9,8},{10,11... | collective-permute-start | bytes 3145736 | tf_op jit(solution)/shard_map/ppermute | solution.py:80
  388.8 18.3 %collective-permute-start.87 = (bf16[128,1024]{1,0:T(8,128)(2,1)S(1)}, bf16[128,1024]{1,0:T(8,128)(2,1)S(1)}, u32[]{:S(2)}, u32[]{:S(2)}) collective-permute-start(bf16[128,1024]{1,0:T(8,128)(2,1)S(1)} %get-tuple-element.451), channel_id=1, source_target_pairs={{0,4},{4,0},{8,12},{12,8},{16,20},{20,16},{24,28},{28,24},{1,5},{5... | collective-permute-start | bytes 786440 | tf_op jit(solution)/shard_map/ppermute | solution.py:76
  391.1 15.9 %collective-permute-start.88 = (bf16[128,1024]{1,0:T(8,128)(2,1)S(1)}, bf16[128,1024]{1,0:T(8,128)(2,1)S(1)}, u32[]{:S(2)}, u32[]{:S(2)}) collective-permute-start(bf16[128,1024]{1,0:T(8,128)(2,1)S(1)} %get-tuple-element.663), channel_id=1, source_target_pairs={{0,8},{4,12},{8,16},{12,20},{16,24},{20,28},{24,0},{28,4},{1,9},{5... | collective-permute-start | bytes 786440 | tf_op jit(solution)/shard_map/ppermute | solution.py:76
  409.3 15.6 %collective-permute-start.90 = (bf16[128,2048]{1,0:T(8,128)(2,1)S(1)}, bf16[128,2048]{1,0:T(8,128)(2,1)S(1)}, u32[]{:S(2)}, u32[]{:S(2)}) collective-permute-start(bf16[128,2048]{1,0:T(8,128)(2,1)S(1)} %get-tuple-element.640), channel_id=1, source_target_pairs={{0,4},{4,0},{8,12},{12,8},{16,20},{20,16},{24,28},{28,24},{1,5},{5... | collective-permute-start | bytes 1572872 | tf_op jit(solution)/shard_map/ppermute | solution.py:76
  409.6 15.3 %collective-permute-start.91 = (bf16[128,2048]{1,0:T(8,128)(2,1)S(1)}, bf16[128,2048]{1,0:T(8,128)(2,1)S(1)}, u32[]{:S(2)}, u32[]{:S(2)}) collective-permute-start(bf16[128,2048]{1,0:T(8,128)(2,1)S(1)} %get-tuple-element.640), channel_id=1, source_target_pairs={{0,8},{4,12},{8,16},{12,20},{16,24},{20,28},{24,0},{28,4},{1,9},{5... | collective-permute-start | bytes 1572872 | tf_op jit(solution)/shard_map/ppermute | solution.py:76
  424.9 17.2 %collective-permute-start.95 = (bf16[128,2048]{1,0:T(8,128)(2,1)S(1)}, bf16[128,2048]{1,0:T(8,128)(2,1)S(1)}, u32[]{:S(2)}, u32[]{:S(2)}) collective-permute-start(bf16[128,2048]{1,0:T(8,128)(2,1)S(1)} %collective-permute-done.91), channel_id=1, source_target_pairs={{0,4},{4,0},{8,12},{12,8},{16,20},{20,16},{24,28},{28,24},{1,5},{5... | collective-permute-start | bytes 1572872 | tf_op jit(solution)/shard_map/ppermute | solution.py:76
  426.1 16.0 %collective-permute-start.96 = (bf16[128,2048]{1,0:T(8,128)(2,1)S(1)}, bf16[128,2048]{1,0:T(8,128)(2,1)}, u32[]{:S(2)}, u32[]{:S(2)}) collective-permute-start(bf16[128,2048]{1,0:T(8,128)(2,1)S(1)} %collective-permute-done.91), channel_id=1, source_target_pairs={{0,8},{4,12},{8,16},{12,20},{16,24},{20,28},{24,0},{28,4},{1,9},{5... | collective-permute-start | bytes 1572872 | tf_op jit(solution)/shard_map/ppermute | solution.py:76
  442.1 16.4 %collective-permute-start.100 = (bf16[128,2048]{1,0:T(8,128)(2,1)}, bf16[128,2048]{1,0:T(8,128)(2,1)}, u32[]{:S(2)}, u32[]{:S(2)}) collective-permute-start(bf16[128,2048]{1,0:T(8,128)(2,1)} %collective-permute-done.96), channel_id=1, source_target_pairs={{0,4},{4,0},{8,12},{12,8},{16,20},{20,16},{24,28},{28,24},{1,5},{5... | collective-permute-start | bytes 1572872 | tf_op jit(solution)/shard_map/ppermute | solution.py:76
  442.5 16.5 %collective-permute-start.101 = (bf16[128,2048]{1,0:T(8,128)(2,1)}, bf16[128,2048]{1,0:T(8,128)(2,1)}, u32[]{:S(2)}, u32[]{:S(2)}) collective-permute-start(bf16[128,2048]{1,0:T(8,128)(2,1)} %collective-permute-done.96), channel_id=1, source_target_pairs={{0,8},{4,12},{8,16},{12,20},{16,24},{20,28},{24,0},{28,4},{1,9},{5... | collective-permute-start | bytes 1572872 | tf_op jit(solution)/shard_map/ppermute | solution.py:76
  459.0 20.8 %collective-permute-start.106 = (bf16[2,1,256,2048]{3,2,1,0:T(8,128)(2,1)}, bf16[2,1,256,2048]{3,2,1,0:T(8,128)(2,1)S(1)}, u32[]{:S(2)}, u32[]{:S(2)}) collective-permute-start(bf16[2,1,256,2048]{3,2,1,0:T(8,128)(2,1)} %get-tuple-element.516), channel_id=1, source_target_pairs={{0,1},{1,0},{2,3},{3,2},{4,5},{5,4},{6,7},{7,6},{8,9},{9,8},{10,11... | collective-permute-start | bytes 6291464 | tf_op jit(solution)/shard_map/ppermute | solution.py:80
  460.3 19.5 %collective-permute-start.105 = (bf16[128,2048]{1,0:T(8,128)(2,1)}, bf16[128,2048]{1,0:T(8,128)(2,1)S(1)}, u32[]{:S(2)}, u32[]{:S(2)}) collective-permute-start(bf16[128,2048]{1,0:T(8,128)(2,1)} %collective-permute-done.101), channel_id=1, source_target_pairs={{0,4},{4,0},{8,12},{12,8},{16,20},{20,16},{24,28},{28,24},{1,5},{5... | collective-permute-start | bytes 1572872 | tf_op jit(solution)/shard_map/ppermute | solution.py:76
  462.0 18.4 %collective-permute-start.110 = (bf16[64,2048]{1,0:T(8,128)(2,1)S(1)}, bf16[64,2048]{1,0:T(8,128)(2,1)S(1)}, u32[]{:S(2)}, u32[]{:S(2)}) collective-permute-start(bf16[64,2048]{1,0:T(8,128)(2,1)S(1)} %get-tuple-element.525), channel_id=1, source_target_pairs={{0,24},{4,28},{8,0},{12,4},{16,8},{20,12},{24,16},{28,20},{1,25},{... | collective-permute-start | bytes 786440 | tf_op jit(solution)/shard_map/ppermute | solution.py:76
  481.6 15.0 %collective-permute-start.113 = (bf16[128,2048]{1,0:T(8,128)(2,1)S(1)}, bf16[128,2048]{1,0:T(8,128)(2,1)S(1)}, u32[]{:S(2)}, u32[]{:S(2)}) collective-permute-start(bf16[128,2048]{1,0:T(8,128)(2,1)S(1)} %get-tuple-element.673), channel_id=1, source_target_pairs={{0,2},{1,3},{2,0},{3,1},{4,6},{5,7},{6,4},{7,5},{8,10},{9,11},{10,... | collective-permute-start | bytes 1572872 | tf_op jit(solution)/shard_map/ppermute | solution.py:80
  496.7 15.8 %collective-permute-start.116 = (bf16[128,2048]{1,0:T(8,128)(2,1)S(1)}, bf16[128,2048]{1,0:T(8,128)(2,1)S(1)}, u32[]{:S(2)}, u32[]{:S(2)}) collective-permute-start(bf16[128,2048]{1,0:T(8,128)(2,1)S(1)} %get-tuple-element.554), channel_id=1, source_target_pairs={{0,2},{1,3},{2,0},{3,1},{4,6},{5,7},{6,4},{7,5},{8,10},{9,11},{10,... | collective-permute-start | bytes 1572872 | tf_op jit(solution)/shard_map/ppermute | solution.py:80
  497.1 15.3 %collective-permute-start.115 = (bf16[64,2048]{1,0:T(8,128)(2,1)S(1)}, bf16[64,2048]{1,0:T(8,128)(2,1)S(1)}, u32[]{:S(2)}, u32[]{:S(2)}) collective-permute-start(bf16[64,2048]{1,0:T(8,128)(2,1)S(1)} %get-tuple-element.552), channel_id=1, source_target_pairs={{0,28},{4,24},{8,4},{12,0},{16,12},{20,8},{24,20},{28,16},{1,29},{... | collective-permute-start | bytes 786440 | tf_op jit(solution)/shard_map/ppermute | solution.py:76
  515.2 18.4 %collective-permute-start.117 = (bf16[128,2048]{1,0:T(8,128)(2,1)S(1)}, bf16[128,2048]{1,0:T(8,128)(2,1)S(1)}, u32[]{:S(2)}, u32[]{:S(2)}) collective-permute-start(bf16[128,2048]{1,0:T(8,128)(2,1)S(1)} %slice.855), channel_id=1, source_target_pairs={{0,4},{4,0},{8,12},{12,8},{16,20},{20,16},{24,28},{28,24},{1,5},{5... | collective-permute-start | bytes 1572872 | tf_op jit(solution)/shard_map/ppermute | solution.py:76
  533.6 17.8 %collective-permute-start.123 = (bf16[2,8,64,384]{3,2,1,0:T(8,128)(2,1)S(1)}, bf16[2,8,64,384]{3,2,1,0:T(8,128)(2,1)S(1)}, u32[]{:S(2)}, u32[]{:S(2)}) collective-permute-start(bf16[2,8,64,384]{3,2,1,0:T(8,128)(2,1)S(1)} %get-tuple-element.589), channel_id=1, source_target_pairs={{0,1},{1,0},{2,3},{3,2},{4,5},{5,4},{6,7},{7,6},{8,9},{9,8},{10,11... | collective-permute-start | bytes 2359304 | tf_op jit(solution)/shard_map/ppermute | solution.py:80
  533.7 17.6 %collective-permute-start.120 = (bf16[128,2048]{1,0:T(8,128)(2,1)}, bf16[128,2048]{1,0:T(8,128)(2,1)S(1)}, u32[]{:S(2)}, u32[]{:S(2)}) collective-permute-start(bf16[128,2048]{1,0:T(8,128)(2,1)} %slice.852), channel_id=1, source_target_pairs={{0,4},{4,0},{8,12},{12,8},{16,20},{20,16},{24,28},{28,24},{1,5},{5... | collective-permute-start | bytes 1572872 | tf_op jit(solution)/shard_map/ppermute | solution.py:76
  535.3 16.1 %collective-permute-start.121 = (bf16[128,2048]{1,0:T(8,128)(2,1)S(1)}, bf16[128,2048]{1,0:T(8,128)(2,1)S(1)}, u32[]{:S(2)}, u32[]{:S(2)}) collective-permute-start(bf16[128,2048]{1,0:T(8,128)(2,1)S(1)} %fusion.12), channel_id=1, source_target_pairs={{0,8},{4,12},{8,16},{12,20},{16,24},{20,28},{24,0},{28,4},{1,9},{5... | collective-permute-start | bytes 1572872 | tf_op jit(solution)/shard_map/ppermute | solution.py:76
  552.4 16.6 %collective-permute-start.127 = (bf16[8,64,384]{2,1,0:T(8,128)(2,1)}, bf16[8,64,384]{2,1,0:T(8,128)(2,1)}, u32[]{:S(2)}, u32[]{:S(2)}) collective-permute-start(bf16[8,64,384]{2,1,0:T(8,128)(2,1)} %fusion.45), channel_id=1, source_target_pairs={{0,2},{1,3},{2,0},{3,1},{4,6},{5,7},{6,4},{7,5},{8,10},{9,11},{10,... | collective-permute-start | bytes 1179656 | tf_op jit(solution)/shard_map/ppermute | solution.py:80
  554.9 15.4 %collective-permute-start.125 = (bf16[128,2048]{1,0:T(8,128)(2,1)}, bf16[128,2048]{1,0:T(8,128)(2,1)}, u32[]{:S(2)}, u32[]{:S(2)}) collective-permute-start(bf16[128,2048]{1,0:T(8,128)(2,1)} %fusion.11), channel_id=1, source_target_pairs={{0,8},{4,12},{8,16},{12,20},{16,24},{20,28},{24,0},{28,4},{1,9},{5... | collective-permute-start | bytes 1572872 | tf_op jit(solution)/shard_map/ppermute | solution.py:76
  555.1 15.1 %collective-permute-start.124 = (bf16[128,2048]{1,0:T(8,128)(2,1)}, bf16[128,2048]{1,0:T(8,128)(2,1)}, u32[]{:S(2)}, u32[]{:S(2)}) collective-permute-start(bf16[128,2048]{1,0:T(8,128)(2,1)} %slice.853), channel_id=1, source_target_pairs={{0,4},{4,0},{8,12},{12,8},{16,20},{20,16},{24,28},{28,24},{1,5},{5... | collective-permute-start | bytes 1572872 | tf_op jit(solution)/shard_map/ppermute | solution.py:76
  (255 other events, 2236.8 us)

commit v4 on v3

--- a/solution.py
+++ b/solution.py
@@ -475,7 +475,7 @@
     stream, width = act.shape
     width, count = width - 128, stream // 2
     base = half * count
-    rows = 256 if stream <= 1024 else 128
+    rows = 512 if stream <= 1024 else 128
     part, by_row, whole = attend_specs(rows, stream, base)
     first = half == 0
     return pl.pallas_call(

time: 615 us -> 610 us (level)
  transfers between devices with their start and end apart: 134 -> 134, of which waited for: 47 -> 46; matrix products, arithmetic and copies ran while one was open for 21% -> 21% of each run, Pallas kernels for 15% -> 15%
where the time goes in v4:
time: 610 us; the launch traced here: 604 us
  waiting for transfers between devices  210 us (34%)
  starting transfers between devices  124 us (20%)
  Pallas kernels  94.5 us (15%)
  other arithmetic  57.3 us (9%)
  matrix products  56.6 us (9%)
  local copies, waits for them, and re-layouts  53.7 us (9%)
  between operations  8.01 us (1%)
    ppermute x92, waiting for transfers between devices, shift(): return lax.ppermute(x, 'ctx', perm)  168 us
    ppermute x92, starting transfers between devices, shift(): return lax.ppermute(x, 'ctx', perm)  99.9 us
    ppermute x42, waiting for transfers between devices, flip(): return lax.ppermute(x, axis, [(i, i ^ bit) for i in range(size)])  42.5 us
    dot_general x16, matrix products, against(): lax.dot_general(left, right, (((1,), (1,)), ((), ())), preferred_element_...  33.9 us
    pallas_call x7, Pallas kernels, term(): pl.pallas_call(functools.partial(term_kernel, count, m), grid_spec=pltpu....  29.4 us
    unnamed x380, local copies, waits for them, and re-layouts  28.8 us
    ppermute x42, starting transfers between devices, flip(): return lax.ppermute(x, axis, [(i, i ^ bit) for i in range(size)])  24.1 us
    dot_general x16, matrix products, mm(): return jnp.dot(left, right, preferred_element_type=F32)  22.7 us
  transfers between devices with their start and end apart: 134, of which 46 were waited for; matrix products, arithmetic and copies ran while one was open for 21% of the time, Pallas kernels for 15%

profile of v4, /device:TPU:0, one launch (start us, length us, event | category | flops | bytes accessed | tf_op | source)
XLA Modules:
  0.0 604.5 jit_solution(2941199809709545793)
XLA Ops:
  0.7 3.0 collective-permute-start
  11.4 2.5 shard_map.238
  16.1 5.0 collective-permute-done.3
  31.7 6.8 %shard_map.242 = bf16[8,64,2048]{2,1,0:T(8,128)(2,1)} custom-call(s32[8]{0:T(128)} %stack.75.spots, bf16[64,8192]{1,0:T(8,128)(2,1)} %refs_8_.1, bf16[64,8192]{1,0:T(8,128)(2,1)} %refs_9_.1, f32[64,1]{1,0:T(8,128)} %copy.51.gain_ref), custom_call_target="tpu_custom_call" | custom-call | tf_op jit(solution)/shard_map/pallas_call | solution.py:251
  38.8 3.4 collective-permute-done.7
  54.9 5.6 collective-permute-done.14.refs_2_
  70.7 4.0 collective-permute-start.20
  85.5 7.3 %shard_map.240 = (bf16[512,256]{1,0:T(8,128)(2,1)S(1)}, f32[512,128]{1,0:T(8,128)S(1)}, bf16[512,256]{1,0:T(8,128)(2,1)S(1)}, bf16[1024,128]{1,0:T(8,128)(2,1)}, f32[1024,128]{1,0:T(8,128)S(1)}) custom-call(f32[1024,384]{1,0:T(8,128)S(1)} %pad_maximum_fusion.act_ref, f32[128,1024]{1,0:T(8,128)S(1)} %concatenate.181.table_ref, ...), custom_call_target="tpu_custom_call" | custom-call | flops 2147483648 | bytes 2097152 | tf_op jit(solution)/shard_map/pallas_call | solution.py:481
  99.2 7.2 %shard_map.243 = (bf16[512,256]{1,0:T(8,128)(2,1)S(1)}, f32[512,128]{1,0:T(8,128)S(1)}, bf16[512,256]{1,0:T(8,128)(2,1)S(1)}, bf16[1024,128]{1,0:T(8,128)(2,1)S(1)}) custom-call(f32[1024,384]{1,0:T(8,128)S(1)} %pad_maximum_fusion.act_ref, f32[128,1024]{1,0:T(8,128)S(1)} %copy-done.58, f32[1024,128]{1,0:T(8,128)S(1)} %get-tuple-element.352.facts_in.facts_ref), custom_call_target="tpu_custom_call" | custom-call | flops 2147483648 | bytes 2097152 | tf_op jit(solution)/shard_map/pallas_call | solution.py:481
  108.3 9.1 %collective-permute-done.24 = bf16[64,2048]{1,0:T(8,128)(2,1)S(1)} collective-permute-done((bf16[64,2048]{1,0:T(8,128)(2,1)S(1)}, bf16[64,2048]{1,0:T(8,128)(2,1)S(1)}, u32[]{:S(2)}, u32[]{:S(2)}) %collective-permute-start.24) | collective-permute-done | bytes 262176 | tf_op jit(solution)/shard_map/ppermute | solution.py:76
  121.9 7.0 %collective-permute-done.29 = bf16[64,2048]{1,0:T(8,128)(2,1)S(1)} collective-permute-done((bf16[64,2048]{1,0:T(8,128)(2,1)S(1)}, bf16[64,2048]{1,0:T(8,128)(2,1)S(1)}, u32[]{:S(2)}, u32[]{:S(2)}) %collective-permute-start.29) | collective-permute-done | bytes 262176 | tf_op jit(solution)/shard_map/ppermute | solution.py:76
  129.7 8.7 %collective-permute-done.28 = bf16[128,2048]{1,0:T(8,128)(2,1)S(1)} collective-permute-done((bf16[128,2048]{1,0:T(8,128)(2,1)S(1)}, bf16[128,2048]{1,0:T(8,128)(2,1)S(1)}, u32[]{:S(2)}, u32[]{:S(2)}) %collective-permute-start.28) | collective-permute-done | bytes 524320 | tf_op jit(solution)/shard_map/ppermute | solution.py:76
  144.4 20.3 %collective-permute-done.35 = bf16[64,2048]{1,0:T(8,128)(2,1)S(1)} collective-permute-done((bf16[64,2048]{1,0:T(8,128)(2,1)S(1)}, bf16[64,2048]{1,0:T(8,128)(2,1)S(1)}, u32[]{:S(2)}, u32[]{:S(2)}) %collective-permute-start.35) | collective-permute-done | bytes 262176 | tf_op jit(solution)/shard_map/ppermute | solution.py:76
  173.5 9.9 %collective-permute-done.43.refs_14_ = bf16[2,64,2048]{2,1,0:T(8,128)(2,1)} collective-permute-done((bf16[2,64,2048]{2,1,0:T(8,128)(2,1)}, bf16[2,64,2048]{2,1,0:T(8,128)(2,1)}, u32[]{:S(2)}, u32[]{:S(2)}) %collective-permute-start.43) | collective-permute-done | bytes 524320 | tf_op jit(solution)/shard_map/ppermute | solution.py:80
  192.6 9.2 %collective-permute-done.44 = bf16[128,2048]{1,0:T(8,128)(2,1)} collective-permute-done((bf16[128,2048]{1,0:T(8,128)(2,1)}, bf16[128,2048]{1,0:T(8,128)(2,1)}, u32[]{:S(2)}, u32[]{:S(2)}) %collective-permute-start.44) | collective-permute-done | bytes 524320 | tf_op jit(solution)/shard_map/ppermute | solution.py:76
  201.8 2.4 collective-permute-done.45
  209.4 5.7 shard_map.245
  215.2 4.6 shard_map.244
  221.4 2.4 fusion.122
  230.2 11.0 %collective-permute-done.54 = bf16[128,2048]{1,0:T(8,128)(2,1)S(1)} collective-permute-done((bf16[128,2048]{1,0:T(8,128)(2,1)S(1)}, bf16[128,2048]{1,0:T(8,128)(2,1)S(1)}, u32[]{:S(2)}, u32[]{:S(2)}) %collective-permute-start.54) | collective-permute-done | bytes 524320 | tf_op jit(solution)/shard_map/ppermute | solution.py:76
  241.4 7.2 %collective-permute-done.51 = bf16[128,2048]{1,0:T(8,128)(2,1)S(1)} collective-permute-done((bf16[128,2048]{1,0:T(8,128)(2,1)S(1)}, bf16[128,2048]{1,0:T(8,128)(2,1)S(1)}, u32[]{:S(2)}, u32[]{:S(2)}) %collective-permute-start.51) | collective-permute-done | bytes 524320 | tf_op jit(solution)/shard_map/ppermute | solution.py:76
  248.7 2.4 fusion.120
  254.9 3.6 fusion.92
  258.6 9.2 %collective-permute-done.55 = bf16[128,2048]{1,0:T(8,128)(2,1)S(1)} collective-permute-done((bf16[128,2048]{1,0:T(8,128)(2,1)S(1)}, bf16[128,2048]{1,0:T(8,128)(2,1)S(1)}, u32[]{:S(2)}, u32[]{:S(2)}) %collective-permute-start.55) | collective-permute-done | bytes 524320 | tf_op jit(solution)/shard_map/ppermute | solution.py:76
  268.2 6.0 collective-permute-done.53
  274.2 2.4 fusion.91
  282.5 5.1 collective-permute-done.57
  288.6 2.5 collective-permute-start.60
  294.5 6.5 %collective-permute-done.60 = bf16[128,2048]{1,0:T(8,128)(2,1)} collective-permute-done((bf16[128,2048]{1,0:T(8,128)(2,1)}, bf16[128,2048]{1,0:T(8,128)(2,1)}, u32[]{:S(2)}, u32[]{:S(2)}) %collective-permute-start.60) | collective-permute-done | bytes 524320 | tf_op jit(solution)/shard_map/ppermute | solution.py:76
  301.0 3.2 multiply_reduce_fusion.4
  306.7 4.7 collective-permute-start.64
  317.8 4.2 collective-permute-done.64
  323.8 4.1 fusion.114
  335.3 2.7 multiply_convert_fusion.1
  338.0 4.1 fusion.117
  348.7 3.6 multiply_convert_fusion.3
  352.4 5.2 fusion.116
  359.7 2.3 fusion.35
  362.1 2.8 collective-permute-start.84
  365.4 2.2 collective-permute-done.74
  367.6 3.8 multiply_convert_fusion.5
  371.4 3.7 fusion.115
  382.2 3.7 shard_map.246
  395.4 3.7 shard_map.247
  399.1 7.8 %collective-permute-done.81 = bf16[128,1024]{1,0:T(8,128)(2,1)S(1)} collective-permute-done((bf16[128,1024]{1,0:T(8,128)(2,1)S(1)}, bf16[128,1024]{1,0:T(8,128)(2,1)S(1)}, u32[]{:S(2)}, u32[]{:S(2)}) %collective-permute-start.81) | collective-permute-done | bytes 262176 | tf_op jit(solution)/shard_map/ppermute | solution.py:76
  412.9 3.7 shard_map.248
  416.7 5.8 collective-permute-done.92
  428.5 3.7 shard_map.249
  432.4 4.7 collective-permute-done.97
  437.1 4.9 collective-permute-done.99
  447.2 3.8 collective-permute-start.102
  451.1 6.9 %shard_map.250 = (bf16[2,1,256,2048]{3,2,1,0:T(8,128)(2,1)S(1)}, bf16[2,1,256,2048]{3,2,1,0:T(8,128)(2,1)}) custom-call(s32[3]{0:T(128)S(1)} %pad_add_fusion.1.spots, bf16[256,1024]{1,0:T(8,128)(2,1)S(1)} %copy-done.38, bf16[256,1024]{1,0:T(8,128)(2,1)S(1)} %copy-done.32, bf16[256,1024]{1,0:T(8,128)(2,1)S(1)} %copy-done.34, ...), custom_call_target="tpu_custom_call" | custom-call | flops 4294967296 | bytes 10485760 | tf_op jit(solution)/shard_map/pallas_call | solution.py:285
  461.9 2.7 collective-permute-start.110
  470.3 9.3 %collective-permute-done.108 = bf16[2,64,2048]{2,1,0:T(8,128)(2,1)S(1)} collective-permute-done((bf16[2,64,2048]{2,1,0:T(8,128)(2,1)S(1)}, bf16[2,64,2048]{2,1,0:T(8,128)(2,1)S(1)}, u32[]{:S(2)}, u32[]{:S(2)}) %collective-permute-start.108) | collective-permute-done | bytes 524320 | tf_op jit(solution)/shard_map/ppermute | solution.py:80
  483.9 9.6 %shard_map.251 = (bf16[512,256]{1,0:T(8,128)(2,1)S(1)}, bf16[512,256]{1,0:T(8,128)(2,1)S(1)}, f32[1024,256]{1,0:T(8,128)S(1)}, f32[1024,256]{1,0:T(8,128)S(1)}) custom-call(bf16[512,256]{1,0:T(8,128)(2,1)S(1)} %copy-done.89, bf16[512,256]{1,0:T(8,128)(2,1)S(1)} %pad_maximum_fusion.17.g_ref, bf16[1024,128]{1,0:T(8,128)(2,1)S(1)} %copy-done.85, ...), custom_call_target="tpu_custom_call" | custom-call | flops 5368709120 | bytes 5242880 | tf_op jit(solution)/shard_map/pallas_call | solution.py:515
  497.0 3.2 collective-permute-start.115
  500.5 11.7 %shard_map.252 = (bf16[512,256]{1,0:T(8,128)(2,1)S(1)}, bf16[512,256]{1,0:T(8,128)(2,1)S(1)}, bf16[1024,128]{1,0:T(8,128)(2,1)S(1)}, bf16[1024,128]{1,0:T(8,128)(2,1)S(1)}) custom-call(bf16[512,256]{1,0:T(8,128)(2,1)S(1)} %copy-done.83, bf16[512,256]{1,0:T(8,128)(2,1)S(1)} %pad_maximum_fusion.18.g_ref, bf16[1024,128]{1,0:T(8,128)(2,1)S(1)} %copy-done.85, ...), custom_call_target="tpu_custom_call" | custom-call | flops 5368709120 | bytes 5242880 | tf_op jit(solution)/shard_map/pallas_call | solution.py:515
  526.0 5.7 shard_map.254
  539.1 12.1 %collective-permute-done.121 = bf16[128,2048]{1,0:T(8,128)(2,1)S(1)} collective-permute-done((bf16[128,2048]{1,0:T(8,128)(2,1)S(1)}, bf16[128,2048]{1,0:T(8,128)(2,1)S(1)}, u32[]{:S(2)}, u32[]{:S(2)}) %collective-permute-start.121) | collective-permute-done | bytes 524320 | tf_op jit(solution)/shard_map/ppermute | solution.py:76
  563.9 4.9 shard_map.255
  579.2 8.5 %collective-permute-done.129 = bf16[128,2048]{1,0:T(8,128)(2,1)S(1)} collective-permute-done((bf16[128,2048]{1,0:T(8,128)(2,1)S(1)}, bf16[128,2048]{1,0:T(8,128)(2,1)S(1)}, u32[]{:S(2)}, u32[]{:S(2)}) %collective-permute-start.129) | collective-permute-done | bytes 524320 | tf_op jit(solution)/shard_map/ppermute | solution.py:76
  588.7 3.4 collective-permute-start.132
  595.4 2.6 collective-permute-done.132
  598.8 2.9 shard_map.256
  (802 shorter events, 244.5 us)
Async XLA Ops:
  0.7 20.4 %collective-permute-start = (bf16[128,2048]{1,0:T(8,128)(2,1)}, bf16[128,2048]{1,0:T(8,128)(2,1)S(1)}, u32[]{:S(2)}, u32[]{:S(2)}) collective-permute-start(bf16[128,2048]{1,0:T(8,128)(2,1)} %bitcast.277), channel_id=1, source_target_pairs={{0,4},{4,0},{8,12},{12,8},{16,20},{20,16},{24,28},{28,24},{1,5},{5... | collective-permute-start | bytes 1572872 | tf_op jit(solution)/shard_map/ppermute | solution.py:76
  3.7 17.4 %collective-permute-start.1 = (bf16[128,2048]{1,0:T(8,128)(2,1)}, bf16[128,2048]{1,0:T(8,128)(2,1)}, u32[]{:S(2)}, u32[]{:S(2)}) collective-permute-start(bf16[128,2048]{1,0:T(8,128)(2,1)} %bitcast.278), channel_id=1, source_target_pairs={{0,8},{4,12},{8,16},{12,20},{16,24},{20,28},{24,0},{28,4},{1,9},{5... | collective-permute-start | bytes 1572872 | tf_op jit(solution)/shard_map/ppermute | solution.py:76
  21.1 26.1 %collective-permute-start.4 = (bf16[128,2048]{1,0:T(8,128)(2,1)}, bf16[128,2048]{1,0:T(8,128)(2,1)}, u32[]{:S(2)}, u32[]{:S(2)}) collective-permute-start(bf16[128,2048]{1,0:T(8,128)(2,1)} %collective-permute-done.1), channel_id=1, source_target_pairs={{0,4},{4,0},{8,12},{12,8},{16,20},{20,16},{24,28},{28,24},{1,5},{5... | collective-permute-start | bytes 1572872 | tf_op jit(solution)/shard_map/ppermute | solution.py:76
  22.9 24.3 %collective-permute-start.5 = (bf16[128,2048]{1,0:T(8,128)(2,1)}, bf16[128,2048]{1,0:T(8,128)(2,1)}, u32[]{:S(2)}, u32[]{:S(2)}) collective-permute-start(bf16[128,2048]{1,0:T(8,128)(2,1)} %collective-permute-done.1), channel_id=1, source_target_pairs={{0,8},{4,12},{8,16},{12,20},{16,24},{20,28},{24,0},{28,4},{1,9},{5... | collective-permute-start | bytes 1572872 | tf_op jit(solution)/shard_map/ppermute | solution.py:76
  26.3 16.0 %collective-permute-start.7 = (bf16[2,80,384]{2,1,0:T(8,128)(2,1)}, bf16[2,80,384]{2,1,0:T(8,128)(2,1)S(1)}, u32[]{:S(2)}, u32[]{:S(2)}) collective-permute-start(bf16[2,80,384]{2,1,0:T(8,128)(2,1)} %get-tuple-element.691), channel_id=1, source_target_pairs={{0,8},{4,12},{8,16},{12,20},{16,24},{20,28},{24,0},{28,4},{1,9},{5... | collective-permute-start | bytes 368648 | tf_op jit(solution)/shard_map/ppermute | solution.py:76
  29.0 16.6 %collective-permute-start.8 = (bf16[2,80,384]{2,1,0:T(8,128)(2,1)}, bf16[2,80,384]{2,1,0:T(8,128)(2,1)S(1)}, u32[]{:S(2)}, u32[]{:S(2)}) collective-permute-start(bf16[2,80,384]{2,1,0:T(8,128)(2,1)} %get-tuple-element.690), channel_id=1, source_target_pairs={{0,16},{4,20},{8,24},{12,28},{16,0},{20,4},{24,8},{28,12},{1,17},{... | collective-permute-start | bytes 368648 | tf_op jit(solution)/shard_map/ppermute | solution.py:76
  30.3 17.0 %collective-permute-start.6 = (bf16[64,2048]{1,0:T(8,128)(2,1)S(1)}, bf16[64,2048]{1,0:T(8,128)(2,1)S(1)}, u32[]{:S(2)}, u32[]{:S(2)}) collective-permute-start(bf16[64,2048]{1,0:T(8,128)(2,1)S(1)} %copy-done.62), channel_id=1, source_target_pairs={{0,2},{1,3},{2,0},{3,1},{4,6},{5,7},{6,4},{7,5},{8,10},{9,11},{10,... | collective-permute-start | bytes 786440 | tf_op jit(solution)/shard_map/ppermute | solution.py:80
  62.7 19.3 %collective-permute-start.17 = (bf16[128,2048]{1,0:T(8,128)(2,1)}, bf16[128,2048]{1,0:T(8,128)(2,1)}, u32[]{:S(2)}, u32[]{:S(2)}) collective-permute-start(bf16[128,2048]{1,0:T(8,128)(2,1)} %collective-permute-done.11), channel_id=1, source_target_pairs={{0,4},{4,0},{8,12},{12,8},{16,20},{20,16},{24,28},{28,24},{1,5},{5... | collective-permute-start | bytes 1572872 | tf_op jit(solution)/shard_map/ppermute | solution.py:76
  64.2 17.8 %collective-permute-start.18 = (bf16[128,2048]{1,0:T(8,128)(2,1)}, bf16[128,2048]{1,0:T(8,128)(2,1)}, u32[]{:S(2)}, u32[]{:S(2)}) collective-permute-start(bf16[128,2048]{1,0:T(8,128)(2,1)} %get-tuple-element.342), channel_id=1, source_target_pairs={{0,2},{1,3},{2,0},{3,1},{4,6},{5,7},{6,4},{7,5},{8,10},{9,11},{10,... | collective-permute-start | bytes 1572872 | tf_op jit(solution)/shard_map/ppermute | solution.py:80
  70.7 24.5 %collective-permute-start.19 = (bf16[64,2048]{1,0:T(8,128)(2,1)}, bf16[64,2048]{1,0:T(8,128)(2,1)}, u32[]{:S(2)}, u32[]{:S(2)}) collective-permute-start(bf16[64,2048]{1,0:T(8,128)(2,1)} %get-tuple-element.672), channel_id=1, source_target_pairs={{0,8},{4,12},{8,16},{12,20},{16,24},{20,28},{24,0},{28,4},{1,9},{5... | collective-permute-start | bytes 786440 | tf_op jit(solution)/shard_map/ppermute | solution.py:76
  70.7 25.2 %collective-permute-start.20 = (bf16[64,2048]{1,0:T(8,128)(2,1)}, bf16[64,2048]{1,0:T(8,128)(2,1)}, u32[]{:S(2)}, u32[]{:S(2)}) collective-permute-start(bf16[64,2048]{1,0:T(8,128)(2,1)} %get-tuple-element.671), channel_id=1, source_target_pairs={{0,24},{4,28},{8,0},{12,4},{16,8},{20,12},{24,16},{28,20},{1,25},{... | collective-permute-start | bytes 786440 | tf_op jit(solution)/shard_map/ppermute | solution.py:76
  74.6 22.9 %collective-permute-start.21 = (bf16[64,2048]{1,0:T(8,128)(2,1)}, bf16[64,2048]{1,0:T(8,128)(2,1)}, u32[]{:S(2)}, u32[]{:S(2)}) collective-permute-start(bf16[64,2048]{1,0:T(8,128)(2,1)} %get-tuple-element.670), channel_id=1, source_target_pairs={{0,16},{4,20},{8,24},{12,28},{16,0},{20,4},{24,8},{28,12},{1,17},{... | collective-permute-start | bytes 786440 | tf_op jit(solution)/shard_map/ppermute | solution.py:76
  93.5 23.9 %collective-permute-start.22 = (bf16[128,2048]{1,0:T(8,128)(2,1)S(1)}, bf16[128,2048]{1,0:T(8,128)(2,1)S(1)}, u32[]{:S(2)}, u32[]{:S(2)}) collective-permute-start(bf16[128,2048]{1,0:T(8,128)(2,1)S(1)} %slice.860), channel_id=1, source_target_pairs={{0,4},{4,0},{8,12},{12,8},{16,20},{20,16},{24,28},{28,24},{1,5},{5... | collective-permute-start | bytes 1572872 | tf_op jit(solution)/shard_map/ppermute | solution.py:76
  94.5 23.1 %collective-permute-start.23 = (bf16[256,2048]{1,0:T(8,128)(2,1)S(1)}, bf16[256,2048]{1,0:T(8,128)(2,1)S(1)}, u32[]{:S(2)}, u32[]{:S(2)}) collective-permute-start(bf16[256,2048]{1,0:T(8,128)(2,1)S(1)} %copy-done.16), channel_id=1, source_target_pairs={{0,1},{1,0},{2,3},{3,2},{4,5},{5,4},{6,7},{7,6},{8,9},{9,8},{10,11... | collective-permute-start | bytes 3145736 | tf_op jit(solution)/shard_map/ppermute | solution.py:80
  95.2 22.3 %collective-permute-start.24 = (bf16[64,2048]{1,0:T(8,128)(2,1)S(1)}, bf16[64,2048]{1,0:T(8,128)(2,1)S(1)}, u32[]{:S(2)}, u32[]{:S(2)}) collective-permute-start(bf16[64,2048]{1,0:T(8,128)(2,1)S(1)} %get-tuple-element.669), channel_id=1, source_target_pairs={{0,4},{4,0},{8,12},{12,8},{16,20},{20,16},{24,28},{28,24},{1,5},{5... | collective-permute-start | bytes 786440 | tf_op jit(solution)/shard_map/ppermute | solution.py:76
  95.9 21.6 %collective-permute-start.25 = (bf16[64,2048]{1,0:T(8,128)(2,1)S(1)}, bf16[64,2048]{1,0:T(8,128)(2,1)S(1)}, u32[]{:S(2)}, u32[]{:S(2)}) collective-permute-start(bf16[64,2048]{1,0:T(8,128)(2,1)S(1)} %get-tuple-element.668), channel_id=1, source_target_pairs={{0,12},{4,8},{8,20},{12,16},{16,28},{20,24},{24,4},{28,0},{1,13},{... | collective-permute-start | bytes 786440 | tf_op jit(solution)/shard_map/ppermute | solution.py:76
  98.6 18.9 %collective-permute-start.26 = (bf16[2,64,2048]{2,1,0:T(8,128)(2,1)S(1)}, bf16[2,64,2048]{2,1,0:T(8,128)(2,1)S(1)}, u32[]{:S(2)}, u32[]{:S(2)}) collective-permute-start(bf16[2,64,2048]{2,1,0:T(8,128)(2,1)S(1)} %pad_maximum_fusion.10.refs_0_), channel_id=1, source_target_pairs={{0,2},{1,3},{2,0},{3,1},{4,6},{5,7},{6,4},{7,5},{8,10},{9,11},{10,... | collective-permute-start | bytes 1572872 | tf_op jit(solution)/shard_map/ppermute | solution.py:80
  117.5 20.9 %collective-permute-start.27 = (bf16[128,2048]{1,0:T(8,128)(2,1)S(1)}, bf16[128,2048]{1,0:T(8,128)(2,1)S(1)}, u32[]{:S(2)}, u32[]{:S(2)}) collective-permute-start(bf16[128,2048]{1,0:T(8,128)(2,1)S(1)} %slice.861), channel_id=1, source_target_pairs={{0,4},{4,0},{8,12},{12,8},{16,20},{20,16},{24,28},{28,24},{1,5},{5... | collective-permute-start | bytes 1572872 | tf_op jit(solution)/shard_map/ppermute | solution.py:76
  120.3 18.1 %collective-permute-start.28 = (bf16[128,2048]{1,0:T(8,128)(2,1)S(1)}, bf16[128,2048]{1,0:T(8,128)(2,1)S(1)}, u32[]{:S(2)}, u32[]{:S(2)}) collective-permute-start(bf16[128,2048]{1,0:T(8,128)(2,1)S(1)} %fusion.19), channel_id=1, source_target_pairs={{0,8},{4,12},{8,16},{12,20},{16,24},{20,28},{24,0},{28,4},{1,9},{5... | collective-permute-start | bytes 1572872 | tf_op jit(solution)/shard_map/ppermute | solution.py:76
  121.9 16.5 %collective-permute-start.30 = (bf16[2,64,2048]{2,1,0:T(8,128)(2,1)S(1)}, bf16[2,64,2048]{2,1,0:T(8,128)(2,1)S(1)}, u32[]{:S(2)}, u32[]{:S(2)}) collective-permute-start(bf16[2,64,2048]{2,1,0:T(8,128)(2,1)S(1)} %pad_maximum_fusion.10.refs_0_), channel_id=1, source_target_pairs={{0,1},{1,0},{2,3},{3,2},{4,5},{5,4},{6,7},{7,6},{8,9},{9,8},{10,11... | collective-permute-start | bytes 1572872 | tf_op jit(solution)/shard_map/ppermute | solution.py:80
  140.0 25.3 %collective-permute-start.33 = (bf16[128,2048]{1,0:T(8,128)(2,1)S(1)}, bf16[128,2048]{1,0:T(8,128)(2,1)S(1)}, u32[]{:S(2)}, u32[]{:S(2)}) collective-permute-start(bf16[128,2048]{1,0:T(8,128)(2,1)S(1)} %slice.862), channel_id=1, source_target_pairs={{0,4},{4,0},{8,12},{12,8},{16,20},{20,16},{24,28},{28,24},{1,5},{5... | collective-permute-start | bytes 1572872 | tf_op jit(solution)/shard_map/ppermute | solution.py:76
  140.7 24.6 %collective-permute-start.38 = (bf16[2,64,2048]{2,1,0:T(8,128)(2,1)S(1)}, bf16[2,64,2048]{2,1,0:T(8,128)(2,1)S(1)}, u32[]{:S(2)}, u32[]{:S(2)}) collective-permute-start(bf16[2,64,2048]{2,1,0:T(8,128)(2,1)S(1)} %pad_maximum_fusion.12.refs_8_), channel_id=1, source_target_pairs={{0,2},{1,3},{2,0},{3,1},{4,6},{5,7},{6,4},{7,5},{8,10},{9,11},{10,... | collective-permute-start | bytes 1572872 | tf_op jit(solution)/shard_map/ppermute | solution.py:80
  142.1 22.6 %collective-permute-start.35 = (bf16[64,2048]{1,0:T(8,128)(2,1)S(1)}, bf16[64,2048]{1,0:T(8,128)(2,1)S(1)}, u32[]{:S(2)}, u32[]{:S(2)}) collective-permute-start(bf16[64,2048]{1,0:T(8,128)(2,1)S(1)} %slice_bitcast_fusion.2), channel_id=1, source_target_pairs={{0,20},{4,16},{8,28},{12,24},{16,4},{20,0},{24,12},{28,8},{1,21},{... | collective-permute-start | bytes 786440 | tf_op jit(solution)/shard_map/ppermute | solution.py:76
  142.8 22.5 %collective-permute-start.34 = (bf16[128,2048]{1,0:T(8,128)(2,1)S(1)}, bf16[128,2048]{1,0:T(8,128)(2,1)S(1)}, u32[]{:S(2)}, u32[]{:S(2)}) collective-permute-start(bf16[128,2048]{1,0:T(8,128)(2,1)S(1)} %fusion.18), channel_id=1, source_target_pairs={{0,8},{4,12},{8,16},{12,20},{16,24},{20,28},{24,0},{28,4},{1,9},{5... | collective-permute-start | bytes 1572872 | tf_op jit(solution)/shard_map/ppermute | solution.py:76
  144.4 20.9 %collective-permute-start.36 = (bf16[2,64,2048]{2,1,0:T(8,128)(2,1)S(1)}, bf16[2,64,2048]{2,1,0:T(8,128)(2,1)S(1)}, u32[]{:S(2)}, u32[]{:S(2)}) collective-permute-start(bf16[2,64,2048]{2,1,0:T(8,128)(2,1)S(1)} %pad_maximum_fusion.11.refs_4_), channel_id=1, source_target_pairs={{0,1},{1,0},{2,3},{3,2},{4,5},{5,4},{6,7},{7,6},{8,9},{9,8},{10,11... | collective-permute-start | bytes 1572872 | tf_op jit(solution)/shard_map/ppermute | solution.py:80
  167.5 18.0 %collective-permute-start.39 = (bf16[128,2048]{1,0:T(8,128)(2,1)S(1)}, bf16[128,2048]{1,0:T(8,128)(2,1)S(1)}, u32[]{:S(2)}, u32[]{:S(2)}) collective-permute-start(bf16[128,2048]{1,0:T(8,128)(2,1)S(1)} %slice.863), channel_id=1, source_target_pairs={{0,4},{4,0},{8,12},{12,8},{16,20},{20,16},{24,28},{28,24},{1,5},{5... | collective-permute-start | bytes 1572872 | tf_op jit(solution)/shard_map/ppermute | solution.py:76
  170.2 15.3 %collective-permute-start.40 = (bf16[128,2048]{1,0:T(8,128)(2,1)S(1)}, bf16[128,2048]{1,0:T(8,128)(2,1)S(1)}, u32[]{:S(2)}, u32[]{:S(2)}) collective-permute-start(bf16[128,2048]{1,0:T(8,128)(2,1)S(1)} %fusion.17), channel_id=1, source_target_pairs={{0,8},{4,12},{8,16},{12,20},{16,24},{20,28},{24,0},{28,4},{1,9},{5... | collective-permute-start | bytes 1572872 | tf_op jit(solution)/shard_map/ppermute | solution.py:76
  170.2 15.2 %collective-permute-start.41 = (bf16[2,64,2048]{2,1,0:T(8,128)(2,1)S(1)}, bf16[2,64,2048]{2,1,0:T(8,128)(2,1)S(1)}, u32[]{:S(2)}, u32[]{:S(2)}) collective-permute-start(bf16[2,64,2048]{2,1,0:T(8,128)(2,1)S(1)} %pad_maximum_fusion.12.refs_8_), channel_id=1, source_target_pairs={{0,1},{1,0},{2,3},{3,2},{4,5},{5,4},{6,7},{7,6},{8,9},{9,8},{10,11... | collective-permute-start | bytes 1572872 | tf_op jit(solution)/shard_map/ppermute | solution.py:80
  170.3 15.9 %collective-permute-start.42 = (bf16[2,64,2048]{2,1,0:T(8,128)(2,1)S(1)}, bf16[2,64,2048]{2,1,0:T(8,128)(2,1)S(1)}, u32[]{:S(2)}, u32[]{:S(2)}) collective-permute-start(bf16[2,64,2048]{2,1,0:T(8,128)(2,1)S(1)} %collective-permute-done.38.refs_10_), channel_id=1, source_target_pairs={{0,1},{1,0},{2,3},{3,2},{4,5},{5,4},{6,7},{7,6},{8,9},{9,8},{10,11... | collective-permute-start | bytes 1572872 | tf_op jit(solution)/shard_map/ppermute | solution.py:80
  204.3 17.0 %collective-permute-start.49 = (bf16[128,2048]{1,0:T(8,128)(2,1)}, bf16[128,2048]{1,0:T(8,128)(2,1)S(1)}, u32[]{:S(2)}, u32[]{:S(2)}) collective-permute-start(bf16[128,2048]{1,0:T(8,128)(2,1)} %collective-permute-done.45), channel_id=1, source_target_pairs={{0,4},{4,0},{8,12},{12,8},{16,20},{20,16},{24,28},{28,24},{1,5},{5... | collective-permute-start | bytes 1572872 | tf_op jit(solution)/shard_map/ppermute | solution.py:76
  205.4 15.9 %collective-permute-start.50 = (bf16[128,2048]{1,0:T(8,128)(2,1)}, bf16[128,2048]{1,0:T(8,128)(2,1)S(1)}, u32[]{:S(2)}, u32[]{:S(2)}) collective-permute-start(bf16[128,2048]{1,0:T(8,128)(2,1)} %collective-permute-done.45), channel_id=1, source_target_pairs={{0,8},{4,12},{8,16},{12,20},{16,24},{20,28},{24,0},{28,4},{1,9},{5... | collective-permute-start | bytes 1572872 | tf_op jit(solution)/shard_map/ppermute | solution.py:76
  229.1 19.5 %collective-permute-start.51 = (bf16[128,2048]{1,0:T(8,128)(2,1)S(1)}, bf16[128,2048]{1,0:T(8,128)(2,1)S(1)}, u32[]{:S(2)}, u32[]{:S(2)}) collective-permute-start(bf16[128,2048]{1,0:T(8,128)(2,1)S(1)} %collective-permute-done.50), channel_id=1, source_target_pairs={{0,4},{4,0},{8,12},{12,8},{16,20},{20,16},{24,28},{28,24},{1,5},{5... | collective-permute-start | bytes 1572872 | tf_op jit(solution)/shard_map/ppermute | solution.py:76
  230.2 18.4 %collective-permute-start.52 = (bf16[128,2048]{1,0:T(8,128)(2,1)S(1)}, bf16[128,2048]{1,0:T(8,128)(2,1)S(1)}, u32[]{:S(2)}, u32[]{:S(2)}) collective-permute-start(bf16[128,2048]{1,0:T(8,128)(2,1)S(1)} %collective-permute-done.50), channel_id=1, source_target_pairs={{0,8},{4,12},{8,16},{12,20},{16,24},{20,28},{24,0},{28,4},{1,9},{5... | collective-permute-start | bytes 1572872 | tf_op jit(solution)/shard_map/ppermute | solution.py:76
  241.4 17.2 %collective-permute-start.56 = (bf16[128,2048]{1,0:T(8,128)(2,1)S(1)}, bf16[128,2048]{1,0:T(8,128)(2,1)S(1)}, u32[]{:S(2)}, u32[]{:S(2)}) collective-permute-start(bf16[128,2048]{1,0:T(8,128)(2,1)S(1)} %fusion.15), channel_id=1, source_target_pairs={{0,8},{4,12},{8,16},{12,20},{16,24},{20,28},{24,0},{28,4},{1,9},{5... | collective-permute-start | bytes 1572872 | tf_op jit(solution)/shard_map/ppermute | solution.py:76
  253.8 20.4 %collective-permute-start.53 = (bf16[128,2048]{1,0:T(8,128)(2,1)S(1)}, bf16[128,2048]{1,0:T(8,128)(2,1)S(1)}, u32[]{:S(2)}, u32[]{:S(2)}) collective-permute-start(bf16[128,2048]{1,0:T(8,128)(2,1)S(1)} %collective-permute-done.52), channel_id=1, source_target_pairs={{0,4},{4,0},{8,12},{12,8},{16,20},{20,16},{24,28},{28,24},{1,5},{5... | collective-permute-start | bytes 1572872 | tf_op jit(solution)/shard_map/ppermute | solution.py:76
  306.7 15.4 %collective-permute-start.64 = (bf16[128,1024]{1,0:T(8,128)(2,1)S(1)}, bf16[128,1024]{1,0:T(8,128)(2,1)S(1)}, u32[]{:S(2)}, u32[]{:S(2)}) collective-permute-start(bf16[128,1024]{1,0:T(8,128)(2,1)S(1)} %get-tuple-element.688), channel_id=1, source_target_pairs={{0,8},{4,12},{8,16},{12,20},{16,24},{20,28},{24,0},{28,4},{1,9},{5... | collective-permute-start | bytes 786440 | tf_op jit(solution)/shard_map/ppermute | solution.py:76
  329.0 15.7 %collective-permute-start.67 = (bf16[128,1024]{1,0:T(8,128)(2,1)}, bf16[128,1024]{1,0:T(8,128)(2,1)}, u32[]{:S(2)}, u32[]{:S(2)}) collective-permute-start(bf16[128,1024]{1,0:T(8,128)(2,1)} %collective-permute-done.66), channel_id=1, source_target_pairs={{0,4},{4,0},{8,12},{12,8},{16,20},{20,16},{24,28},{28,24},{1,5},{5... | collective-permute-start | bytes 786440 | tf_op jit(solution)/shard_map/ppermute | solution.py:76
  331.1 15.6 %collective-permute-start.68 = (bf16[128,1024]{1,0:T(8,128)(2,1)}, bf16[128,1024]{1,0:T(8,128)(2,1)}, u32[]{:S(2)}, u32[]{:S(2)}) collective-permute-start(bf16[128,1024]{1,0:T(8,128)(2,1)} %collective-permute-done.66), channel_id=1, source_target_pairs={{0,8},{4,12},{8,16},{12,20},{16,24},{20,28},{24,0},{28,4},{1,9},{5... | collective-permute-start | bytes 786440 | tf_op jit(solution)/shard_map/ppermute | solution.py:76
  344.7 15.1 %collective-permute-start.75 = (bf16[128,1024]{1,0:T(8,128)(2,1)S(1)}, bf16[128,1024]{1,0:T(8,128)(2,1)}, u32[]{:S(2)}, u32[]{:S(2)}) collective-permute-start(bf16[128,1024]{1,0:T(8,128)(2,1)S(1)} %get-tuple-element.676), channel_id=1, source_target_pairs={{0,4},{4,0},{8,12},{12,8},{16,20},{20,16},{24,28},{28,24},{1,5},{5... | collective-permute-start | bytes 786440 | tf_op jit(solution)/shard_map/ppermute | solution.py:76
  346.6 18.6 %collective-permute-start.73 = (bf16[128,1024]{1,0:T(8,128)(2,1)}, bf16[128,1024]{1,0:T(8,128)(2,1)}, u32[]{:S(2)}, u32[]{:S(2)}) collective-permute-start(bf16[128,1024]{1,0:T(8,128)(2,1)} %collective-permute-done.68), channel_id=1, source_target_pairs={{0,4},{4,0},{8,12},{12,8},{16,20},{20,16},{24,28},{28,24},{1,5},{5... | collective-permute-start | bytes 786440 | tf_op jit(solution)/shard_map/ppermute | solution.py:76
  346.8 20.7 %collective-permute-start.74 = (bf16[128,1024]{1,0:T(8,128)(2,1)}, bf16[128,1024]{1,0:T(8,128)(2,1)}, u32[]{:S(2)}, u32[]{:S(2)}) collective-permute-start(bf16[128,1024]{1,0:T(8,128)(2,1)} %collective-permute-done.72), channel_id=1, source_target_pairs={{0,4},{4,0},{8,12},{12,8},{16,20},{20,16},{24,28},{28,24},{1,5},{5... | collective-permute-start | bytes 786440 | tf_op jit(solution)/shard_map/ppermute | solution.py:76
  359.6 15.5 %collective-permute-start.83 = (bf16[128,1024]{1,0:T(8,128)(2,1)}, bf16[128,1024]{1,0:T(8,128)(2,1)S(1)}, u32[]{:S(2)}, u32[]{:S(2)}) collective-permute-start(bf16[128,1024]{1,0:T(8,128)(2,1)} %get-tuple-element.436), channel_id=1, source_target_pairs={{0,4},{4,0},{8,12},{12,8},{16,20},{20,16},{24,28},{28,24},{1,5},{5... | collective-permute-start | bytes 786440 | tf_op jit(solution)/shard_map/ppermute | solution.py:76
  387.6 19.3 %collective-permute-start.89 = (bf16[2,2,64,2048]{3,2,1,0:T(8,128)(2,1)S(1)}, bf16[2,2,64,2048]{3,2,1,0:T(8,128)(2,1)S(1)}, u32[]{:S(2)}, u32[]{:S(2)}) collective-permute-start(bf16[2,2,64,2048]{3,2,1,0:T(8,128)(2,1)S(1)} %get-tuple-element.463), channel_id=1, source_target_pairs={{0,1},{1,0},{2,3},{3,2},{4,5},{5,4},{6,7},{7,6},{8,9},{9,8},{10,11... | collective-permute-start | bytes 3145736 | tf_op jit(solution)/shard_map/ppermute | solution.py:80
  388.8 18.1 %collective-permute-start.87 = (bf16[128,1024]{1,0:T(8,128)(2,1)S(1)}, bf16[128,1024]{1,0:T(8,128)(2,1)S(1)}, u32[]{:S(2)}, u32[]{:S(2)}) collective-permute-start(bf16[128,1024]{1,0:T(8,128)(2,1)S(1)} %get-tuple-element.451), channel_id=1, source_target_pairs={{0,4},{4,0},{8,12},{12,8},{16,20},{20,16},{24,28},{28,24},{1,5},{5... | collective-permute-start | bytes 786440 | tf_op jit(solution)/shard_map/ppermute | solution.py:76
  391.0 15.9 %collective-permute-start.88 = (bf16[128,1024]{1,0:T(8,128)(2,1)S(1)}, bf16[128,1024]{1,0:T(8,128)(2,1)S(1)}, u32[]{:S(2)}, u32[]{:S(2)}) collective-permute-start(bf16[128,1024]{1,0:T(8,128)(2,1)S(1)} %get-tuple-element.663), channel_id=1, source_target_pairs={{0,8},{4,12},{8,16},{12,20},{16,24},{20,28},{24,0},{28,4},{1,9},{5... | collective-permute-start | bytes 786440 | tf_op jit(solution)/shard_map/ppermute | solution.py:76
  409.2 15.6 %collective-permute-start.90 = (bf16[128,2048]{1,0:T(8,128)(2,1)S(1)}, bf16[128,2048]{1,0:T(8,128)(2,1)S(1)}, u32[]{:S(2)}, u32[]{:S(2)}) collective-permute-start(bf16[128,2048]{1,0:T(8,128)(2,1)S(1)} %get-tuple-element.640), channel_id=1, source_target_pairs={{0,4},{4,0},{8,12},{12,8},{16,20},{20,16},{24,28},{28,24},{1,5},{5... | collective-permute-start | bytes 1572872 | tf_op jit(solution)/shard_map/ppermute | solution.py:76
  409.5 15.3 %collective-permute-start.91 = (bf16[128,2048]{1,0:T(8,128)(2,1)S(1)}, bf16[128,2048]{1,0:T(8,128)(2,1)S(1)}, u32[]{:S(2)}, u32[]{:S(2)}) collective-permute-start(bf16[128,2048]{1,0:T(8,128)(2,1)S(1)} %get-tuple-element.640), channel_id=1, source_target_pairs={{0,8},{4,12},{8,16},{12,20},{16,24},{20,28},{24,0},{28,4},{1,9},{5... | collective-permute-start | bytes 1572872 | tf_op jit(solution)/shard_map/ppermute | solution.py:76
  424.8 17.2 %collective-permute-start.95 = (bf16[128,2048]{1,0:T(8,128)(2,1)S(1)}, bf16[128,2048]{1,0:T(8,128)(2,1)S(1)}, u32[]{:S(2)}, u32[]{:S(2)}) collective-permute-start(bf16[128,2048]{1,0:T(8,128)(2,1)S(1)} %collective-permute-done.91), channel_id=1, source_target_pairs={{0,4},{4,0},{8,12},{12,8},{16,20},{20,16},{24,28},{28,24},{1,5},{5... | collective-permute-start | bytes 1572872 | tf_op jit(solution)/shard_map/ppermute | solution.py:76
  425.9 16.1 %collective-permute-start.96 = (bf16[128,2048]{1,0:T(8,128)(2,1)S(1)}, bf16[128,2048]{1,0:T(8,128)(2,1)}, u32[]{:S(2)}, u32[]{:S(2)}) collective-permute-start(bf16[128,2048]{1,0:T(8,128)(2,1)S(1)} %collective-permute-done.91), channel_id=1, source_target_pairs={{0,8},{4,12},{8,16},{12,20},{16,24},{20,28},{24,0},{28,4},{1,9},{5... | collective-permute-start | bytes 1572872 | tf_op jit(solution)/shard_map/ppermute | solution.py:76
  442.0 16.4 %collective-permute-start.100 = (bf16[128,2048]{1,0:T(8,128)(2,1)}, bf16[128,2048]{1,0:T(8,128)(2,1)}, u32[]{:S(2)}, u32[]{:S(2)}) collective-permute-start(bf16[128,2048]{1,0:T(8,128)(2,1)} %collective-permute-done.96), channel_id=1, source_target_pairs={{0,4},{4,0},{8,12},{12,8},{16,20},{20,16},{24,28},{28,24},{1,5},{5... | collective-permute-start | bytes 1572872 | tf_op jit(solution)/shard_map/ppermute | solution.py:76
  442.4 16.4 %collective-permute-start.101 = (bf16[128,2048]{1,0:T(8,128)(2,1)}, bf16[128,2048]{1,0:T(8,128)(2,1)}, u32[]{:S(2)}, u32[]{:S(2)}) collective-permute-start(bf16[128,2048]{1,0:T(8,128)(2,1)} %collective-permute-done.96), channel_id=1, source_target_pairs={{0,8},{4,12},{8,16},{12,20},{16,24},{20,28},{24,0},{28,4},{1,9},{5... | collective-permute-start | bytes 1572872 | tf_op jit(solution)/shard_map/ppermute | solution.py:76
  458.9 20.8 %collective-permute-start.106 = (bf16[2,1,256,2048]{3,2,1,0:T(8,128)(2,1)}, bf16[2,1,256,2048]{3,2,1,0:T(8,128)(2,1)S(1)}, u32[]{:S(2)}, u32[]{:S(2)}) collective-permute-start(bf16[2,1,256,2048]{3,2,1,0:T(8,128)(2,1)} %get-tuple-element.516), channel_id=1, source_target_pairs={{0,1},{1,0},{2,3},{3,2},{4,5},{5,4},{6,7},{7,6},{8,9},{9,8},{10,11... | collective-permute-start | bytes 6291464 | tf_op jit(solution)/shard_map/ppermute | solution.py:80
  460.1 19.5 %collective-permute-start.105 = (bf16[128,2048]{1,0:T(8,128)(2,1)}, bf16[128,2048]{1,0:T(8,128)(2,1)S(1)}, u32[]{:S(2)}, u32[]{:S(2)}) collective-permute-start(bf16[128,2048]{1,0:T(8,128)(2,1)} %collective-permute-done.101), channel_id=1, source_target_pairs={{0,4},{4,0},{8,12},{12,8},{16,20},{20,16},{24,28},{28,24},{1,5},{5... | collective-permute-start | bytes 1572872 | tf_op jit(solution)/shard_map/ppermute | solution.py:76
  461.9 18.4 %collective-permute-start.110 = (bf16[64,2048]{1,0:T(8,128)(2,1)S(1)}, bf16[64,2048]{1,0:T(8,128)(2,1)S(1)}, u32[]{:S(2)}, u32[]{:S(2)}) collective-permute-start(bf16[64,2048]{1,0:T(8,128)(2,1)S(1)} %get-tuple-element.525), channel_id=1, source_target_pairs={{0,24},{4,28},{8,0},{12,4},{16,8},{20,12},{24,16},{28,20},{1,25},{... | collective-permute-start | bytes 786440 | tf_op jit(solution)/shard_map/ppermute | solution.py:76
  481.5 15.0 %collective-permute-start.113 = (bf16[128,2048]{1,0:T(8,128)(2,1)S(1)}, bf16[128,2048]{1,0:T(8,128)(2,1)S(1)}, u32[]{:S(2)}, u32[]{:S(2)}) collective-permute-start(bf16[128,2048]{1,0:T(8,128)(2,1)S(1)} %get-tuple-element.673), channel_id=1, source_target_pairs={{0,2},{1,3},{2,0},{3,1},{4,6},{5,7},{6,4},{7,5},{8,10},{9,11},{10,... | collective-permute-start | bytes 1572872 | tf_op jit(solution)/shard_map/ppermute | solution.py:80
  496.5 15.8 %collective-permute-start.116 = (bf16[128,2048]{1,0:T(8,128)(2,1)S(1)}, bf16[128,2048]{1,0:T(8,128)(2,1)S(1)}, u32[]{:S(2)}, u32[]{:S(2)}) collective-permute-start(bf16[128,2048]{1,0:T(8,128)(2,1)S(1)} %get-tuple-element.554), channel_id=1, source_target_pairs={{0,2},{1,3},{2,0},{3,1},{4,6},{5,7},{6,4},{7,5},{8,10},{9,11},{10,... | collective-permute-start | bytes 1572872 | tf_op jit(solution)/shard_map/ppermute | solution.py:80
  497.0 15.3 %collective-permute-start.115 = (bf16[64,2048]{1,0:T(8,128)(2,1)S(1)}, bf16[64,2048]{1,0:T(8,128)(2,1)S(1)}, u32[]{:S(2)}, u32[]{:S(2)}) collective-permute-start(bf16[64,2048]{1,0:T(8,128)(2,1)S(1)} %get-tuple-element.552), channel_id=1, source_target_pairs={{0,28},{4,24},{8,4},{12,0},{16,12},{20,8},{24,20},{28,16},{1,29},{... | collective-permute-start | bytes 786440 | tf_op jit(solution)/shard_map/ppermute | solution.py:76
  515.1 18.4 %collective-permute-start.117 = (bf16[128,2048]{1,0:T(8,128)(2,1)S(1)}, bf16[128,2048]{1,0:T(8,128)(2,1)S(1)}, u32[]{:S(2)}, u32[]{:S(2)}) collective-permute-start(bf16[128,2048]{1,0:T(8,128)(2,1)S(1)} %slice.855), channel_id=1, source_target_pairs={{0,4},{4,0},{8,12},{12,8},{16,20},{20,16},{24,28},{28,24},{1,5},{5... | collective-permute-start | bytes 1572872 | tf_op jit(solution)/shard_map/ppermute | solution.py:76
  533.5 17.8 %collective-permute-start.123 = (bf16[2,8,64,384]{3,2,1,0:T(8,128)(2,1)S(1)}, bf16[2,8,64,384]{3,2,1,0:T(8,128)(2,1)S(1)}, u32[]{:S(2)}, u32[]{:S(2)}) collective-permute-start(bf16[2,8,64,384]{3,2,1,0:T(8,128)(2,1)S(1)} %get-tuple-element.589), channel_id=1, source_target_pairs={{0,1},{1,0},{2,3},{3,2},{4,5},{5,4},{6,7},{7,6},{8,9},{9,8},{10,11... | collective-permute-start | bytes 2359304 | tf_op jit(solution)/shard_map/ppermute | solution.py:80
  533.6 17.6 %collective-permute-start.120 = (bf16[128,2048]{1,0:T(8,128)(2,1)}, bf16[128,2048]{1,0:T(8,128)(2,1)S(1)}, u32[]{:S(2)}, u32[]{:S(2)}) collective-permute-start(bf16[128,2048]{1,0:T(8,128)(2,1)} %slice.852), channel_id=1, source_target_pairs={{0,4},{4,0},{8,12},{12,8},{16,20},{20,16},{24,28},{28,24},{1,5},{5... | collective-permute-start | bytes 1572872 | tf_op jit(solution)/shard_map/ppermute | solution.py:76
  535.2 16.1 %collective-permute-start.121 = (bf16[128,2048]{1,0:T(8,128)(2,1)S(1)}, bf16[128,2048]{1,0:T(8,128)(2,1)S(1)}, u32[]{:S(2)}, u32[]{:S(2)}) collective-permute-start(bf16[128,2048]{1,0:T(8,128)(2,1)S(1)} %fusion.12), channel_id=1, source_target_pairs={{0,8},{4,12},{8,16},{12,20},{16,24},{20,28},{24,0},{28,4},{1,9},{5... | collective-permute-start | bytes 1572872 | tf_op jit(solution)/shard_map/ppermute | solution.py:76
  552.2 16.6 %collective-permute-start.127 = (bf16[8,64,384]{2,1,0:T(8,128)(2,1)}, bf16[8,64,384]{2,1,0:T(8,128)(2,1)}, u32[]{:S(2)}, u32[]{:S(2)}) collective-permute-start(bf16[8,64,384]{2,1,0:T(8,128)(2,1)} %fusion.45), channel_id=1, source_target_pairs={{0,2},{1,3},{2,0},{3,1},{4,6},{5,7},{6,4},{7,5},{8,10},{9,11},{10,... | collective-permute-start | bytes 1179656 | tf_op jit(solution)/shard_map/ppermute | solution.py:80
  554.7 15.4 %collective-permute-start.125 = (bf16[128,2048]{1,0:T(8,128)(2,1)}, bf16[128,2048]{1,0:T(8,128)(2,1)}, u32[]{:S(2)}, u32[]{:S(2)}) collective-permute-start(bf16[128,2048]{1,0:T(8,128)(2,1)} %fusion.11), channel_id=1, source_target_pairs={{0,8},{4,12},{8,16},{12,20},{16,24},{20,28},{24,0},{28,4},{1,9},{5... | collective-permute-start | bytes 1572872 | tf_op jit(solution)/shard_map/ppermute | solution.py:76
  555.0 15.1 %collective-permute-start.124 = (bf16[128,2048]{1,0:T(8,128)(2,1)}, bf16[128,2048]{1,0:T(8,128)(2,1)}, u32[]{:S(2)}, u32[]{:S(2)}) collective-permute-start(bf16[128,2048]{1,0:T(8,128)(2,1)} %slice.853), channel_id=1, source_target_pairs={{0,4},{4,0},{8,12},{12,8},{16,20},{20,16},{24,28},{28,24},{1,5},{5... | collective-permute-start | bytes 1572872 | tf_op jit(solution)/shard_map/ppermute | solution.py:76
  (255 other events, 2238.0 us)
